TPU v7x, 32 devices: a whole 2x2x4 slice. The times are simulated.
32 devices in a mesh: batch: 4 (over y, x), seq: 8 (over z, core).
Axes of the slice: x: 2, y: 2, z: 4, core: 2. Of those that a mesh axis runs over, the one named last changes fastest.
Arguments:
- tokens: bfloat16 [2, 4, 1536, 512], P(None, 'batch', 'seq'), may hold values from -6 to 6
- lengths: int32 [2, 4, 2], P(None, 'batch'), may hold values from 499 to 1032, as said below
- ln1_gain: bfloat16 [512], P(('batch', 'seq')), may hold values from 0.5 to 1.5
- ln1_bias: bfloat16 [512], P(('batch', 'seq')), may hold values from -4 to 4
- w_query: bfloat16 [512, 512], P(('batch', 'seq')), may hold values from -0.25 to 0.25
- w_key: bfloat16 [512, 512], P(('batch', 'seq')), may hold values from -0.25 to 0.25
- w_value: bfloat16 [512, 512], P(('batch', 'seq')), may hold values from -0.25 to 0.25
- conv_key: bfloat16 [3, 512, 512], P(None, ('batch', 'seq')), may hold values from -0.15625 to 0.15625
- conv_value: bfloat16 [3, 512, 512], P(None, ('batch', 'seq')), may hold values from -0.15625 to 0.15625
- w_out: bfloat16 [512, 512], P(('batch', 'seq')), may hold values from -0.75 to 0.75
- ln2_gain: bfloat16 [512], P(('batch', 'seq')), may hold values from 0.5 to 1.5
- ln2_bias: bfloat16 [512], P(('batch', 'seq')), may hold values from -4 to 4
- w_up: bfloat16 [512, 2048], P(('batch', 'seq')), may hold values from -0.25 to 0.25
- b_up: bfloat16 [2048], P(('batch', 'seq')), may hold values from -6 to 6
- w_down: bfloat16 [2048, 512], P(('batch', 'seq')), may hold values from -0.125 to 0.125
- b_down: bfloat16 [512], P(('batch', 'seq')), may hold values from -4 to 4
- cotangent: bfloat16 [2, 4, 1536, 512], P(None, 'batch', 'seq'), may hold values from -6 to 6
Outputs:
- layer_out: bfloat16 [2, 4, 1536, 512], P(None, 'batch', 'seq')
- input_grad: bfloat16 [2, 4, 1536, 512], P(None, 'batch', 'seq')
- grad_ln1_gain: float32 [512], P(('batch', 'seq'))
- grad_ln1_bias: float32 [512], P(('batch', 'seq'))
- grad_w_query: float32 [512, 512], P(('batch', 'seq'))
- grad_w_key: float32 [512, 512], P(('batch', 'seq'))
- grad_w_value: float32 [512, 512], P(('batch', 'seq'))
- grad_conv_key: float32 [3, 512, 512], P(None, ('batch', 'seq'))
- grad_conv_value: float32 [3, 512, 512], P(None, ('batch', 'seq'))
- grad_w_out: float32 [512, 512], P(('batch', 'seq'))
- grad_ln2_gain: float32 [512], P(('batch', 'seq'))
- grad_ln2_bias: float32 [512], P(('batch', 'seq'))
- grad_w_up: float32 [512, 2048], P(('batch', 'seq'))
- grad_b_up: float32 [2048], P(('batch', 'seq'))
- grad_w_down: float32 [2048, 512], P(('batch', 'seq'))
- grad_b_down: float32 [512], P(('batch', 'seq'))
Inputs may be any that keep to these rules, and one draw needn't show every extreme that they name: Each row holds two items; their lengths padded up to multiples of 3 sum to 1533. The shorter one, first or second, has a padded length of 3 * min(167, 170) or more and at most half of 1533.
All inputs are finite; a program needn't handle non-finite values.
Results may differ from a plain program's by a relative error of at most 0.019.
Values may be sent and summed in bfloat16 or wider, within the bound.
No kernel may reach another device: no remote copies, remote signals or barrier semaphores. Data moves between devices by JAX's collectives and lax.ppermute only.
A program may use at most 128 MiB of HBM per device.

v0:
```python
import functools

import jax
import jax.numpy as jnp
from jax import lax
from jax.experimental import pallas as pl
from jax.experimental.pallas import tpu as pltpu
from jax.sharding import PartitionSpec as P

HEADS = 8
HEAD_DIM = 64
SCALE = HEAD_DIM ** (-0.5)
EPSILON = 1e-06
AXES = ("batch", "seq")
GROUPS = 32
UNIT = 16
PAIR = 2 * HEAD_DIM
RIM = 8
MASKED = -1e30
F32 = jnp.float32
BF16 = jnp.bfloat16
TN = ((0,), (0,))
NT = ((1,), (1,))
ERF_STEP = 0.3275911
ERF_TERMS = (1.061405429, -1.453152027, 1.421413741, -0.284496736, 0.254829592)


def device_count():
    return lax.axis_size("batch") * lax.axis_size("seq")


def device_index():
    return lax.axis_index("batch") * lax.axis_size("seq") + lax.axis_index("seq")


def powers(low, high):
    masks = []
    while low < high:
        masks.append(low)
        low *= 2
    return masks


def swap(array, mask):
    return lax.ppermute(array, AXES, [(i, i ^ mask) for i in range(device_count())])


def upper_half(mask):
    return ((device_index() & mask) != 0).astype(jnp.int32)


class Order:
    def __init__(self):
        self.last = None
        bits = device_count().bit_length() - 1
        self.uppers = jnp.stack([upper_half(1 << bit) for bit in range(bits)])

    def turn(self, array):
        if self.last is not None:
            array = lax.optimization_barrier((array, self.last))[0]
        return array

    def done(self, array):
        self.last = array


def axis_of(bits, mask):
    return sum(b > mask for b in bits)


def bit_shape(bits, rows):
    return (2,) * len(bits) + tuple(rows)


def at_bit(rank, axis, index, rows):
    where = [slice(None)] * rank
    where[axis] = pl.ds(index, 1)
    where[-2] = rows
    return tuple(where)


def overlaps(lefts, rights):
    found, left_at = [], 0
    for i, left in enumerate(lefts):
        right_at = 0
        for j, right in enumerate(rights):
            low = max(left_at, right_at)
            high = min(left_at + left, right_at + right)
            if low < high:
                found.append(
                    (i, j, slice(low - left_at, high - left_at), slice(low - right_at, high - right_at))
                )
            right_at += right
        left_at += left
    return found


def place_kernel(axes, masks, cuts, uppers, *refs):
    count = len(axes)
    for i, j, inside, outside in cuts:
        mine, other, out = refs[2 * i], refs[2 * i + 1], refs[2 * count + j]
        rank, axis, at = len(out.shape), axes[i], uppers[masks[i].bit_length() - 1]
        source = (slice(None),) * (rank - 3) + (inside, slice(None))
        out[at_bit(rank, axis, at, outside)] = jnp.expand_dims(mine[source], axis)
        out[at_bit(rank, axis, 1 - at, outside)] = jnp.expand_dims(other[source], axis)


def add_kernel(axes, masks, cuts, count, uppers, *refs):
    for i, j, inside, outside in cuts:
        keep, other = refs[2 * i], refs[2 * i + 1]
        next_keep, next_send = refs[2 * count + 2 * j], refs[2 * count + 2 * j + 1]
        rank, axis, at = len(keep.shape), axes[j], uppers[masks[j].bit_length() - 1]
        into = (slice(None),) * (rank - 3) + (outside, slice(None))
        here, there = at_bit(rank, axis, at, inside), at_bit(rank, axis, 1 - at, inside)
        next_send[into] = jnp.squeeze(keep[there] + other[there], axis)
        next_keep[into] = jnp.squeeze(keep[here] + other[here], axis)


def place(order, *jobs):
    axes, masks, cuts, args, outs, plans = [], [], [], [], [], []
    for gather, sizes in jobs:
        olds = [p.shape[-2] for p in gather.parts]
        sizes = sizes or olds
        bits = [sorted(b + [m], reverse=True) for b, m in zip(gather.bits, gather.masks)]
        own_axes = [axis_of(b, m) for b, m in zip(gather.bits, gather.masks)]
        bits = [bits[min(j, len(bits) - 1)] for j in range(len(sizes))]
        found = overlaps(olds, sizes)
        plans.append((gather, olds, sizes, bits, own_axes, len(outs)))
        cuts += [(len(axes) + i, len(outs) + j, x, y) for i, j, x, y in found]
        axes += own_axes
        masks += gather.masks
        for mine, other in zip(gather.parts, gather.others):
            args += [order.turn(mine), other]
        width = gather.parts[0].shape[-1]
        outs += [(bit_shape(b, (r, width)), BF16) for b, r in zip(bits, sizes)]
    if device_count() == GROUPS:
        body = functools.partial(place_kernel, axes, masks, cuts)
        placed = kernel(body, (order.uppers, *args), outs, 0, 24)
        order.done(placed[0])
    for gather, olds, sizes, bits, own_axes, at in plans:
        if device_count() == GROUPS:
            parts = placed[at : at + len(sizes)]
        else:
            held = []
            sides = zip(gather.parts, gather.others, own_axes, gather.masks)
            for mine, other, axis, mask in sides:
                up = upper_half(mask)
                low, high = jnp.where(up, other, mine), jnp.where(up, mine, other)
                held.append(jnp.stack([low, high], axis=axis))
            parts = cut_rows(held, olds, sizes)
        gather.parts, gather.bits = parts, bits


def add(order, *jobs):
    axes, all_masks, cuts, args, outs, plans, count = [], [], [], [], [], [], 0
    for chain, masks, sizes in jobs:
        olds = [p.shape[-2] for p in chain.keeps]
        sizes = sizes or olds
        bits = [chain.bits[min(j, len(olds) - 1)] for j in range(len(sizes))]
        own_axes = [axis_of(b, m) for b, m in zip(bits, masks)]
        left = [[b for b in old if b != m] for old, m in zip(bits, masks)]
        plans.append((chain, masks, olds, sizes, own_axes, left, len(axes)))
        cuts += [(count + i, len(axes) + j, x, y) for i, j, x, y in overlaps(olds, sizes)]
        axes += own_axes
        all_masks += masks
        count += len(olds)
        for keep, other in zip(chain.keeps, chain.others):
            args += [order.turn(keep), other]
        width = chain.keeps[0].shape[-1]
        for b, r in zip(left, sizes):
            outs += [(bit_shape(b, (r, width)), BF16)] * 2
    if device_count() == GROUPS:
        body = functools.partial(add_kernel, axes, all_masks, cuts, count)
        both = kernel(body, (order.uppers, *args), outs, 0, 24)
        order.done(both[0])
    for chain, masks, olds, sizes, own_axes, left, at in plans:
        if device_count() == GROUPS:
            found = both[2 * at : 2 * (at + len(sizes))]
            chain.keeps, chain.sends = found[0::2], found[1::2]
        else:
            sums = [
                (k.astype(F32) + o.astype(F32)).astype(BF16)
                for k, o in zip(chain.keeps, chain.others)
            ]
            sums = cut_rows(sums, olds, sizes)
            sides = list(zip(sums, [upper_half(m) for m in masks], own_axes))
            take = lax.dynamic_index_in_dim
            chain.keeps = [take(t, u, axis, False) for t, u, axis in sides]
            chain.sends = [take(t, 1 - u, axis, False) for t, u, axis in sides]
        chain.bits = left


class Gather:
    def __init__(self, order, *parts):
        self.order, self.parts, self.bits = order, list(parts), [[] for _ in parts]

    def go(self, *masks, wait=False):
        self.masks = masks
        parts = [self.order.turn(p) for p in self.parts] if wait else self.parts
        self.others = [swap(p, m) for p, m in zip(parts, masks)]

    def place(self, *sizes):
        place(self.order, (self, sizes))
        return self

    def whole(self):
        held = self.parts[0]
        return held.reshape((-1,) + held.shape[-2:])


def cut_rows(arrays, olds, sizes):
    if list(olds) == list(sizes):
        return arrays
    joint = jnp.concatenate(arrays, axis=-2)
    ends = [sum(sizes[: j + 1]) for j in range(len(sizes) - 1)]
    return jnp.split(joint, ends, axis=-2)


class Reduce:
    def __init__(self, order, keep, send, bits):
        shape = bit_shape(bits, keep.shape[-2:])
        self.order, self.bits = order, [bits]
        self.keeps, self.sends = [keep.reshape(shape)], [send.reshape(shape)]

    def go(self, *masks, wait=False):
        sends = [self.order.turn(p) for p in self.sends] if wait else self.sends
        self.others = [swap(p, m) for p, m in zip(sends, masks)]

    def add(self, masks, *sizes):
        add(self.order, (self, masks, sizes))
        return self

    def total(self):
        keep, other = self.keeps[0], self.others[0]
        return (keep.astype(F32) + other.astype(F32)).reshape(keep.shape[-2:])


def split_cores(blocks):
    pairs = blocks.reshape((-1, 2) + blocks.shape[1:])
    upper = upper_half(1)
    keep = lax.dynamic_index_in_dim(pairs, upper, 1, keepdims=False)
    return keep, lax.dynamic_index_in_dim(pairs, 1 - upper, 1, keepdims=False)


def joined(keep, send):
    return jnp.stack([keep, send], axis=1).reshape((-1,) + keep.shape[1:])


def grouped(buffer, sizes):
    count = buffer.shape[0]
    if count == GROUPS:
        return buffer
    width = buffer.shape[-1]
    share = width // count
    parts, start = [], 0
    for size in sizes:
        part = buffer[:, start : start + share * size]
        parts.append(part.reshape(GROUPS, UNIT * size, width))
        start += share * size
    return jnp.concatenate(parts, axis=1)


def scattered(buffer, sizes):
    count, width = device_count(), buffer.shape[-1]
    if count == GROUPS:
        return buffer
    parts, start = [], 0
    for size in sizes:
        part = buffer[:, start : start + UNIT * size]
        parts.append(part.reshape(count, width // count * size, width))
        start += UNIT * size
    return jnp.concatenate(parts, axis=1)


def vector_pack(vectors, rows, width):
    filled = jnp.pad(vectors, ((0, 0), (0, width - vectors.shape[1])))
    return jnp.pad(filled[:, None], ((0, 0), (0, rows - 1), (0, 0)))


def vector_regroup(vectors, parts, lengths):
    pieces, start = [], 0
    for length in lengths:
        pieces.append(vectors[:, start : start + length].reshape(parts, -1))
        start += length
    return jnp.concatenate(pieces, axis=1)


def dot(a, b, dims=((1,), (0,))):
    return lax.dot_general(a, b, (dims, ((), ())), preferred_element_type=F32)


def iota(shape, axis):
    return lax.broadcasted_iota(jnp.int32, shape, axis)


def tile(ref, place, size=1):
    rows = ref[:, UNIT * place : UNIT * (place + size), :]
    return rows.reshape(GROUPS * UNIT * size, rows.shape[-1])


def kernel(body, args, outs, flops, limit, scratch=()):
    spec = {jnp.dtype(jnp.int32): pltpu.SMEM}
    return pl.pallas_call(
        body,
        in_specs=[pl.BlockSpec(memory_space=spec.get(a.dtype, pltpu.VMEM)) for a in args],
        out_specs=[pl.BlockSpec(memory_space=pltpu.VMEM) for _ in outs],
        out_shape=[jax.ShapeDtypeStruct(shape, dtype) for shape, dtype in outs],
        scratch_shapes=list(scratch),
        compiler_params=pltpu.CompilerParams(vmem_limit_bytes=limit << 20),
        cost_estimate=pl.CostEstimate(
            flops=flops,
            bytes_accessed=sum(a.size * a.dtype.itemsize for a in args),
            transcendentals=0,
        ),
    )(*args)


def unit_norm(values):
    center = values - jnp.mean(values, axis=-1, keepdims=True)
    spread = jnp.mean(center * center, axis=-1, keepdims=True)
    inverse = lax.rsqrt(spread + EPSILON)
    return center * inverse, inverse


def norm_back(grad, unit, inverse, gain):
    e = grad * gain
    mean_e = jnp.mean(e, axis=-1, keepdims=True)
    mean_x = jnp.mean(e * unit, axis=-1, keepdims=True)
    return inverse * (e - mean_e - unit * mean_x)


def column_sum(values):
    return jnp.sum(values, axis=0, keepdims=True)


def valid_column(info, m, start, rows):
    place = start + iota((rows, 1), 0)
    first = (place >= 1) & (place < info[m, 0])
    second = (place >= info[m, 1]) & (place < info[m, 2])
    return jnp.where(first | second, 1.0, 0.0).astype(F32)


def segment_start(info, m, place):
    start = jnp.where(place >= 1, 1, 0)
    start = jnp.where(place >= info[m, 1], info[m, 1], start)
    return jnp.where(place >= info[m, 3], info[m, 3], start)


VECTORS = 5
BIAS_AT = VECTORS * UNIT


def vector_maps(width):
    lanes = width // 2
    fine = (iota((lanes, width), 0) & 15) == (iota((lanes, width), 1) & 15)
    wide = ((iota((lanes, width), 0) + 48) & 63) == (iota((lanes, width), 1) & 63)
    own_fine = iota((GROUPS, width), 1) >> 4 == iota((GROUPS, width), 0)
    own_wide = iota((GROUPS, width), 1) >> 6 == (iota((GROUPS, width), 0) & 7)
    as_bf16 = [jnp.where(m, 1.0, 0.0).astype(BF16) for m in (fine, wide)]
    as_f32 = [jnp.where(m, 1.0, 0.0).astype(F32) for m in (own_fine, own_wide)]
    return as_bf16 + as_f32


def lane_window(lanes, k):
    place = iota((GROUPS, lanes), 1)
    if k == VECTORS:
        return (place >= BIAS_AT) & (place < BIAS_AT + 64)
    return (place >= UNIT * k) & (place < UNIT * (k + 1))


def window_map(micro, each, tap):
    slots = each // 3
    shape = (micro * slots, micro * (each + RIM))
    row, place = iota(shape, 0), iota(shape, 1)
    m = jnp.zeros(shape, jnp.int32)
    for i in range(1, micro):
        m = m + jnp.where(row >= slots * i, 1, 0)
    source = 3 * (row - slots * m) - 2 + tap
    rim = micro * each + RIM * m + RIM + source
    target = jnp.where(source >= 0, each * m + source, rim)
    return jnp.where(place == target, 1.0, 0.0).astype(BF16)


def keep_and_compress(info, low, weights, kept, window, memory):
    micro = info.shape[0]
    each = low.shape[0] // micro - RIM
    valid = [valid_column(info, m, info[m, 4], each) for m in range(micro)]
    valid += [valid_column(info, m, info[m, 4] - RIM, RIM) for m in range(micro)]
    rows = (dot(low, tile(weights, 0)) * jnp.concatenate(valid, axis=0)).astype(BF16)
    kept[...] = rows
    total = None
    for tap in range(3):
        taken = dot(window_map(micro, each, tap), rows).astype(BF16)
        window[tap] = taken
        part = dot(taken, tile(weights, 1 + tap))
        total = part if total is None else total + part
    memory[...] = total.astype(BF16)


def key_kernel(info, tok, halo, weights, normed, kept, window, memory, vec):
    width = tok.shape[-1]
    lanes = width // 2
    fine, wide, own_fine, own_wide = vector_maps(width)
    rows = jnp.sum(weights[:, 4 * UNIT : 5 * UNIT, :lanes].astype(F32), axis=1)
    picked = [jnp.where(lane_window(lanes, k), rows, 0.0) for k in range(VECTORS + 1)]
    spread = dot(jnp.concatenate(picked[:VECTORS], axis=0).astype(BF16), fine)
    vectors = [
        column_sum(spread[GROUPS * k : GROUPS * (k + 1)] * own_fine) for k in range(VECTORS)
    ]
    bias = dot(picked[VECTORS].astype(BF16), wide) * own_wide
    bias = jnp.sum(bias.reshape(4, 8, width), axis=1)
    vec[...] = jnp.concatenate(vectors + [bias, jnp.zeros((7, width), F32)], axis=0)
    values = jnp.concatenate([tok[...], halo[...]], axis=0).astype(F32)
    unit, _ = unit_norm(values)
    low = (unit * vectors[0] + vectors[1]).astype(BF16)
    normed[...] = low
    keep_and_compress(info, low, weights, kept, window, memory)


def value_kernel(info, normed, weights, query, kept, window, memory):
    low = normed[...]
    keep_and_compress(info, low, weights, kept, window, memory)
    query[...] = dot(low[: query.shape[0]], tile(weights, 4)).astype(BF16)


def stacked(values, lower):
    zero = jnp.zeros_like(values)
    return jnp.concatenate(
        [jnp.where(lower, values, zero), jnp.where(lower, zero, values)], axis=0
    )


def merged(values, lower):
    half = values.shape[0] // 2
    return jnp.where(lower, values[:half], values[half:])


def memory_pair(memory, m, pair, micro):
    slots = memory.shape[1] // micro
    rows = memory[:, slots * m : slots * (m + 1), PAIR * pair : PAIR * (pair + 1)]
    return rows.reshape(memory.shape[0] * slots, PAIR)


def attend_kernel(info, query, keys, values, memory_keys, memory_values, attended, stats):
    micro = info.shape[0]
    count, width = query.shape
    each = count // micro
    slots = memory_keys.shape[0] * memory_keys.shape[1] // micro
    pairs = width // PAIR
    lower = iota((each, PAIR), 1) < HEAD_DIM
    lane = iota((2 * each, 128), 1)
    found = jnp.zeros((2 * each, 128), F32)
    for m in range(micro):
        rows = slice(each * m, each * (m + 1))
        place = info[m, 4] + iota((each, 1), 0)
        start = segment_start(info, m, place)
        end = 3 * iota((each, slots), 1)
        bias = jnp.where((end <= place) & (end >= start), 0.0, MASKED).astype(F32)
        bias = jnp.concatenate([bias, bias], axis=0)
        for pair in range(pairs):
            cols = slice(PAIR * pair, PAIR * (pair + 1))
            key = keys[rows, cols].astype(F32)
            value = values[rows, cols].astype(F32)
            queries = stacked(query[rows, cols].astype(F32) * SCALE, lower)
            own = jnp.sum(queries * jnp.concatenate([key, key], axis=0), axis=1, keepdims=True)
            memory_key = memory_pair(memory_keys, m, pair, micro)
            memory_value = memory_pair(memory_values, m, pair, micro)
            scores = dot(queries.astype(BF16), memory_key, NT) + bias
            top = jnp.maximum(jnp.max(scores, axis=1, keepdims=True), own)
            expos = jnp.exp(scores - top)
            own = jnp.exp(own - top)
            total = jnp.sum(expos, axis=1, keepdims=True) + own
            inverse = 1.0 / total
            mixed = dot(expos.astype(BF16), memory_value) * inverse
            weight = jnp.broadcast_to(own * inverse, mixed.shape)
            attended[rows, cols] = merged(mixed, lower) + merged(weight, lower) * value
            found = jnp.where(lane == m * pairs + pair, top + jnp.log(total), found)
    stats[...] = found


def gelu_parts(hidden):
    falling = jnp.exp(hidden * hidden * -0.5)
    step = 1.0 / (1.0 + (ERF_STEP * 0.7071067811865476) * jnp.abs(hidden))
    tail = 0.5 * ERF_TERMS[0]
    for term in ERF_TERMS[1:]:
        tail = tail * step + 0.5 * term
    tail = tail * step * falling
    return jnp.where(hidden >= 0.0, 1.0 - tail, tail), falling


def even_first(flag, rows, size):
    pairs = rows.reshape(-1, 2, size, rows.shape[-1])
    even, odd = pairs[:, 0], pairs[:, 1]
    halves = [jnp.where(flag == 0, even, odd), jnp.where(flag == 0, odd, even)]
    return jnp.concatenate(halves, axis=0).reshape(rows.shape)


def deal(value, rows, keep, send, blocks, start):
    halves = value.astype(BF16).reshape(2, -1, rows, value.shape[-1])
    keep[blocks, start : start + rows, :] = halves[0]
    send[blocks, start : start + rows, :] = halves[1]


def deal_tile(value, place, keep, send):
    deal(value, UNIT, keep, send, slice(None), UNIT * place)


def feed_kernel(
    info,
    tok,
    cot,
    attended,
    vec,
    rest,
    out,
    grad_mid,
    grad_att,
    keep,
    send,
    vec_grad,
):
    count, width = tok.shape
    wide = 4
    low_att = attended[...].astype(BF16)
    w_out = tile(rest, 0)
    middle = tok[...].astype(F32) + dot(low_att, w_out)
    unit, inverse = unit_norm(middle)
    gain = vec[2:3, :]
    low = (unit * gain + vec[3:4, :]).astype(BF16)
    flag = info[0, 5]
    low_t = even_first(flag, low.T, UNIT)
    cots = cot[...]
    total = middle + vec[4:5, :]
    grad_low = jnp.zeros((count, width), F32)
    bias_rows = []
    eighth = GROUPS // wide
    for c in range(wide):
        w_up = tile(rest, 1 + c)
        down = slice(eighth * c, eighth * (c + 1))
        w_down = rest[down, UNIT * (1 + wide) :, :].reshape(width, width)
        hidden = dot(low, w_up) + vec[5 + c : 6 + c, :]
        share, falling = gelu_parts(hidden)
        slope = share + (0.3989422804014327 * hidden) * falling
        active = (hidden * share).astype(BF16)
        total = total + dot(active, w_down)
        grad_hidden_f = dot(cots, w_down, NT) * slope
        grad_hidden = grad_hidden_f.astype(BF16)
        bias_rows.append(column_sum(grad_hidden.astype(F32)))
        grad_low = grad_low + dot(grad_hidden, w_up, NT)
        deal_tile(dot(low_t, grad_hidden), 1 + c, keep, send)
        where = slice(eighth // 2 * c, eighth // 2 * (c + 1))
        active_t = even_first(flag, active.T, UNIT * wide)
        deal(dot(active_t, cots), UNIT * wide, keep, send, where, UNIT * (1 + wide))
    out[...] = total.astype(BF16)
    cots_f = cots.astype(F32)
    grad_middle = cots_f + norm_back(grad_low, unit, inverse, gain)
    grad_mid[...] = grad_middle
    branch = grad_middle.astype(BF16)
    deal_tile(dot(even_first(flag, low_att.T, UNIT), branch), 0, keep, send)
    grad_att[...] = dot(branch, w_out, NT).astype(BF16)
    rows = [jnp.zeros((2, width), F32), column_sum(grad_low * unit), column_sum(grad_low)]
    rows += [column_sum(cots_f)] + bias_rows + [jnp.zeros((7, width), F32)]
    vec_grad[...] = jnp.concatenate(rows, axis=0)


def memory_turned(flag, memory, m, pair, micro):
    slots = memory.shape[2] // micro
    rows, cols = slice(slots * m, slots * (m + 1)), slice(PAIR * pair, PAIR * (pair + 1))
    halves = [memory[:, pl.ds(at, 1), rows, cols] for at in (flag, 1 - flag)]
    return jnp.concatenate([h.reshape(-1, PAIR) for h in halves], axis=0)


def attend_back_kernel(
    info,
    query,
    keys,
    values,
    memory_keys,
    memory_values,
    attended,
    stats,
    grad_att,
    grad_query,
    key_keep,
    key_send,
    value_keep,
    value_send,
    own_key,
    own_value,
):
    micro = info.shape[0]
    count, width = query.shape
    each = count // micro
    chips = memory_keys.shape[0]
    share = memory_keys.shape[2] // micro
    slots = 2 * chips * share
    flag = info[0, 6]
    pairs = width // PAIR
    lower = iota((each, PAIR), 1) < HEAD_DIM
    lane = iota((2 * each, 128), 1)
    found = stats[...]
    deltas = jnp.zeros((2 * each, 128), F32)
    parts = {}
    for m in range(micro):
        rows = slice(each * m, each * (m + 1))
        for pair in range(pairs):
            cols = slice(PAIR * pair, PAIR * (pair + 1))
            grad = grad_att[rows, cols].astype(F32)
            product = stacked(grad * attended[rows, cols], lower)
            delta = jnp.sum(product, axis=1, keepdims=True)
            deltas = jnp.where(lane == m * pairs + pair, delta, deltas)
            parts[m, pair] = delta
    found_t, deltas_t = found.T, deltas.T
    for m in range(micro):
        rows = slice(each * m, each * (m + 1))
        lanes = iota((1, 2 * each), 1)
        place = info[m, 4] + jnp.where(lanes >= each, lanes - each, lanes)
        start = segment_start(info, m, place)
        row = iota((slots, 1), 0)
        late = row >= chips * share
        row = jnp.where(late, row - chips * share, row)
        block = jnp.zeros((slots, 1), jnp.int32)
        for chip in range(1, chips):
            block = block + jnp.where(row >= share * chip, 1, 0)
        core = jnp.where(late, 1 - flag, flag)
        end = 3 * (row + share * (block + core))
        bias = jnp.where((end <= place) & (end >= start), 0.0, MASKED).astype(F32)
        for pair in range(pairs):
            cols = slice(PAIR * pair, PAIR * (pair + 1))
            at = m * pairs + pair
            key = keys[rows, cols].astype(F32)
            value = values[rows, cols].astype(F32)
            query_f = query[rows, cols].astype(F32) * SCALE
            grad_f = grad_att[rows, cols].astype(F32)
            queries = stacked(query_f, lower)
            grads = stacked(grad_f, lower)
            own = jnp.sum(queries * jnp.concatenate([key, key], axis=0), axis=1, keepdims=True)
            own = jnp.exp(own - found[:, at : at + 1])
            grad_own = jnp.sum(
                grads * jnp.concatenate([value, value], axis=0), axis=1, keepdims=True
            )
            grad_own = (own * (grad_own - parts[m, pair])).astype(BF16).astype(F32)
            queries, grads = queries.astype(BF16), grads.astype(BF16)
            memory_key = memory_turned(flag, memory_keys, m, pair, micro)
            memory_value = memory_turned(flag, memory_values, m, pair, micro)
            scores = dot(memory_key, queries, NT) + bias
            probs = jnp.exp(scores - found_t[at : at + 1, :])
            grad_probs = dot(memory_value, grads, NT)
            grad_scores = (probs * (grad_probs - deltas_t[at : at + 1, :])).astype(BF16)
            sides = (
                (dot(grad_scores, queries), key_keep, key_send),
                (dot(probs.astype(BF16), grads), value_keep, value_send),
            )
            for grad, keep, send in sides:
                halves = grad.astype(BF16).reshape(2, chips, share, PAIR)
                keep[:, share * m : share * (m + 1), cols] = halves[0]
                send[:, share * m : share * (m + 1), cols] = halves[1]
            turned = dot(memory_key.T, grad_scores).T
            own_grad = merged(jnp.broadcast_to(grad_own, (2 * each, PAIR)), lower)
            own_weight = merged(jnp.broadcast_to(own, (2 * each, PAIR)), lower)
            grad_query[rows, cols] = (
                SCALE * (merged(turned, lower) + own_grad * key)
            ).astype(BF16)
            own_key[rows, cols] = own_grad * query_f
            own_value[rows, cols] = own_weight * grad_f


def compress_back_kernel(
    info,
    key_memory,
    value_memory,
    key_window,
    value_window,
    key_weights,
    value_weights,
    normed,
    grad_query,
    key_grad,
    value_grad,
    rims,
    keep,
    send,
):
    micro = info.shape[0]
    count, width = key_grad.shape
    each = count // micro
    flag = info[0, 5]
    places = [window_map(micro, each, tap) for tap in range(3)]
    sides = (
        (key_memory, key_window, key_weights, key_grad),
        (value_memory, value_window, value_weights, value_grad),
    )
    for kind, (memory, window, weights, out) in enumerate(sides):
        grad = memory[...]
        total = None
        for tap in range(3):
            window_t = even_first(flag, window[tap].T, UNIT)
            deal_tile(dot(window_t, grad), 4 * kind + tap, keep, send)
            part = dot(grad, tile(weights, 1 + tap), NT)
            high = part.astype(BF16)
            rest = (part - high.astype(F32)).astype(BF16)
            part = dot(places[tap], high, TN) + dot(places[tap], rest, TN)
            total = part if total is None else total + part
        out[...] = total[:count]
        rims[:, width * kind : width * (kind + 1)] = total[count:]
    low_t = even_first(flag, normed[:count, :].T, UNIT)
    deal_tile(dot(low_t, grad_query[...]), 3, keep, send)


def input_kernel(
    info,
    tok,
    normed,
    grad_query,
    key_grad,
    value_grad,
    rims,
    own_key,
    own_value,
    key_weights,
    value_weights,
    vec,
    grad_mid,
    vec_grad,
    grad_in,
    keep,
    send,
    total,
):
    count, width = tok.shape
    micro = info.shape[0]
    each = count // micro
    valid = [valid_column(info, m, info[m, 4], each) for m in range(micro)]
    valid = jnp.concatenate(valid, axis=0)
    flag = info[0, 5]
    low_t = even_first(flag, normed[:count, :].T, UNIT)
    grad_low = dot(grad_query[...], tile(value_weights, 4), NT)
    sides = ((key_grad, own_key, key_weights), (value_grad, own_value, value_weights))
    for kind, (grad, own, weights) in enumerate(sides):
        total[...] = grad[...] + own[...]
        for m in range(micro):
            rows = slice(each * (m + 1) - RIM, each * (m + 1))
            rim = rims[RIM * m : RIM * (m + 1), width * kind : width * (kind + 1)]
            total[rows, :] = total[rows, :] + rim
        low_grad = (total[...] * valid).astype(BF16)
        grad_low = grad_low + dot(low_grad, tile(weights, 0), NT)
        deal_tile(dot(low_t, low_grad), kind, keep, send)
    unit, inverse = unit_norm(tok[...].astype(F32))
    back = norm_back(grad_low, unit, inverse, vec[0:1, :])
    grad_in[...] = (grad_mid[...] + back).astype(BF16)

    lanes = width // 2
    fine, wide, own_fine, own_wide = vector_maps(width)
    vectors = [column_sum(grad_low * unit), column_sum(grad_low)]
    vectors += [vec_grad[k : k + 1, :] for k in range(2, VECTORS)]
    dealt = jnp.concatenate([own_fine * v for v in vectors], axis=0).astype(BF16)
    dealt = dot(dealt, fine, NT)
    bias = [
        jnp.broadcast_to(vec_grad[VECTORS + c : VECTORS + c + 1, :], (8, width)) for c in range(4)
    ]
    bias = (jnp.concatenate(bias, axis=0) * own_wide).astype(BF16)
    packed = jnp.where(lane_window(lanes, VECTORS), dot(bias, wide, NT), 0.0)
    for k in range(VECTORS):
        packed = jnp.where(lane_window(lanes, k), dealt[GROUPS * k : GROUPS * (k + 1)], packed)
    packed = jnp.concatenate([packed, jnp.zeros((GROUPS, width - lanes), F32)], axis=1)
    spot = iota((GROUPS, UNIT, width), 1) == 0
    spread = jnp.broadcast_to(packed[:, None, :], (GROUPS, UNIT, width))
    packed = jnp.where(spot, spread, 0.0).reshape(GROUPS * UNIT, width)
    deal_tile(even_first(flag, packed, UNIT), 2, keep, send)


def per_device(
    tokens,
    lengths,
    ln1_gain,
    ln1_bias,
    w_query,
    w_key,
    w_value,
    conv_key,
    conv_value,
    w_out,
    ln2_gain,
    ln2_bias,
    w_up,
    b_up,
    w_down,
    b_down,
    cotangent,
):
    count = device_count()
    micro, _, each, width = tokens.shape
    ff = w_up.shape[1]
    wide = ff // width
    share = width // count
    seq = lax.axis_size("seq")
    all_tokens = micro * each
    slots = micro * each // 3
    memory_bytes = 4 * seq * slots * width

    whole = count == GROUPS
    vector_lengths = [share] * VECTORS + [ff // count]
    vectors, start = 0.0, 0
    for part in (ln1_gain, ln1_bias, ln2_gain, ln2_bias, b_down, b_up):
        end = start + part.shape[0]
        pad = ((0, (UNIT if whole else 2) - 1), (start, width - end))
        vectors, start = vectors + jnp.pad(part[None], pad), end
    vectors = vectors.astype(BF16)
    across = powers(seq, count)
    along = powers(2, seq)[::-1]
    back = along[::-1]
    order = Order()
    lengths = lengths[:, 0]
    first_pad = 3 * ((lengths[:, 0] + 2) // 3)
    second_pad = 3 * ((lengths[:, 1] + 2) // 3)
    start = 1 + first_pad
    seats = [lax.axis_index("seq") * each, upper_half(1) if whole else 0, upper_half(1)]
    seats = [jnp.full_like(start, seat) for seat in seats]
    info = [1 + lengths[:, 0], start, start + lengths[:, 1], start + second_pad]
    info = jnp.stack(info + seats, axis=1).astype(jnp.int32)
    first = jnp.concatenate([w_key, *conv_key, vectors], axis=0)
    second = jnp.concatenate([w_value, *conv_value, w_query], axis=0)
    ups = [w_up[:, width * c : width * (c + 1)] for c in range(wide)]
    rest = jnp.concatenate([w_out] + ups + [w_down], axis=0)
    rest_rows = rest.shape[0]
    upper_rows = share * (1 + wide)
    one, two, both = Gather(order, first), Gather(order, second), Gather(order, rest)
    one.go(along[0])
    two.go(back[0])
    last_rows = lax.optimization_barrier((tokens[:, 0, each - RIM :], first))[0]
    halo = lax.ppermute(last_rows, "seq", [(i, i + 1) for i in range(seq - 1)])
    halo = halo.reshape(micro * RIM, width)
    for at in range(1, len(along)):
        one.place()
        one.go(along[at])
        two.place()
        two.go(back[at])
    order.done((halo, info, rest))
    one.place()
    one.go(across[0])
    two.place()
    two.go(across[-1])
    both.go(along[0], wait=True)
    for at in range(1, max(len(across), len(along))):
        jobs = []
        if at < len(across):
            one.place()
            one.go(across[at])
            jobs.append((two, ()))
        if at < len(along):
            jobs.append((both, ()))
        place(order, *jobs)
        if at < len(across):
            two.go(across[-1 - at])
        if at < len(along):
            both.go(along[at])
    one.place()
    one.go(1)
    place(order, (two, ()), (both, (upper_rows, rest_rows - upper_rows)))
    two.go(1)
    both.go(across[0], across[-1])
    first = one.place().whole()
    first_sizes, rest_sizes = [1] * 5, [1] * (1 + wide) + [wide]
    if not whole:
        dealt = vector_regroup(first[:, 4 * share], GROUPS, vector_lengths)
        dealt = vector_pack(dealt, UNIT, width)
        first = jnp.concatenate([grouped(first, [1] * 4), dealt], axis=1)

    tok = tokens.reshape(all_tokens, width)
    cot = cotangent.reshape(all_tokens, width)
    rows = (all_tokens, width)
    grown = 4 * max(memory_bytes // (1 << 20) - 2, 0)
    limits = [16, 16, 16 + grown, 28, 28 + grown, 28, 28]
    matmul = 2 * all_tokens * width * width

    padded = (all_tokens + micro * RIM, width)
    windows = (3, slots, width)

    normed, keys, key_window, memory_key, vec = kernel(
        key_kernel,
        (info, order.turn(tok), halo, first),
        ((padded, BF16), (padded, BF16), (windows, BF16), ((slots, width), BF16), ((16, width), F32)),
        2 * matmul,
        limits[0],
    )
    order.done(memory_key)
    keys_side = Gather(order, memory_key)
    keys_side.go(along[0])
    second = grouped(two.place().whole(), first_sizes)
    query, values, value_window, memory_value = kernel(
        value_kernel,
        (info, normed, second),
        ((rows, BF16), (padded, BF16), (windows, BF16), ((slots, width), BF16)),
        3 * matmul,
        limits[1],
    )
    order.done(memory_value)
    values_side = Gather(order, memory_value)
    values_side.go(back[0])
    for at in range(1, max(len(across), len(along))):
        jobs = []
        if at < len(along):
            keys_side.place()
            keys_side.go(along[at])
            jobs.append((values_side, ()))
        if at < len(across):
            jobs.append((both, ()))
        place(order, *jobs)
        if at < len(along):
            values_side.go(back[at])
        if at < len(across):
            both.go(across[at], across[-1 - at])
    keys_side.place()
    keys_side.go(1)
    place(order, (values_side, ()), (both, (rest_rows,)))
    values_side.go(1)
    both.go(1)
    memories = [keys_side.place().whole(), values_side.place().whole()]
    attended, stats = kernel(
        attend_kernel,
        (info, order.turn(query), keys, values, *memories),
        ((rows, F32), ((2 * each, 128), F32)),
        4 * matmul,
        limits[2],
    )
    order.done(attended)
    rest = grouped(both.place().whole(), rest_sizes)
    half = GROUPS // 2

    def pieces(size):
        return (((half, UNIT * size, width), BF16),) * 2

    output, grad_mid, grad_att, *halves, vec_grad = kernel(
        feed_kernel,
        (info, order.turn(tok), cot, attended, vec, rest),
        ((rows, BF16), (rows, F32), (rows, BF16)) + pieces(1 + 2 * wide) + (((16, width), F32),),
        27 * matmul,
        limits[3],
    )
    order.done(halves[0])
    all_bits = powers(2, count)[::-1]

    def begin(keep, send, size):
        if not whole:
            keep, send = split_cores(scattered(joined(keep, send), size))
        return Reduce(order, keep, send, all_bits)

    feeds = begin(*halves, rest_sizes)
    feeds.go(1)
    memory_half = ((seq // 2, slots, width), BF16)
    chips = (seq // 2, 2, slots, width)
    grad_query, *halves, own_key, own_value = kernel(
        attend_back_kernel,
        (
            info,
            order.turn(query),
            keys,
            values,
            memories[0].reshape(chips),
            memories[1].reshape(chips),
            attended,
            stats,
            grad_att,
        ),
        ((rows, BF16),) + (memory_half,) * 4 + ((rows, F32), (rows, F32)),
        10 * matmul,
        limits[4],
    )
    order.done(grad_query)
    keys_side = Reduce(order, *halves[:2], along)
    values_side = Reduce(order, *halves[2:], along)
    keys_side.go(1)
    values_side.go(1)
    cross = [(across[-1 - at], across[at]) for at in range(len(across))]
    keys_side.add((back[0],))
    keys_side.go(back[0])
    cuts = (upper_rows, rest_rows - upper_rows)
    add(order, (values_side, (along[0],), ()), (feeds, cross[0], cuts))
    values_side.go(along[0])
    feeds.go(*cross[0])
    for at in range(1, max(len(along), len(cross))):
        jobs = []
        if at < len(along):
            keys_side.add((back[at],))
            keys_side.go(back[at])
            jobs.append((values_side, (along[at],), ()))
        if at < len(cross):
            jobs.append((feeds, cross[at], ()))
        add(order, *jobs)
        if at < len(along):
            values_side.go(along[at])
        if at < len(cross):
            feeds.go(*cross[at])
    feeds.add((back[0],), rest_rows)
    key_grad, value_grad = (held.total().astype(BF16) for held in (keys_side, values_side))
    key_kept, value_kept, rims, *halves = kernel(
        compress_back_kernel,
        (
            info,
            order.turn(key_grad),
            value_grad,
            key_window,
            value_window,
            first,
            second,
            normed,
            grad_query,
        ),
        ((rows, F32), (rows, F32), ((micro * RIM, 2 * width), F32)) + pieces(7),
        5 * matmul,
        limits[5],
    )
    order.done(rims)
    rims = lax.ppermute(rims, "seq", [(i + 1, i) for i in range(seq - 1)])
    convs = begin(*halves, [1] * 7)
    convs.go(1)
    grad_in, *halves = kernel(
        input_kernel,
        (
            info,
            order.turn(tok),
            normed,
            grad_query,
            key_kept,
            value_kept,
            rims,
            own_key,
            own_value,
            first,
            second,
            vec,
            grad_mid,
            vec_grad,
        ),
        ((rows, BF16),) + pieces(3),
        6 * matmul,
        limits[6],
        (pltpu.VMEM(rows, F32),),
    )
    order.done(grad_in)
    if whole:
        inputs = begin(*halves, [1] * 3)
    else:
        dealt = joined(*halves)
        vectors = dealt[:, 2 * UNIT, : VECTORS * UNIT + ff // GROUPS]
        vectors = vector_regroup(vectors, count, [UNIT] * VECTORS + [ff // GROUPS])
        dealt = [scattered(dealt, [1] * 2), vector_pack(vectors, 2, width)]
        dealt = split_cores(jnp.concatenate(dealt, axis=1))
        inputs = Reduce(order, *dealt, all_bits)
    inputs.go(1)
    line = [masks[1] for masks in cross]
    cuts = (5 * share, 2 * share)
    convs.add(cross[0], *cuts)
    convs.go(*cross[0])
    feeds.go(back[0])
    inputs.add((line[0],))
    inputs.go(line[0])
    for at in range(1, max(len(along), len(cross))):
        jobs = []
        if at < len(cross):
            jobs.append((convs, cross[at], ()))
        if at < len(along):
            jobs.append((feeds, (back[at],), ()))
        add(order, *jobs)
        if at < len(cross):
            convs.go(*cross[at])
        if at < len(along):
            feeds.go(back[at])
        if at < len(cross):
            inputs.add((line[at],))
            inputs.go(line[at])
    for at in range(len(along)):
        convs.add((back[at],), 7 * share)
        convs.go(back[at])
        inputs.add((along[at],))
        inputs.go(along[at])
    feeds, convs, late_inputs = feeds.total(), convs.total(), inputs.total()
    conv_keys = convs[: 3 * share].reshape(3, share, width)
    conv_values = convs[4 * share :].reshape(3, share, width)

    def own(buffer, number):
        return buffer[share * number : share * (number + 1)]

    vector_row = late_inputs[2 * share]

    def own_vector(number, length=share):
        return vector_row[share * number : share * number + length]

    return (
        output.reshape(tokens.shape),
        grad_in.reshape(tokens.shape),
        own_vector(0),
        own_vector(1),
        own(convs, 3),
        own(late_inputs, 0),
        own(late_inputs, 1),
        conv_keys,
        conv_values,
        own(feeds, 0),
        own_vector(2),
        own_vector(3),
        jnp.concatenate([own(feeds, 1 + c) for c in range(wide)], axis=1),
        own_vector(VECTORS, ff // count),
        feeds[share * (1 + wide) :],
        own_vector(4),
    )


def solution(mesh):
    rows = P(AXES, None)
    vector = P(AXES)
    conv = P(None, AXES, None)
    part = P(None, "batch", "seq", None)
    weights = (vector, vector, rows, rows, rows, conv, conv, rows, vector, vector)
    weights = weights + (rows, vector, rows, vector)
    return jax.shard_map(
        per_device,
        mesh=mesh,
        in_specs=(part, P(None, "batch", None)) + weights + (part,),
        out_specs=(part, part) + weights,
        check_vma=False,
    )
```

profile of v0, /device:TPU:0, one launch (start us, length us, event | category | flops | bytes accessed | tf_op | source)
XLA Modules:
  0.0 216.5 jit_solution(10902620807531704419)
XLA Ops:
  4.3 4.1 %collective-permute-start = (bf16[80,512]{1,0:T(8,128)(2,1)S(1)}, bf16[80,512]{1,0:T(8,128)(2,1)S(1)}, u32[]{:S(2)}, u32[]{:S(2)}) collective-permute-start(bf16[80,512]{1,0:T(8,128)(2,1)S(1)} %constant_dynamic-update-slice_fusion.refs_0_), channel_id=1, source_target_pairs={{0,4},{1,5},{2,6},{3,7},{4,0},{5,1},{6,2},{7,3},{8,12},{9,13},{10,... | collective-permute-start | bytes 245768 | tf_op jit(solution)/shard_map/ppermute | solution.py:45
  24.3 4.3 %collective-permute-done.2.refs_1_ = bf16[2,80,512]{2,1,0:T(8,128)(2,1)S(1)} collective-permute-done((bf16[2,80,512]{2,1,0:T(8,128)(2,1)S(1)}, bf16[2,80,512]{2,1,0:T(8,128)(2,1)S(1)}, u32[]{:S(2)}, u32[]{:S(2)}) %collective-permute-start.2) | collective-permute-done | bytes 163872 | tf_op jit(solution)/shard_map/ppermute | solution.py:45
  30.7 2.4 %collective-permute-done.4.refs_1_ = bf16[2,80,512]{2,1,0:T(8,128)(2,1)S(1)} collective-permute-done((bf16[2,80,512]{2,1,0:T(8,128)(2,1)S(1)}, bf16[2,80,512]{2,1,0:T(8,128)(2,1)S(1)}, u32[]{:S(2)}, u32[]{:S(2)}) %collective-permute-start.4) | collective-permute-done | bytes 163872 | tf_op jit(solution)/shard_map/ppermute | solution.py:45
  35.3 2.5 %collective-permute-done.5.refs_1_ = bf16[2,2,80,512]{3,2,1,0:T(8,128)(2,1)S(1)} collective-permute-done((bf16[2,2,80,512]{3,2,1,0:T(8,128)(2,1)S(1)}, bf16[2,2,80,512]{3,2,1,0:T(8,128)(2,1)S(1)}, u32[]{:S(2)}, u32[]{:S(2)}) %collective-permute-start.5) | collective-permute-done | bytes 327712 | tf_op jit(solution)/shard_map/ppermute | solution.py:45
  39.9 2.9 %collective-permute-done.7.refs_3_ = bf16[144,512]{1,0:T(8,128)(2,1)S(1)} collective-permute-done((bf16[144,512]{1,0:T(8,128)(2,1)S(1)}, bf16[144,512]{1,0:T(8,128)(2,1)S(1)}, u32[]{:S(2)}, u32[]{:S(2)}) %collective-permute-start.7) | collective-permute-done | bytes 147488 | tf_op jit(solution)/shard_map/ppermute | solution.py:45
  46.5 11.2 %collective-permute-done.8.refs_1_ = bf16[2,2,2,80,512]{4,3,2,1,0:T(8,128)(2,1)S(1)} collective-permute-done((bf16[2,2,2,80,512]{4,3,2,1,0:T(8,128)(2,1)S(1)}, bf16[2,2,2,80,512]{4,3,2,1,0:T(8,128)(2,1)S(1)}, u32[]{:S(2)}, u32[]{:S(2)}) %collective-permute-start.8) | collective-permute-done | bytes 655392 | tf_op jit(solution)/shard_map/ppermute | solution.py:45
  70.3 3.1 %collective-permute-done.13.refs_1_ = bf16[128,512]{1,0:T(8,128)(2,1)S(1)} collective-permute-done((bf16[128,512]{1,0:T(8,128)(2,1)S(1)}, bf16[128,512]{1,0:T(8,128)(2,1)S(1)}, u32[]{:S(2)}, u32[]{:S(2)}) %collective-permute-start.13) | collective-permute-done | bytes 131104 | tf_op jit(solution)/shard_map/ppermute | solution.py:45
  79.7 2.7 %collective-permute-start.18 = (bf16[2,128,512]{2,1,0:T(8,128)(2,1)S(1)}, bf16[2,128,512]{2,1,0:T(8,128)(2,1)S(1)}, u32[]{:S(2)}, u32[]{:S(2)}) collective-permute-start(bf16[2,128,512]{2,1,0:T(8,128)(2,1)S(1)} %get-tuple-element.176.refs_0_), channel_id=1, source_target_pairs={{0,4},{1,5},{2,6},{3,7},{4,0},{5,1},{6,2},{7,3},{8,12},{9,13},{10,... | collective-permute-start | bytes 786440 | tf_op jit(solution)/shard_map/ppermute | solution.py:45
  82.4 10.1 %collective-permute-done.17.refs_1_ = bf16[2,128,512]{2,1,0:T(8,128)(2,1)S(1)} collective-permute-done((bf16[2,128,512]{2,1,0:T(8,128)(2,1)S(1)}, bf16[2,128,512]{2,1,0:T(8,128)(2,1)S(1)}, u32[]{:S(2)}, u32[]{:S(2)}) %collective-permute-start.17) | collective-permute-done | bytes 262176 | tf_op jit(solution)/shard_map/ppermute | solution.py:45
  95.4 4.7 %collective-permute-done.21.refs_1_ = bf16[2,2,128,512]{3,2,1,0:T(8,128)(2,1)S(1)} collective-permute-done((bf16[2,2,128,512]{3,2,1,0:T(8,128)(2,1)S(1)}, bf16[2,2,128,512]{3,2,1,0:T(8,128)(2,1)S(1)}, u32[]{:S(2)}, u32[]{:S(2)}) %collective-permute-start.21) | collective-permute-done | bytes 524320 | tf_op jit(solution)/shard_map/ppermute | solution.py:45
  101.4 3.8 %shard_map.306 = (f32[384,512]{1,0:T(8,128)S(1)}, f32[384,128]{1,0:T(8,128)S(1)}) custom-call(s32[2,7]{1,0:T(2,128)S(1)} %stack.37.info, bf16[384,512]{1,0:T(8,128)(2,1)S(1)} %get-tuple-element.195.query, bf16[400,512]{1,0:T(8,128)(2,1)S(1)} %get-tuple-element.187.keys, bf16[400,512]{1,0:T(8,128)(2,1)S(1)} %get-tuple-element.188.values, ...), custom_call_target="tpu_custom_call" | custom-call | flops 805306368 | bytes 3309624 | tf_op jit(solution)/shard_map/pallas_call | solution.py:303
  106.2 9.7 %shard_map.308 = (bf16[384,512]{1,0:T(8,128)(2,1)}, f32[384,512]{1,0:T(8,128)S(1)}, bf16[384,512]{1,0:T(8,128)(2,1)S(1)}, bf16[16,144,512]{2,1,0:T(8,128)(2,1)S(...) custom-call(s32[2,7]{1,0:T(2,128)S(1)} %stack.37.info, bf16[384,512]{1,0:T(8,128)(2,1)S(1)} %bitcast.80, ...), custom_call_target="tpu_custom_call" | custom-call | flops 5435817984 | bytes 6324280 | tf_op jit(solution)/shard_map/pallas_call | solution.py:303
  116.2 6.5 %shard_map.309 = (bf16[384,512]{1,0:T(8,128)(2,1)S(1)}, bf16[4,128,512]{2,1,0:T(8,128)(2,1)S(1)}, bf16[4,128,512]{2,1,0:T(8,128)(2,1)S(1)}, bf16[4,128,512]{2,1,...) custom-call(s32[2,7]{1,0:T(2,128)S(1)} %stack.37.info, ...), custom_call_target="tpu_custom_call" | custom-call | flops 2013265920 | bytes 4685880 | tf_op jit(solution)/shard_map/pallas_call | solution.py:303
  128.7 2.7 %collective-permute-start.29 = (bf16[2,128,512]{2,1,0:T(8,128)(2,1)S(1)}, bf16[2,128,512]{2,1,0:T(8,128)(2,1)S(1)}, u32[]{:S(2)}, u32[]{:S(2)}) collective-permute-start(bf16[2,128,512]{2,1,0:T(8,128)(2,1)S(1)} %get-tuple-element.214), channel_id=1, source_target_pairs={{0,4},{1,5},{2,6},{3,7},{4,0},{5,1},{6,2},{7,3},{8,12},{9,13},{10,... | collective-permute-start | bytes 786440 | tf_op jit(solution)/shard_map/ppermute | solution.py:45
  131.4 10.5 %collective-permute-done.27.refs_1_ = bf16[2,128,512]{2,1,0:T(8,128)(2,1)S(1)} collective-permute-done((bf16[2,128,512]{2,1,0:T(8,128)(2,1)S(1)}, bf16[2,128,512]{2,1,0:T(8,128)(2,1)S(1)}, u32[]{:S(2)}, u32[]{:S(2)}) %collective-permute-start.27) | collective-permute-done | bytes 262176 | tf_op jit(solution)/shard_map/ppermute | solution.py:45
  147.2 2.7 %collective-permute-done.28 = bf16[128,512]{1,0:T(8,128)(2,1)S(1)} collective-permute-done((bf16[128,512]{1,0:T(8,128)(2,1)S(1)}, bf16[128,512]{1,0:T(8,128)(2,1)S(1)}, u32[]{:S(2)}, u32[]{:S(2)}) %collective-permute-start.28) | collective-permute-done | bytes 131104 | tf_op jit(solution)/shard_map/ppermute | solution.py:45
  154.6 4.8 %shard_map.315 = (f32[384,512]{1,0:T(8,128)S(1)}, f32[384,512]{1,0:T(8,128)S(1)}, f32[16,1024]{1,0:T(8,128)S(1)}, bf16[16,112,512]{2,1,0:T(8,128)(2,1)S(1)}, bf16[16,112,512]{2,1,0:T(8,128)(2,1)S(1)}) custom-call(s32[2,7]{1,0:T(2,128)S(1)} %stack.37.info, bf16[128,512]{1,0:T(8,128)(2,1)S(1)} %add_convert_fusion.1.key_memory, ...), custom_call_target="tpu_custom_call" | custom-call | flops 1006632960 | bytes 7094328 | tf_op jit(solution)/shard_map/pallas_call | solution.py:303
  160.8 2.6 %collective-permute-done.35.rims = f32[16,1024]{1,0:T(8,128)S(1)} collective-permute-done((f32[16,1024]{1,0:T(8,128)S(1)}, f32[16,1024]{1,0:T(8,128)S(1)}, u32[]{:S(2)}, u32[]{:S(2)}) %collective-permute-start.35) | collective-permute-done | bytes 65568 | tf_op jit(solution)/shard_map/ppermute | solution.py:1014
  163.4 2.9 %shard_map.316 = (bf16[384,512]{1,0:T(8,128)(2,1)}, bf16[16,48,512]{2,1,0:T(8,128)(2,1)S(1)}, bf16[16,48,512]{2,1,0:T(8,128)(2,1)S(1)}) custom-call(s32[2,7]{1,0:T(2,128)S(1)} %stack.37.info, bf16[384,512]{1,0:T(8,128)(2,1)S(1)} %bitcast.81, bf16[400,512]{1,0:T(8,128)(2,1)S(1)} %get-tuple-element.164.normed, ...), custom_call_target="tpu_custom_call" | custom-call | flops 1207959552 | bytes 10502200 | tf_op jit(solution)/shard_map/pallas_call | solution.py:303
  174.8 4.6 %collective-permute-done.40.refs_5_ = bf16[2,144,512]{2,1,0:T(8,128)(2,1)S(1)} collective-permute-done((bf16[2,144,512]{2,1,0:T(8,128)(2,1)S(1)}, bf16[2,144,512]{2,1,0:T(8,128)(2,1)S(1)}, u32[]{:S(2)}, u32[]{:S(2)}) %collective-permute-start.40) | collective-permute-done | bytes 294944 | tf_op jit(solution)/shard_map/ppermute | solution.py:45
  181.3 4.6 %collective-permute-done.38.refs_1_ = bf16[2,2,2,80,512]{4,3,2,1,0:T(8,128)(2,1)S(1)} collective-permute-done((bf16[2,2,2,80,512]{4,3,2,1,0:T(8,128)(2,1)S(1)}, bf16[2,2,2,80,512]{4,3,2,1,0:T(8,128)(2,1)S(1)}, u32[]{:S(2)}, u32[]{:S(2)}) %collective-permute-start.38) | collective-permute-done | bytes 655392 | tf_op jit(solution)/shard_map/ppermute | solution.py:45
  186.6 2.9 %collective-permute-start.49 = (bf16[144,512]{1,0:T(8,128)(2,1)S(1)}, bf16[144,512]{1,0:T(8,128)(2,1)S(1)}, u32[]{:S(2)}, u32[]{:S(2)}) collective-permute-start(bf16[144,512]{1,0:T(8,128)(2,1)S(1)} %get-tuple-element.279), channel_id=1, source_target_pairs={{0,4},{1,5},{2,6},{3,7},{4,0},{5,1},{6,2},{7,3},{8,12},{9,13},{10,... | collective-permute-start | bytes 442376 | tf_op jit(solution)/shard_map/ppermute | solution.py:45
  193.2 2.7 %collective-permute-done.49 = bf16[144,512]{1,0:T(8,128)(2,1)S(1)} collective-permute-done((bf16[144,512]{1,0:T(8,128)(2,1)S(1)}, bf16[144,512]{1,0:T(8,128)(2,1)S(1)}, u32[]{:S(2)}, u32[]{:S(2)}) %collective-permute-start.49) | collective-permute-done | bytes 147488 | tf_op jit(solution)/shard_map/ppermute | solution.py:45
  201.7 4.9 %collective-permute-done.45.refs_1_ = bf16[2,112,512]{2,1,0:T(8,128)(2,1)S(1)} collective-permute-done((bf16[2,112,512]{2,1,0:T(8,128)(2,1)S(1)}, bf16[2,112,512]{2,1,0:T(8,128)(2,1)S(1)}, u32[]{:S(2)}, u32[]{:S(2)}) %collective-permute-start.45) | collective-permute-done | bytes 229408 | tf_op jit(solution)/shard_map/ppermute | solution.py:45
  (153 shorter events, 101.5 us)
Async XLA Ops:
  4.3 16.4 %collective-permute-start = (bf16[80,512]{1,0:T(8,128)(2,1)S(1)}, bf16[80,512]{1,0:T(8,128)(2,1)S(1)}, u32[]{:S(2)}, u32[]{:S(2)}) collective-permute-start(bf16[80,512]{1,0:T(8,128)(2,1)S(1)} %constant_dynamic-update-slice_fusion.refs_0_), channel_id=1, source_target_pairs={{0,4},{1,5},{2,6},{3,7},{4,0},{5,1},{6,2},{7,3},{8,12},{9,13},{10,... | collective-permute-start | bytes 245768 | tf_op jit(solution)/shard_map/ppermute | solution.py:45
  9.1 15.1 %collective-permute-start.1 = (bf16[2,8,512]{2,1,0:T(8,128)(2,1)S(1)}, bf16[2,8,512]{2,1,0:T(8,128)(2,1)S(1)}, u32[]{:S(2)}, u32[]{:S(2)}) collective-permute-start(bf16[2,8,512]{2,1,0:T(8,128)(2,1)S(1)} %slice_bitcast_fusion), channel_id=1, source_target_pairs={{0,1},{1,2},{2,3},{3,4},{4,5},{5,6},{6,7},{8,9},{9,10},{10,11},{11... | collective-permute-start | bytes 49160 | tf_op jit(solution)/shard_map/ppermute | solution.py:831
  22.0 11.1 %collective-permute-start.4 = (bf16[2,80,512]{2,1,0:T(8,128)(2,1)S(1)}, bf16[2,80,512]{2,1,0:T(8,128)(2,1)S(1)}, u32[]{:S(2)}, u32[]{:S(2)}) collective-permute-start(bf16[2,80,512]{2,1,0:T(8,128)(2,1)S(1)} %shard_map.290.refs_0_), channel_id=1, source_target_pairs={{0,4},{1,5},{2,6},{3,7},{4,0},{5,1},{6,2},{7,3},{8,12},{9,13},{10,... | collective-permute-start | bytes 491528 | tf_op jit(solution)/shard_map/ppermute | solution.py:45
  33.7 10.6 %collective-permute-start.6 = (bf16[2,2,80,512]{3,2,1,0:T(8,128)(2,1)S(1)}, bf16[2,2,80,512]{3,2,1,0:T(8,128)(2,1)S(1)}, u32[]{:S(2)}, u32[]{:S(2)}) collective-permute-start(bf16[2,2,80,512]{3,2,1,0:T(8,128)(2,1)S(1)} %shard_map.291.refs_0_), channel_id=1, source_target_pairs={{0,16},{1,17},{2,18},{3,19},{4,20},{5,21},{6,22},{7,23},{8,24},{9,... | collective-permute-start | bytes 983048 | tf_op jit(solution)/shard_map/ppermute | solution.py:45
  38.4 19.3 %collective-permute-start.8 = (bf16[2,2,2,80,512]{4,3,2,1,0:T(8,128)(2,1)S(1)}, bf16[2,2,2,80,512]{4,3,2,1,0:T(8,128)(2,1)S(1)}, u32[]{:S(2)}, u32[]{:S(2)}) collective-permute-start(bf16[2,2,2,80,512]{4,3,2,1,0:T(8,128)(2,1)S(1)} %shard_map.292.refs_0_), channel_id=1, source_target_pairs={{0,16},{1,17},{2,18},{3,19},{4,20},{5,21},{6,22},{7,23},{8,24},{9,... | collective-permute-start | bytes 1966088 | tf_op jit(solution)/shard_map/ppermute | solution.py:45
  44.9 15.4 %collective-permute-start.9 = (bf16[2,2,2,80,512]{4,3,2,1,0:T(8,128)(2,1)S(1)}, bf16[2,2,2,80,512]{4,3,2,1,0:T(8,128)(2,1)S(1)}, u32[]{:S(2)}, u32[]{:S(2)}) collective-permute-start(bf16[2,2,2,80,512]{4,3,2,1,0:T(8,128)(2,1)S(1)} %get-tuple-element.158.refs_0_), channel_id=1, source_target_pairs={{0,8},{1,9},{2,10},{3,11},{4,12},{5,13},{6,14},{7,15},{8,0},{9,1},... | collective-permute-start | bytes 1966088 | tf_op jit(solution)/shard_map/ppermute | solution.py:45
  46.5 11.9 %collective-permute-start.10 = (bf16[2,144,512]{2,1,0:T(8,128)(2,1)S(1)}, bf16[2,144,512]{2,1,0:T(8,128)(2,1)S(1)}, u32[]{:S(2)}, u32[]{:S(2)}) collective-permute-start(bf16[2,144,512]{2,1,0:T(8,128)(2,1)S(1)} %get-tuple-element.160.refs_2_), channel_id=1, source_target_pairs={{0,2},{1,3},{2,0},{3,1},{4,6},{5,7},{6,4},{7,5},{8,10},{9,11},{10,... | collective-permute-start | bytes 884744 | tf_op jit(solution)/shard_map/ppermute | solution.py:45
  61.1 12.8 %collective-permute-start.15 = (bf16[2,2,80,512]{3,2,1,0:T(8,128)(2,1)S(1)}, bf16[2,2,80,512]{3,2,1,0:T(8,128)(2,1)S(1)}, u32[]{:S(2)}, u32[]{:S(2)}) collective-permute-start(bf16[2,2,80,512]{3,2,1,0:T(8,128)(2,1)S(1)} %get-tuple-element.171.refs_2_), channel_id=1, source_target_pairs={{0,8},{1,9},{2,10},{3,11},{4,12},{5,13},{6,14},{7,15},{8,0},{9,1},... | collective-permute-start | bytes 983048 | tf_op jit(solution)/shard_map/ppermute | solution.py:45
  62.7 11.3 %collective-permute-start.16 = (bf16[2,2,64,512]{3,2,1,0:T(8,128)(2,1)S(1)}, bf16[2,2,64,512]{3,2,1,0:T(8,128)(2,1)S(1)}, u32[]{:S(2)}, u32[]{:S(2)}) collective-permute-start(bf16[2,2,64,512]{3,2,1,0:T(8,128)(2,1)S(1)} %get-tuple-element.173.refs_4_), channel_id=1, source_target_pairs={{0,16},{1,17},{2,18},{3,19},{4,20},{5,21},{6,22},{7,23},{8,24},{9,... | collective-permute-start | bytes 786440 | tf_op jit(solution)/shard_map/ppermute | solution.py:45
  76.7 17.2 %collective-permute-start.19 = (bf16[2,2,2,80,512]{4,3,2,1,0:T(8,128)(2,1)S(1)}, bf16[2,2,2,80,512]{4,3,2,1,0:T(8,128)(2,1)S(1)}, u32[]{:S(2)}, u32[]{:S(2)}) collective-permute-start(bf16[2,2,2,80,512]{4,3,2,1,0:T(8,128)(2,1)S(1)} %get-tuple-element.178.refs_2_), channel_id=1, source_target_pairs={{0,16},{1,17},{2,18},{3,19},{4,20},{5,21},{6,22},{7,23},{8,24},{9,... | collective-permute-start | bytes 1966088 | tf_op jit(solution)/shard_map/ppermute | solution.py:45
  78.2 15.7 %collective-permute-start.20 = (bf16[2,2,2,64,512]{4,3,2,1,0:T(8,128)(2,1)S(1)}, bf16[2,2,2,64,512]{4,3,2,1,0:T(8,128)(2,1)S(1)}, u32[]{:S(2)}, u32[]{:S(2)}) collective-permute-start(bf16[2,2,2,64,512]{4,3,2,1,0:T(8,128)(2,1)S(1)} %get-tuple-element.180.refs_4_), channel_id=1, source_target_pairs={{0,8},{1,9},{2,10},{3,11},{4,12},{5,13},{6,14},{7,15},{8,0},{9,1},... | collective-permute-start | bytes 1572872 | tf_op jit(solution)/shard_map/ppermute | solution.py:45
  79.7 12.8 %collective-permute-start.17 = (bf16[2,128,512]{2,1,0:T(8,128)(2,1)S(1)}, bf16[2,128,512]{2,1,0:T(8,128)(2,1)S(1)}, u32[]{:S(2)}, u32[]{:S(2)}) collective-permute-start(bf16[2,128,512]{2,1,0:T(8,128)(2,1)S(1)} %shard_map.300.refs_0_), channel_id=1, source_target_pairs={{0,2},{1,3},{2,0},{3,1},{4,6},{5,7},{6,4},{7,5},{8,10},{9,11},{10,... | collective-permute-start | bytes 786440 | tf_op jit(solution)/shard_map/ppermute | solution.py:45
  79.7 14.2 %collective-permute-start.18 = (bf16[2,128,512]{2,1,0:T(8,128)(2,1)S(1)}, bf16[2,128,512]{2,1,0:T(8,128)(2,1)S(1)}, u32[]{:S(2)}, u32[]{:S(2)}) collective-permute-start(bf16[2,128,512]{2,1,0:T(8,128)(2,1)S(1)} %get-tuple-element.176.refs_0_), channel_id=1, source_target_pairs={{0,4},{1,5},{2,6},{3,7},{4,0},{5,1},{6,2},{7,3},{8,12},{9,13},{10,... | collective-permute-start | bytes 786440 | tf_op jit(solution)/shard_map/ppermute | solution.py:45
  94.7 10.5 %collective-permute-start.23 = (bf16[2,2,2,2,144,512]{5,4,3,2,1,0:T(8,128)(2,1)S(1)}, bf16[2,2,2,2,144,512]{5,4,3,2,1,0:T(8,128)(2,1)S(1)}, u32[]{:S(2)}, u32[]{:S(2)}) collective-permute-start(bf16[2,2,2,2,144,512]{5,4,3,2,1,0:T(8,128)(2,1)S(1)} %get-tuple-element.190.refs_0_), channel_id=1, source_target_pairs={{0,1},{1,0},{2,3},{3,2},{4,5},{5,4},{6,7},{7,6},{8,9},{9,8},{10,11... | collective-permute-start | bytes 7077896 | tf_op jit(solution)/shard_map/ppermute | solution.py:45
  116.0 9.4 %collective-permute-start.26 = (bf16[2,2,2,2,144,512]{5,4,3,2,1,0:T(8,128)(2,1)S(1)}, bf16[2,2,2,2,144,512]{5,4,3,2,1,0:T(8,128)(2,1)S(1)}, u32[]{:S(2)}, u32[]{:S(2)}) collective-permute-start(bf16[2,2,2,2,144,512]{5,4,3,2,1,0:T(8,128)(2,1)S(1)} %bitcast.86), channel_id=1, source_target_pairs={{0,1},{1,0},{2,3},{3,2},{4,5},{5,4},{6,7},{7,6},{8,9},{9,8},{10,11... | collective-permute-start | bytes 7077896 | tf_op jit(solution)/shard_map/ppermute | solution.py:45
  126.2 17.1 %collective-permute-start.30 = (bf16[2,2,2,80,512]{4,3,2,1,0:T(8,128)(2,1)S(1)}, bf16[2,2,2,80,512]{4,3,2,1,0:T(8,128)(2,1)S(1)}, u32[]{:S(2)}, u32[]{:S(2)}) collective-permute-start(bf16[2,2,2,80,512]{4,3,2,1,0:T(8,128)(2,1)S(1)} %get-tuple-element.217), channel_id=1, source_target_pairs={{0,16},{1,17},{2,18},{3,19},{4,20},{5,21},{6,22},{7,23},{8,24},{9,... | collective-permute-start | bytes 1966088 | tf_op jit(solution)/shard_map/ppermute | solution.py:45
  127.2 16.1 %collective-permute-start.31 = (bf16[2,2,2,64,512]{4,3,2,1,0:T(8,128)(2,1)S(1)}, bf16[2,2,2,64,512]{4,3,2,1,0:T(8,128)(2,1)S(1)}, u32[]{:S(2)}, u32[]{:S(2)}) collective-permute-start(bf16[2,2,2,64,512]{4,3,2,1,0:T(8,128)(2,1)S(1)} %get-tuple-element.220), channel_id=1, source_target_pairs={{0,8},{1,9},{2,10},{3,11},{4,12},{5,13},{6,14},{7,15},{8,0},{9,1},... | collective-permute-start | bytes 1572872 | tf_op jit(solution)/shard_map/ppermute | solution.py:45
  128.7 13.1 %collective-permute-start.27 = (bf16[2,128,512]{2,1,0:T(8,128)(2,1)S(1)}, bf16[2,128,512]{2,1,0:T(8,128)(2,1)S(1)}, u32[]{:S(2)}, u32[]{:S(2)}) collective-permute-start(bf16[2,128,512]{2,1,0:T(8,128)(2,1)S(1)} %get-tuple-element.210), channel_id=1, source_target_pairs={{0,2},{1,3},{2,0},{3,1},{4,6},{5,7},{6,4},{7,5},{8,10},{9,11},{10,... | collective-permute-start | bytes 786440 | tf_op jit(solution)/shard_map/ppermute | solution.py:45
  128.7 14.6 %collective-permute-start.29 = (bf16[2,128,512]{2,1,0:T(8,128)(2,1)S(1)}, bf16[2,128,512]{2,1,0:T(8,128)(2,1)S(1)}, u32[]{:S(2)}, u32[]{:S(2)}) collective-permute-start(bf16[2,128,512]{2,1,0:T(8,128)(2,1)S(1)} %get-tuple-element.214), channel_id=1, source_target_pairs={{0,4},{1,5},{2,6},{3,7},{4,0},{5,1},{6,2},{7,3},{8,12},{9,13},{10,... | collective-permute-start | bytes 786440 | tf_op jit(solution)/shard_map/ppermute | solution.py:45
  159.4 9.1 %collective-permute-start.36 = (bf16[2,2,2,2,112,512]{5,4,3,2,1,0:T(8,128)(2,1)S(1)}, bf16[2,2,2,2,112,512]{5,4,3,2,1,0:T(8,128)(2,1)S(1)}, u32[]{:S(2)}, u32[]{:S(2)}) collective-permute-start(bf16[2,2,2,2,112,512]{5,4,3,2,1,0:T(8,128)(2,1)S(1)} %bitcast.87), channel_id=1, source_target_pairs={{0,1},{1,0},{2,3},{3,2},{4,5},{5,4},{6,7},{7,6},{8,9},{9,8},{10,11... | collective-permute-start | bytes 5505032 | tf_op jit(solution)/shard_map/ppermute | solution.py:45
  169.2 16.7 %collective-permute-start.38 = (bf16[2,2,2,80,512]{4,3,2,1,0:T(8,128)(2,1)S(1)}, bf16[2,2,2,80,512]{4,3,2,1,0:T(8,128)(2,1)S(1)}, u32[]{:S(2)}, u32[]{:S(2)}) collective-permute-start(bf16[2,2,2,80,512]{4,3,2,1,0:T(8,128)(2,1)S(1)} %get-tuple-element.251), channel_id=1, source_target_pairs={{0,16},{1,17},{2,18},{3,19},{4,20},{5,21},{6,22},{7,23},{8,24},{9,... | collective-permute-start | bytes 1966088 | tf_op jit(solution)/shard_map/ppermute | solution.py:45
  172.1 9.2 %collective-permute-start.39 = (bf16[2,2,2,32,512]{4,3,2,1,0:T(8,128)(2,1)S(1)}, bf16[2,2,2,32,512]{4,3,2,1,0:T(8,128)(2,1)S(1)}, u32[]{:S(2)}, u32[]{:S(2)}) collective-permute-start(bf16[2,2,2,32,512]{4,3,2,1,0:T(8,128)(2,1)S(1)} %get-tuple-element.254), channel_id=1, source_target_pairs={{0,8},{1,9},{2,10},{3,11},{4,12},{5,13},{6,14},{7,15},{8,0},{9,1},... | collective-permute-start | bytes 786440 | tf_op jit(solution)/shard_map/ppermute | solution.py:45
  173.6 16.9 %collective-permute-start.41 = (bf16[2,2,2,48,512]{4,3,2,1,0:T(8,128)(2,1)S(1)}, bf16[2,2,2,48,512]{4,3,2,1,0:T(8,128)(2,1)S(1)}, u32[]{:S(2)}, u32[]{:S(2)}) collective-permute-start(bf16[2,2,2,48,512]{4,3,2,1,0:T(8,128)(2,1)S(1)} %get-tuple-element.259), channel_id=1, source_target_pairs={{0,8},{1,9},{2,10},{3,11},{4,12},{5,13},{6,14},{7,15},{8,0},{9,1},... | collective-permute-start | bytes 1179656 | tf_op jit(solution)/shard_map/ppermute | solution.py:45
  186.6 9.2 %collective-permute-start.49 = (bf16[144,512]{1,0:T(8,128)(2,1)S(1)}, bf16[144,512]{1,0:T(8,128)(2,1)S(1)}, u32[]{:S(2)}, u32[]{:S(2)}) collective-permute-start(bf16[144,512]{1,0:T(8,128)(2,1)S(1)} %get-tuple-element.279), channel_id=1, source_target_pairs={{0,4},{1,5},{2,6},{3,7},{4,0},{5,1},{6,2},{7,3},{8,12},{9,13},{10,... | collective-permute-start | bytes 442376 | tf_op jit(solution)/shard_map/ppermute | solution.py:45
  (28 other events, 170.3 us)
where the time goes:
time: 218 us; the launch traced here: 216 us
  waiting for transfers between devices  92.1 us (42%)
  starting transfers between devices  52.9 us (24%)
  Pallas kernels  50.7 us (23%)
  local copies, waits for them, and re-layouts  16.3 us (7%)
  other arithmetic  3.28 us (2%)
    ppermute x48, waiting for transfers between devices, swap(): lax.ppermute(array, AXES, [(i, i ^ mask) for i in range(device_count())])  89.5 us
    pallas_call x37, Pallas kernels, kernel(): pl.pallas_call(body, in_specs=[pl.BlockSpec(memory_space=spec.get(a.dtype...  50.7 us
    ppermute x48, starting transfers between devices, swap(): lax.ppermute(array, AXES, [(i, i ^ mask) for i in range(device_count())])  50.2 us
    unnamed x17, local copies, waits for them, and re-layouts  9.47 us
  transfers between devices with their start and end apart: 50, of which 31 were waited for; matrix products, arithmetic and copies ran while one was open for 7% of the time, Pallas kernels for 15%

commit v1 on v0

--- a/solution.py
+++ b/solution.py
@@ -298,6 +298,29 @@
     return rows.reshape(GROUPS * UNIT * size, rows.shape[-1])
 
 
+def pack_kernel(moves, counts, *refs):
+    inputs, outs, sems = refs[: counts[0]], refs[counts[0] : -1], refs[-1]
+    copies = []
+    for at, (source, where, out, start, rows) in enumerate(moves):
+        into = outs[out].at[pl.ds(start, rows)]
+        piece = inputs[source] if where is None else inputs[source].at[where]
+        copies.append(pltpu.make_async_copy(piece, into, sems.at[at]))
+        copies[-1].start()
+    for copy in copies:
+        copy.wait()
+
+
+def packed(args, moves, shapes):
+    return pl.pallas_call(
+        functools.partial(pack_kernel, moves, (len(args),)),
+        in_specs=[pl.BlockSpec(memory_space=pltpu.HBM) for _ in args],
+        out_specs=[pl.BlockSpec(memory_space=pltpu.VMEM) for _ in shapes],
+        out_shape=[jax.ShapeDtypeStruct(shape, BF16) for shape in shapes],
+        scratch_shapes=[pltpu.SemaphoreType.DMA((len(moves),))],
+        compiler_params=pltpu.CompilerParams(vmem_limit_bytes=62 << 20),
+    )(*args)
+
+
 def kernel(body, args, outs, flops, limit, scratch=()):
     spec = {jnp.dtype(jnp.int32): pltpu.SMEM}
     return pl.pallas_call(
@@ -368,36 +391,37 @@
     return (place >= UNIT * k) & (place < UNIT * (k + 1))
 
 
-def window_map(micro, each, tap):
-    slots = each // 3
-    shape = (micro * slots, micro * (each + RIM))
-    row, place = iota(shape, 0), iota(shape, 1)
-    m = jnp.zeros(shape, jnp.int32)
-    for i in range(1, micro):
-        m = m + jnp.where(row >= slots * i, 1, 0)
-    source = 3 * (row - slots * m) - 2 + tap
-    rim = micro * each + RIM * m + RIM + source
-    target = jnp.where(source >= 0, each * m + source, rim)
-    return jnp.where(place == target, 1.0, 0.0).astype(BF16)
-
-
-def keep_and_compress(info, low, weights, kept, window, memory):
+def line_cuts(line):
+    micro, cuts = line.shape[:2]
+    found = [(m, c) for m in range(micro) for c in range(cuts)]
+    return [(m, c, slice(128 * c, 128 * (c + 1))) for m, c in found]
+
+
+def keep_and_compress(info, low, weights, kept, window, memory, line):
     micro = info.shape[0]
     each = low.shape[0] // micro - RIM
+    slots = each // 3
+    count = micro * each
     valid = [valid_column(info, m, info[m, 4], each) for m in range(micro)]
     valid += [valid_column(info, m, info[m, 4] - RIM, RIM) for m in range(micro)]
     rows = (dot(low, tile(weights, 0)) * jnp.concatenate(valid, axis=0)).astype(BF16)
-    kept[...] = rows
+    kept[...] = rows[:count]
+    rows = rows.astype(F32)
+    for m, cut, cols in line_cuts(line):
+        line[m, cut, :RIM] = rows[count + RIM * m : count + RIM * (m + 1), cols]
+        line[m, cut, RIM:] = rows[each * m : each * (m + 1), cols]
     total = None
     for tap in range(3):
-        taken = dot(window_map(micro, each, tap), rows).astype(BF16)
-        window[tap] = taken
-        part = dot(taken, tile(weights, 1 + tap))
+        start = RIM - 2 + tap
+        for m, cut, cols in line_cuts(line):
+            taken = line[m, cut, pl.ds(start, slots, stride=3), :]
+            window[tap, slots * m : slots * (m + 1), cols] = taken.astype(BF16)
+        part = dot(window[tap], tile(weights, 1 + tap))
         total = part if total is None else total + part
     memory[...] = total.astype(BF16)
 
 
-def key_kernel(info, tok, halo, weights, normed, kept, window, memory, vec):
+def key_kernel(info, tok, halo, weights, normed, kept, window, memory, vec, line):
     width = tok.shape[-1]
     lanes = width // 2
     fine, wide, own_fine, own_wide = vector_maps(width)
@@ -414,12 +438,12 @@
     unit, _ = unit_norm(values)
     low = (unit * vectors[0] + vectors[1]).astype(BF16)
     normed[...] = low
-    keep_and_compress(info, low, weights, kept, window, memory)
-
-
-def value_kernel(info, normed, weights, query, kept, window, memory):
+    keep_and_compress(info, low, weights, kept, window, memory, line)
+
+
+def value_kernel(info, normed, weights, query, kept, window, memory, line):
     low = normed[...]
-    keep_and_compress(info, low, weights, kept, window, memory)
+    keep_and_compress(info, low, weights, kept, window, memory, line)
     query[...] = dot(low[: query.shape[0]], tile(weights, 4)).astype(BF16)
 
 
@@ -680,29 +704,33 @@
     rims,
     keep,
     send,
+    line,
 ):
     micro = info.shape[0]
     count, width = key_grad.shape
     each = count // micro
     flag = info[0, 5]
-    places = [window_map(micro, each, tap) for tap in range(3)]
+    own_slots = each // 3
+    edge = iota((RIM, width), 0) >= RIM - 2
     sides = (
         (key_memory, key_window, key_weights, key_grad),
         (value_memory, value_window, value_weights, value_grad),
     )
     for kind, (memory, window, weights, out) in enumerate(sides):
         grad = memory[...]
-        total = None
         for tap in range(3):
             window_t = even_first(flag, window[tap].T, UNIT)
             deal_tile(dot(window_t, grad), 4 * kind + tap, keep, send)
             part = dot(grad, tile(weights, 1 + tap), NT)
-            high = part.astype(BF16)
-            rest = (part - high.astype(F32)).astype(BF16)
-            part = dot(places[tap], high, TN) + dot(places[tap], rest, TN)
-            total = part if total is None else total + part
-        out[...] = total[:count]
-        rims[:, width * kind : width * (kind + 1)] = total[count:]
+            for m, cut, cols in line_cuts(line):
+                rows = slice(own_slots * m, own_slots * (m + 1))
+                line[m, cut, pl.ds(tap, own_slots, stride=3), :] = part[rows, cols]
+        for m, cut, cols in line_cuts(line):
+            out[each * m : each * (m + 1), cols] = line[m, cut]
+        for m in range(micro):
+            first = pltpu.roll(out[each * m : each * m + RIM, :], RIM - 2, 0)
+            into = (slice(RIM * m, RIM * (m + 1)), slice(width * kind, width * (kind + 1)))
+            rims[into] = jnp.where(edge, first, 0.0)
     low_t = even_first(flag, normed[:count, :].T, UNIT)
     deal_tile(dot(low_t, grad_query[...]), 3, keep, send)
 
@@ -735,10 +763,13 @@
     flag = info[0, 5]
     low_t = even_first(flag, normed[:count, :].T, UNIT)
     grad_low = dot(grad_query[...], tile(value_weights, 4), NT)
+    inner = iota((each, width), 0) < each - 2
     sides = ((key_grad, own_key, key_weights), (value_grad, own_value, value_weights))
     for kind, (grad, own, weights) in enumerate(sides):
-        total[...] = grad[...] + own[...]
         for m in range(micro):
+            rows = slice(each * m, each * (m + 1))
+            moved = pltpu.roll(grad[rows, :], each - 2, 0)
+            total[rows, :] = jnp.where(inner, moved, 0.0) + own[rows, :]
             rows = slice(each * (m + 1) - RIM, each * (m + 1))
             rim = rims[RIM * m : RIM * (m + 1), width * kind : width * (kind + 1)]
             total[rows, :] = total[rows, :] + rim
@@ -818,10 +849,23 @@
     seats = [jnp.full_like(start, seat) for seat in seats]
     info = [1 + lengths[:, 0], start, start + lengths[:, 1], start + second_pad]
     info = jnp.stack(info + seats, axis=1).astype(jnp.int32)
-    first = jnp.concatenate([w_key, *conv_key, vectors], axis=0)
-    second = jnp.concatenate([w_value, *conv_value, w_query], axis=0)
-    ups = [w_up[:, width * c : width * (c + 1)] for c in range(wide)]
-    rest = jnp.concatenate([w_out] + ups + [w_down], axis=0)
+    if whole:
+        moves = [(kind, None, kind, 0, UNIT) for kind in range(2)]
+        moves += [(2 + k, tap, k, UNIT * (1 + tap), UNIT) for k in range(2) for tap in range(3)]
+        moves += [(4 + kind, None, kind, 4 * UNIT, UNIT) for kind in range(2)]
+        moves += [(6, None, 2, 0, UNIT)]
+        for c in range(wide):
+            cols = (slice(None), pl.ds(width * c, width))
+            moves.append((7, cols, 2, UNIT * (1 + c), UNIT))
+        moves.append((8, None, 2, UNIT * (1 + wide), UNIT * wide))
+        rows = (5 * UNIT, 5 * UNIT, (1 + 2 * wide) * UNIT)
+        args = (w_key, w_value, conv_key, conv_value, vectors, w_query, w_out, w_up, w_down)
+        first, second, rest = packed(args, moves, [(r, width) for r in rows])
+    else:
+        first = jnp.concatenate([w_key, *conv_key, vectors], axis=0)
+        second = jnp.concatenate([w_value, *conv_value, w_query], axis=0)
+        ups = [w_up[:, width * c : width * (c + 1)] for c in range(wide)]
+        rest = jnp.concatenate([w_out] + ups + [w_down], axis=0)
     rest_rows = rest.shape[0]
     upper_rows = share * (1 + wide)
     one, two, both = Gather(order, first), Gather(order, second), Gather(order, rest)
@@ -875,13 +919,15 @@
 
     padded = (all_tokens + micro * RIM, width)
     windows = (3, slots, width)
+    line = (pltpu.VMEM((micro, width // 128, RIM + each, 128), F32),)
 
     normed, keys, key_window, memory_key, vec = kernel(
         key_kernel,
         (info, order.turn(tok), halo, first),
-        ((padded, BF16), (padded, BF16), (windows, BF16), ((slots, width), BF16), ((16, width), F32)),
+        ((padded, BF16), (rows, BF16), (windows, BF16), ((slots, width), BF16), ((16, width), F32)),
         2 * matmul,
         limits[0],
+        line,
     )
     order.done(memory_key)
     keys_side = Gather(order, memory_key)
@@ -890,9 +936,10 @@
     query, values, value_window, memory_value = kernel(
         value_kernel,
         (info, normed, second),
-        ((rows, BF16), (padded, BF16), (windows, BF16), ((slots, width), BF16)),
+        ((rows, BF16), (rows, BF16), (windows, BF16), ((slots, width), BF16)),
         3 * matmul,
         limits[1],
+        line,
     )
     order.done(memory_value)
     values_side = Gather(order, memory_value)
@@ -900,19 +947,17 @@
     for at in range(1, max(len(across), len(along))):
         jobs = []
         if at < len(along):
-            keys_side.place()
-            keys_side.go(along[at])
-            jobs.append((values_side, ()))
+            jobs += [(keys_side, ()), (values_side, ())]
         if at < len(across):
             jobs.append((both, ()))
         place(order, *jobs)
         if at < len(along):
+            keys_side.go(along[at])
             values_side.go(back[at])
         if at < len(across):
             both.go(across[at], across[-1 - at])
-    keys_side.place()
+    place(order, (keys_side, ()), (values_side, ()), (both, (rest_rows,)))
     keys_side.go(1)
-    place(order, (values_side, ()), (both, (rest_rows,)))
     values_side.go(1)
     both.go(1)
     memories = [keys_side.place().whole(), values_side.place().whole()]
@@ -1009,6 +1054,7 @@
         ((rows, F32), (rows, F32), ((micro * RIM, 2 * width), F32)) + pieces(7),
         5 * matmul,
         limits[5],
+        (pltpu.VMEM((micro, width // 128, each, 128), F32),),
     )
     order.done(rims)
     rims = lax.ppermute(rims, "seq", [(i + 1, i) for i in range(seq - 1)])

time: 218 us -> 210 us (0.963)
  local copies, waits for them, and re-layouts: 16.3 us -> 7.21 us
  waiting for transfers between devices: 92.1 us -> 94.5 us
    unnamed x17 -> x10, local copies, waits for them, and re-layouts: 9.47 us -> 1.91 us
    pallas_call x37 -> x35, Pallas kernels: 50.7 us -> 47.1 us  [kernel(): pl.pallas_call(body, in_specs=[pl.BlockSpec(memory_space=spec.get(a.dtype...]
    ppermute x48, waiting for transfers between devices: 89.5 us -> 91.9 us  [swap(): lax.ppermute(array, AXES, [(i, i ^ mask) for i in range(device_count())])]
  transfers between devices with their start and end apart: 50 -> 50, of which waited for: 31 -> 35; matrix products, arithmetic and copies ran while one was open for 7% -> 3% of each run, Pallas kernels for 15% -> 14%
where the time goes in v1:
time: 210 us
  waiting for transfers between devices  94.5 us (45%)
  starting transfers between devices  54.2 us (26%)
  Pallas kernels  48.9 us (23%)
  local copies, waits for them, and re-layouts  7.21 us (3%)
  other arithmetic  3.89 us (2%)
    ppermute x48, waiting for transfers between devices, swap(): lax.ppermute(array, AXES, [(i, i ^ mask) for i in range(device_count())])  91.9 us
    ppermute x48, starting transfers between devices, swap(): lax.ppermute(array, AXES, [(i, i ^ mask) for i in range(device_count())])  51.5 us
    pallas_call x35, Pallas kernels, kernel(): pl.pallas_call(body, in_specs=[pl.BlockSpec(memory_space=spec.get(a.dtype...  47.1 us
  transfers between devices with their start and end apart: 50, of which 35 were waited for; matrix products, arithmetic and copies ran while one was open for 3% of the time, Pallas kernels for 14%

profile of v1, /device:TPU:0, one launch (start us, length us, event | category | flops | bytes accessed | tf_op | source)
XLA Modules:
  0.0 209.8 jit_solution(573328000653082338)
XLA Ops:
  4.0 4.1 %collective-permute-start = (bf16[80,512]{1,0:T(8,128)(2,1)}, bf16[80,512]{1,0:T(8,128)(2,1)S(1)}, u32[]{:S(2)}, u32[]{:S(2)}) collective-permute-start(bf16[80,512]{1,0:T(8,128)(2,1)} %get-tuple-element.153.refs_0_), channel_id=1, source_target_pairs={{0,4},{1,5},{2,6},{3,7},{4,0},{5,1},{6,2},{7,3},{8,12},{9,13},{10,... | collective-permute-start | bytes 245768 | tf_op jit(solution)/shard_map/ppermute | solution.py:45
  16.4 3.3 %collective-permute-start.4 = (bf16[2,80,512]{2,1,0:T(8,128)(2,1)S(1)}, bf16[2,80,512]{2,1,0:T(8,128)(2,1)S(1)}, u32[]{:S(2)}, u32[]{:S(2)}) collective-permute-start(bf16[2,80,512]{2,1,0:T(8,128)(2,1)S(1)} %shard_map.291.refs_0_), channel_id=1, source_target_pairs={{0,4},{1,5},{2,6},{3,7},{4,0},{5,1},{6,2},{7,3},{8,12},{9,13},{10,... | collective-permute-start | bytes 491528 | tf_op jit(solution)/shard_map/ppermute | solution.py:45
  23.2 5.2 %collective-permute-done.4.refs_1_ = bf16[2,80,512]{2,1,0:T(8,128)(2,1)S(1)} collective-permute-done((bf16[2,80,512]{2,1,0:T(8,128)(2,1)S(1)}, bf16[2,80,512]{2,1,0:T(8,128)(2,1)S(1)}, u32[]{:S(2)}, u32[]{:S(2)}) %collective-permute-start.4) | collective-permute-done | bytes 163872 | tf_op jit(solution)/shard_map/ppermute | solution.py:45
  32.7 5.9 %collective-permute-done.7.refs_3_ = bf16[144,512]{1,0:T(8,128)(2,1)S(1)} collective-permute-done((bf16[144,512]{1,0:T(8,128)(2,1)}, bf16[144,512]{1,0:T(8,128)(2,1)S(1)}, u32[]{:S(2)}, u32[]{:S(2)}) %collective-permute-start.7) | collective-permute-done | bytes 147488 | tf_op jit(solution)/shard_map/ppermute | solution.py:45
  41.7 11.0 %collective-permute-done.8.refs_1_ = bf16[2,2,2,80,512]{4,3,2,1,0:T(8,128)(2,1)S(1)} collective-permute-done((bf16[2,2,2,80,512]{4,3,2,1,0:T(8,128)(2,1)S(1)}, bf16[2,2,2,80,512]{4,3,2,1,0:T(8,128)(2,1)S(1)}, u32[]{:S(2)}, u32[]{:S(2)}) %collective-permute-start.8) | collective-permute-done | bytes 655392 | tf_op jit(solution)/shard_map/ppermute | solution.py:45
  53.4 2.5 %collective-permute-done.9.refs_1_ = bf16[2,2,2,80,512]{4,3,2,1,0:T(8,128)(2,1)S(1)} collective-permute-done((bf16[2,2,2,80,512]{4,3,2,1,0:T(8,128)(2,1)S(1)}, bf16[2,2,2,80,512]{4,3,2,1,0:T(8,128)(2,1)S(1)}, u32[]{:S(2)}, u32[]{:S(2)}) %collective-permute-start.9) | collective-permute-done | bytes 655392 | tf_op jit(solution)/shard_map/ppermute | solution.py:45
  64.0 2.4 %collective-permute-start.14 = (bf16[128,512]{1,0:T(8,128)(2,1)S(1)}, bf16[128,512]{1,0:T(8,128)(2,1)S(1)}, u32[]{:S(2)}, u32[]{:S(2)}) collective-permute-start(bf16[128,512]{1,0:T(8,128)(2,1)S(1)} %get-tuple-element.177.refs_2_), channel_id=1, source_target_pairs={{0,2},{1,3},{2,0},{3,1},{4,6},{5,7},{6,4},{7,5},{8,10},{9,11},{10,... | collective-permute-start | bytes 393224 | tf_op jit(solution)/shard_map/ppermute | solution.py:45
  66.9 3.1 %collective-permute-done.13.refs_1_ = bf16[128,512]{1,0:T(8,128)(2,1)S(1)} collective-permute-done((bf16[128,512]{1,0:T(8,128)(2,1)S(1)}, bf16[128,512]{1,0:T(8,128)(2,1)S(1)}, u32[]{:S(2)}, u32[]{:S(2)}) %collective-permute-start.13) | collective-permute-done | bytes 131104 | tf_op jit(solution)/shard_map/ppermute | solution.py:45
  70.0 2.4 %collective-permute-done.14.refs_3_ = bf16[128,512]{1,0:T(8,128)(2,1)S(1)} collective-permute-done((bf16[128,512]{1,0:T(8,128)(2,1)S(1)}, bf16[128,512]{1,0:T(8,128)(2,1)S(1)}, u32[]{:S(2)}, u32[]{:S(2)}) %collective-permute-start.14) | collective-permute-done | bytes 131104 | tf_op jit(solution)/shard_map/ppermute | solution.py:45
  77.4 10.8 %collective-permute-done.18.refs_3_ = bf16[2,128,512]{2,1,0:T(8,128)(2,1)S(1)} collective-permute-done((bf16[2,128,512]{2,1,0:T(8,128)(2,1)S(1)}, bf16[2,128,512]{2,1,0:T(8,128)(2,1)S(1)}, u32[]{:S(2)}, u32[]{:S(2)}) %collective-permute-start.18) | collective-permute-done | bytes 262176 | tf_op jit(solution)/shard_map/ppermute | solution.py:45
  90.9 4.7 %collective-permute-done.21.refs_1_ = bf16[2,2,128,512]{3,2,1,0:T(8,128)(2,1)S(1)} collective-permute-done((bf16[2,2,128,512]{3,2,1,0:T(8,128)(2,1)S(1)}, bf16[2,2,128,512]{3,2,1,0:T(8,128)(2,1)S(1)}, u32[]{:S(2)}, u32[]{:S(2)}) %collective-permute-start.21) | collective-permute-done | bytes 524320 | tf_op jit(solution)/shard_map/ppermute | solution.py:45
  97.0 3.8 %shard_map.305 = (f32[384,512]{1,0:T(8,128)S(1)}, f32[384,128]{1,0:T(8,128)S(1)}) custom-call(s32[2,7]{1,0:T(2,128)S(1)} %stack.37.info, bf16[384,512]{1,0:T(8,128)(2,1)S(1)} %get-tuple-element.205.query, bf16[384,512]{1,0:T(8,128)(2,1)S(1)} %get-tuple-element.197.keys, bf16[384,512]{1,0:T(8,128)(2,1)S(1)} %get-tuple-element.198.values, ...), custom_call_target="tpu_custom_call" | custom-call | flops 805306368 | bytes 3276856 | tf_op jit(solution)/shard_map/pallas_call | solution.py:326
  101.8 9.8 %shard_map.307 = (bf16[384,512]{1,0:T(8,128)(2,1)}, f32[384,512]{1,0:T(8,128)S(1)}, bf16[384,512]{1,0:T(8,128)(2,1)S(1)}, bf16[16,144,512]{2,1,0:T(8,128)(2,1)S(...) custom-call(s32[2,7]{1,0:T(2,128)S(1)} %stack.37.info, bf16[384,512]{1,0:T(8,128)(2,1)S(1)} %bitcast.68, ...), custom_call_target="tpu_custom_call" | custom-call | flops 5435817984 | bytes 6324280 | tf_op jit(solution)/shard_map/pallas_call | solution.py:326
  111.8 6.5 %shard_map.308 = (bf16[384,512]{1,0:T(8,128)(2,1)S(1)}, bf16[4,128,512]{2,1,0:T(8,128)(2,1)S(1)}, bf16[4,128,512]{2,1,0:T(8,128)(2,1)S(1)}, bf16[4,128,512]{2,1,...) custom-call(s32[2,7]{1,0:T(2,128)S(1)} %stack.37.info, ...), custom_call_target="tpu_custom_call" | custom-call | flops 2013265920 | bytes 4653112 | tf_op jit(solution)/shard_map/pallas_call | solution.py:326
  126.2 10.5 %collective-permute-done.27.refs_1_ = bf16[2,128,512]{2,1,0:T(8,128)(2,1)S(1)} collective-permute-done((bf16[2,128,512]{2,1,0:T(8,128)(2,1)S(1)}, bf16[2,128,512]{2,1,0:T(8,128)(2,1)S(1)}, u32[]{:S(2)}, u32[]{:S(2)}) %collective-permute-start.27) | collective-permute-done | bytes 262176 | tf_op jit(solution)/shard_map/ppermute | solution.py:45
  147.5 2.6 %collective-permute-done.32.refs_1_ = bf16[2,2,80,512]{3,2,1,0:T(8,128)(2,1)S(1)} collective-permute-done((bf16[2,2,80,512]{3,2,1,0:T(8,128)(2,1)S(1)}, bf16[2,2,80,512]{3,2,1,0:T(8,128)(2,1)S(1)}, u32[]{:S(2)}, u32[]{:S(2)}) %collective-permute-start.32) | collective-permute-done | bytes 327712 | tf_op jit(solution)/shard_map/ppermute | solution.py:45
  150.7 2.9 %shard_map.314 = (f32[384,512]{1,0:T(8,128)S(1)}, f32[384,512]{1,0:T(8,128)S(1)}, f32[16,1024]{1,0:T(8,128)S(1)}, bf16[16,112,512]{2,1,0:T(8,128)(2,1)S(1)}, bf16[16,112,512]{2,1,0:T(8,128)(2,1)S(1)}) custom-call(s32[2,7]{1,0:T(2,128)S(1)} %stack.37.info, bf16[128,512]{1,0:T(8,128)(2,1)S(1)} %add_convert_fusion.1.key_memory, ...), custom_call_target="tpu_custom_call" | custom-call | flops 1006632960 | bytes 7094328 | tf_op jit(solution)/shard_map/pallas_call | solution.py:326
  155.0 2.6 %collective-permute-done.35.rims = f32[16,1024]{1,0:T(8,128)S(1)} collective-permute-done((f32[16,1024]{1,0:T(8,128)S(1)}, f32[16,1024]{1,0:T(8,128)S(1)}, u32[]{:S(2)}, u32[]{:S(2)}) %collective-permute-start.35) | collective-permute-done | bytes 65568 | tf_op jit(solution)/shard_map/ppermute | solution.py:1060
  157.6 2.9 %shard_map.315 = (bf16[384,512]{1,0:T(8,128)(2,1)}, bf16[16,48,512]{2,1,0:T(8,128)(2,1)S(1)}, bf16[16,48,512]{2,1,0:T(8,128)(2,1)S(1)}) custom-call(s32[2,7]{1,0:T(2,128)S(1)} %stack.37.info, bf16[384,512]{1,0:T(8,128)(2,1)S(1)} %bitcast.69, bf16[400,512]{1,0:T(8,128)(2,1)S(1)} %get-tuple-element.173.normed, ...), custom_call_target="tpu_custom_call" | custom-call | flops 1207959552 | bytes 10502200 | tf_op jit(solution)/shard_map/pallas_call | solution.py:326
  168.5 4.2 %collective-permute-done.40.refs_5_ = bf16[2,144,512]{2,1,0:T(8,128)(2,1)S(1)} collective-permute-done((bf16[2,144,512]{2,1,0:T(8,128)(2,1)S(1)}, bf16[2,144,512]{2,1,0:T(8,128)(2,1)S(1)}, u32[]{:S(2)}, u32[]{:S(2)}) %collective-permute-start.40) | collective-permute-done | bytes 294944 | tf_op jit(solution)/shard_map/ppermute | solution.py:45
  175.0 5.2 %collective-permute-done.38.refs_1_ = bf16[2,2,2,80,512]{4,3,2,1,0:T(8,128)(2,1)S(1)} collective-permute-done((bf16[2,2,2,80,512]{4,3,2,1,0:T(8,128)(2,1)S(1)}, bf16[2,2,2,80,512]{4,3,2,1,0:T(8,128)(2,1)S(1)}, u32[]{:S(2)}, u32[]{:S(2)}) %collective-permute-start.38) | collective-permute-done | bytes 655392 | tf_op jit(solution)/shard_map/ppermute | solution.py:45
  186.0 3.8 %collective-permute-done.49 = bf16[144,512]{1,0:T(8,128)(2,1)S(1)} collective-permute-done((bf16[144,512]{1,0:T(8,128)(2,1)S(1)}, bf16[144,512]{1,0:T(8,128)(2,1)S(1)}, u32[]{:S(2)}, u32[]{:S(2)}) %collective-permute-start.49) | collective-permute-done | bytes 147488 | tf_op jit(solution)/shard_map/ppermute | solution.py:45
  195.9 4.0 %collective-permute-done.45.refs_1_ = bf16[2,112,512]{2,1,0:T(8,128)(2,1)S(1)} collective-permute-done((bf16[2,112,512]{2,1,0:T(8,128)(2,1)S(1)}, bf16[2,112,512]{2,1,0:T(8,128)(2,1)S(1)}, u32[]{:S(2)}, u32[]{:S(2)}) %collective-permute-start.45) | collective-permute-done | bytes 229408 | tf_op jit(solution)/shard_map/ppermute | solution.py:45
  202.8 2.3 %collective-permute-start.48 = (bf16[112,512]{1,0:T(8,128)(2,1)S(1)}, bf16[112,512]{1,0:T(8,128)(2,1)S(1)}, u32[]{:S(2)}, u32[]{:S(2)}) collective-permute-start(bf16[112,512]{1,0:T(8,128)(2,1)S(1)} %get-tuple-element.287), channel_id=1, source_target_pairs={{0,4},{1,5},{2,6},{3,7},{4,0},{5,1},{6,2},{7,3},{8,12},{9,13},{10,... | collective-permute-start | bytes 344072 | tf_op jit(solution)/shard_map/ppermute | solution.py:45
  (143 shorter events, 92.1 us)
Async XLA Ops:
  4.0 9.3 %collective-permute-start = (bf16[80,512]{1,0:T(8,128)(2,1)}, bf16[80,512]{1,0:T(8,128)(2,1)S(1)}, u32[]{:S(2)}, u32[]{:S(2)}) collective-permute-start(bf16[80,512]{1,0:T(8,128)(2,1)} %get-tuple-element.153.refs_0_), channel_id=1, source_target_pairs={{0,4},{1,5},{2,6},{3,7},{4,0},{5,1},{6,2},{7,3},{8,12},{9,13},{10,... | collective-permute-start | bytes 245768 | tf_op jit(solution)/shard_map/ppermute | solution.py:45
  8.8 11.9 %collective-permute-start.1 = (bf16[2,8,512]{2,1,0:T(8,128)(2,1)S(1)}, bf16[2,8,512]{2,1,0:T(8,128)(2,1)S(1)}, u32[]{:S(2)}, u32[]{:S(2)}) collective-permute-start(bf16[2,8,512]{2,1,0:T(8,128)(2,1)S(1)} %slice_bitcast_fusion), channel_id=1, source_target_pairs={{0,1},{1,2},{2,3},{3,4},{4,5},{5,6},{6,7},{8,9},{9,10},{10,11},{11... | collective-permute-start | bytes 49160 | tf_op jit(solution)/shard_map/ppermute | solution.py:875
  16.4 11.9 %collective-permute-start.4 = (bf16[2,80,512]{2,1,0:T(8,128)(2,1)S(1)}, bf16[2,80,512]{2,1,0:T(8,128)(2,1)S(1)}, u32[]{:S(2)}, u32[]{:S(2)}) collective-permute-start(bf16[2,80,512]{2,1,0:T(8,128)(2,1)S(1)} %shard_map.291.refs_0_), channel_id=1, source_target_pairs={{0,4},{1,5},{2,6},{3,7},{4,0},{5,1},{6,2},{7,3},{8,12},{9,13},{10,... | collective-permute-start | bytes 491528 | tf_op jit(solution)/shard_map/ppermute | solution.py:45
  21.6 9.0 %collective-permute-start.5 = (bf16[2,2,80,512]{3,2,1,0:T(8,128)(2,1)S(1)}, bf16[2,2,80,512]{3,2,1,0:T(8,128)(2,1)S(1)}, u32[]{:S(2)}, u32[]{:S(2)}) collective-permute-start(bf16[2,2,80,512]{3,2,1,0:T(8,128)(2,1)S(1)} %shard_map.290.refs_0_), channel_id=1, source_target_pairs={{0,8},{1,9},{2,10},{3,11},{4,12},{5,13},{6,14},{7,15},{8,0},{9,1},... | collective-permute-start | bytes 983048 | tf_op jit(solution)/shard_map/ppermute | solution.py:45
  28.9 10.6 %collective-permute-start.6 = (bf16[2,2,80,512]{3,2,1,0:T(8,128)(2,1)S(1)}, bf16[2,2,80,512]{3,2,1,0:T(8,128)(2,1)S(1)}, u32[]{:S(2)}, u32[]{:S(2)}) collective-permute-start(bf16[2,2,80,512]{3,2,1,0:T(8,128)(2,1)S(1)} %shard_map.292.refs_0_), channel_id=1, source_target_pairs={{0,16},{1,17},{2,18},{3,19},{4,20},{5,21},{6,22},{7,23},{8,24},{9,... | collective-permute-start | bytes 983048 | tf_op jit(solution)/shard_map/ppermute | solution.py:45
  31.2 21.6 %collective-permute-start.8 = (bf16[2,2,2,80,512]{4,3,2,1,0:T(8,128)(2,1)S(1)}, bf16[2,2,2,80,512]{4,3,2,1,0:T(8,128)(2,1)S(1)}, u32[]{:S(2)}, u32[]{:S(2)}) collective-permute-start(bf16[2,2,2,80,512]{4,3,2,1,0:T(8,128)(2,1)S(1)} %shard_map.293.refs_0_), channel_id=1, source_target_pairs={{0,16},{1,17},{2,18},{3,19},{4,20},{5,21},{6,22},{7,23},{8,24},{9,... | collective-permute-start | bytes 1966088 | tf_op jit(solution)/shard_map/ppermute | solution.py:45
  40.1 15.9 %collective-permute-start.9 = (bf16[2,2,2,80,512]{4,3,2,1,0:T(8,128)(2,1)S(1)}, bf16[2,2,2,80,512]{4,3,2,1,0:T(8,128)(2,1)S(1)}, u32[]{:S(2)}, u32[]{:S(2)}) collective-permute-start(bf16[2,2,2,80,512]{4,3,2,1,0:T(8,128)(2,1)S(1)} %get-tuple-element.166.refs_0_), channel_id=1, source_target_pairs={{0,8},{1,9},{2,10},{3,11},{4,12},{5,13},{6,14},{7,15},{8,0},{9,1},... | collective-permute-start | bytes 1966088 | tf_op jit(solution)/shard_map/ppermute | solution.py:45
  41.7 11.8 %collective-permute-start.10 = (bf16[2,144,512]{2,1,0:T(8,128)(2,1)S(1)}, bf16[2,144,512]{2,1,0:T(8,128)(2,1)S(1)}, u32[]{:S(2)}, u32[]{:S(2)}) collective-permute-start(bf16[2,144,512]{2,1,0:T(8,128)(2,1)S(1)} %get-tuple-element.168.refs_2_), channel_id=1, source_target_pairs={{0,2},{1,3},{2,0},{3,1},{4,6},{5,7},{6,4},{7,5},{8,10},{9,11},{10,... | collective-permute-start | bytes 884744 | tf_op jit(solution)/shard_map/ppermute | solution.py:45
  56.7 10.1 %collective-permute-start.15 = (bf16[2,2,80,512]{3,2,1,0:T(8,128)(2,1)S(1)}, bf16[2,2,80,512]{3,2,1,0:T(8,128)(2,1)S(1)}, u32[]{:S(2)}, u32[]{:S(2)}) collective-permute-start(bf16[2,2,80,512]{3,2,1,0:T(8,128)(2,1)S(1)} %get-tuple-element.179.refs_4_), channel_id=1, source_target_pairs={{0,8},{1,9},{2,10},{3,11},{4,12},{5,13},{6,14},{7,15},{8,0},{9,1},... | collective-permute-start | bytes 983048 | tf_op jit(solution)/shard_map/ppermute | solution.py:45
  73.1 16.4 %collective-permute-start.19 = (bf16[2,2,2,80,512]{4,3,2,1,0:T(8,128)(2,1)S(1)}, bf16[2,2,2,80,512]{4,3,2,1,0:T(8,128)(2,1)S(1)}, u32[]{:S(2)}, u32[]{:S(2)}) collective-permute-start(bf16[2,2,2,80,512]{4,3,2,1,0:T(8,128)(2,1)S(1)} %get-tuple-element.187.refs_4_), channel_id=1, source_target_pairs={{0,16},{1,17},{2,18},{3,19},{4,20},{5,21},{6,22},{7,23},{8,24},{9,... | collective-permute-start | bytes 1966088 | tf_op jit(solution)/shard_map/ppermute | solution.py:45
  74.6 13.8 %collective-permute-start.20 = (bf16[2,2,2,64,512]{4,3,2,1,0:T(8,128)(2,1)S(1)}, bf16[2,2,2,64,512]{4,3,2,1,0:T(8,128)(2,1)S(1)}, u32[]{:S(2)}, u32[]{:S(2)}) collective-permute-start(bf16[2,2,2,64,512]{4,3,2,1,0:T(8,128)(2,1)S(1)} %get-tuple-element.189.refs_6_), channel_id=1, source_target_pairs={{0,8},{1,9},{2,10},{3,11},{4,12},{5,13},{6,14},{7,15},{8,0},{9,1},... | collective-permute-start | bytes 1572872 | tf_op jit(solution)/shard_map/ppermute | solution.py:45
  75.2 13.0 %collective-permute-start.18 = (bf16[2,128,512]{2,1,0:T(8,128)(2,1)S(1)}, bf16[2,128,512]{2,1,0:T(8,128)(2,1)S(1)}, u32[]{:S(2)}, u32[]{:S(2)}) collective-permute-start(bf16[2,128,512]{2,1,0:T(8,128)(2,1)S(1)} %get-tuple-element.185.refs_2_), channel_id=1, source_target_pairs={{0,4},{1,5},{2,6},{3,7},{4,0},{5,1},{6,2},{7,3},{8,12},{9,13},{10,... | collective-permute-start | bytes 786440 | tf_op jit(solution)/shard_map/ppermute | solution.py:45
  75.2 13.2 %collective-permute-start.17 = (bf16[2,128,512]{2,1,0:T(8,128)(2,1)S(1)}, bf16[2,128,512]{2,1,0:T(8,128)(2,1)S(1)}, u32[]{:S(2)}, u32[]{:S(2)}) collective-permute-start(bf16[2,128,512]{2,1,0:T(8,128)(2,1)S(1)} %get-tuple-element.183.refs_0_), channel_id=1, source_target_pairs={{0,2},{1,3},{2,0},{3,1},{4,6},{5,7},{6,4},{7,5},{8,10},{9,11},{10,... | collective-permute-start | bytes 786440 | tf_op jit(solution)/shard_map/ppermute | solution.py:45
  90.3 10.5 %collective-permute-start.23 = (bf16[2,2,2,2,144,512]{5,4,3,2,1,0:T(8,128)(2,1)S(1)}, bf16[2,2,2,2,144,512]{5,4,3,2,1,0:T(8,128)(2,1)S(1)}, u32[]{:S(2)}, u32[]{:S(2)}) collective-permute-start(bf16[2,2,2,2,144,512]{5,4,3,2,1,0:T(8,128)(2,1)S(1)} %get-tuple-element.200.refs_0_), channel_id=1, source_target_pairs={{0,1},{1,0},{2,3},{3,2},{4,5},{5,4},{6,7},{7,6},{8,9},{9,8},{10,11... | collective-permute-start | bytes 7077896 | tf_op jit(solution)/shard_map/ppermute | solution.py:45
  111.6 9.4 %collective-permute-start.26 = (bf16[2,2,2,2,144,512]{5,4,3,2,1,0:T(8,128)(2,1)S(1)}, bf16[2,2,2,2,144,512]{5,4,3,2,1,0:T(8,128)(2,1)S(1)}, u32[]{:S(2)}, u32[]{:S(2)}) collective-permute-start(bf16[2,2,2,2,144,512]{5,4,3,2,1,0:T(8,128)(2,1)S(1)} %bitcast.74), channel_id=1, source_target_pairs={{0,1},{1,0},{2,3},{3,2},{4,5},{5,4},{6,7},{7,6},{8,9},{9,8},{10,11... | collective-permute-start | bytes 7077896 | tf_op jit(solution)/shard_map/ppermute | solution.py:45
  121.9 17.1 %collective-permute-start.30 = (bf16[2,2,2,80,512]{4,3,2,1,0:T(8,128)(2,1)S(1)}, bf16[2,2,2,80,512]{4,3,2,1,0:T(8,128)(2,1)S(1)}, u32[]{:S(2)}, u32[]{:S(2)}) collective-permute-start(bf16[2,2,2,80,512]{4,3,2,1,0:T(8,128)(2,1)S(1)} %get-tuple-element.227), channel_id=1, source_target_pairs={{0,16},{1,17},{2,18},{3,19},{4,20},{5,21},{6,22},{7,23},{8,24},{9,... | collective-permute-start | bytes 1966088 | tf_op jit(solution)/shard_map/ppermute | solution.py:45
  123.4 15.1 %collective-permute-start.31 = (bf16[2,2,2,64,512]{4,3,2,1,0:T(8,128)(2,1)S(1)}, bf16[2,2,2,64,512]{4,3,2,1,0:T(8,128)(2,1)S(1)}, u32[]{:S(2)}, u32[]{:S(2)}) collective-permute-start(bf16[2,2,2,64,512]{4,3,2,1,0:T(8,128)(2,1)S(1)} %get-tuple-element.230), channel_id=1, source_target_pairs={{0,8},{1,9},{2,10},{3,11},{4,12},{5,13},{6,14},{7,15},{8,0},{9,1},... | collective-permute-start | bytes 1572872 | tf_op jit(solution)/shard_map/ppermute | solution.py:45
  124.0 12.7 %collective-permute-start.27 = (bf16[2,128,512]{2,1,0:T(8,128)(2,1)S(1)}, bf16[2,128,512]{2,1,0:T(8,128)(2,1)S(1)}, u32[]{:S(2)}, u32[]{:S(2)}) collective-permute-start(bf16[2,128,512]{2,1,0:T(8,128)(2,1)S(1)} %get-tuple-element.220), channel_id=1, source_target_pairs={{0,2},{1,3},{2,0},{3,1},{4,6},{5,7},{6,4},{7,5},{8,10},{9,11},{10,... | collective-permute-start | bytes 786440 | tf_op jit(solution)/shard_map/ppermute | solution.py:45
  124.0 14.6 %collective-permute-start.29 = (bf16[2,128,512]{2,1,0:T(8,128)(2,1)S(1)}, bf16[2,128,512]{2,1,0:T(8,128)(2,1)S(1)}, u32[]{:S(2)}, u32[]{:S(2)}) collective-permute-start(bf16[2,128,512]{2,1,0:T(8,128)(2,1)S(1)} %get-tuple-element.224), channel_id=1, source_target_pairs={{0,4},{1,5},{2,6},{3,7},{4,0},{5,1},{6,2},{7,3},{8,12},{9,13},{10,... | collective-permute-start | bytes 786440 | tf_op jit(solution)/shard_map/ppermute | solution.py:45
  153.7 9.1 %collective-permute-start.36 = (bf16[2,2,2,2,112,512]{5,4,3,2,1,0:T(8,128)(2,1)S(1)}, bf16[2,2,2,2,112,512]{5,4,3,2,1,0:T(8,128)(2,1)S(1)}, u32[]{:S(2)}, u32[]{:S(2)}) collective-permute-start(bf16[2,2,2,2,112,512]{5,4,3,2,1,0:T(8,128)(2,1)S(1)} %bitcast.75), channel_id=1, source_target_pairs={{0,1},{1,0},{2,3},{3,2},{4,5},{5,4},{6,7},{7,6},{8,9},{9,8},{10,11... | collective-permute-start | bytes 5505032 | tf_op jit(solution)/shard_map/ppermute | solution.py:45
  163.5 16.7 %collective-permute-start.38 = (bf16[2,2,2,80,512]{4,3,2,1,0:T(8,128)(2,1)S(1)}, bf16[2,2,2,80,512]{4,3,2,1,0:T(8,128)(2,1)S(1)}, u32[]{:S(2)}, u32[]{:S(2)}) collective-permute-start(bf16[2,2,2,80,512]{4,3,2,1,0:T(8,128)(2,1)S(1)} %get-tuple-element.261), channel_id=1, source_target_pairs={{0,16},{1,17},{2,18},{3,19},{4,20},{5,21},{6,22},{7,23},{8,24},{9,... | collective-permute-start | bytes 1966088 | tf_op jit(solution)/shard_map/ppermute | solution.py:45
  165.8 9.3 %collective-permute-start.39 = (bf16[2,2,2,32,512]{4,3,2,1,0:T(8,128)(2,1)S(1)}, bf16[2,2,2,32,512]{4,3,2,1,0:T(8,128)(2,1)S(1)}, u32[]{:S(2)}, u32[]{:S(2)}) collective-permute-start(bf16[2,2,2,32,512]{4,3,2,1,0:T(8,128)(2,1)S(1)} %get-tuple-element.264), channel_id=1, source_target_pairs={{0,8},{1,9},{2,10},{3,11},{4,12},{5,13},{6,14},{7,15},{8,0},{9,1},... | collective-permute-start | bytes 786440 | tf_op jit(solution)/shard_map/ppermute | solution.py:45
  166.9 16.4 %collective-permute-start.41 = (bf16[2,2,2,48,512]{4,3,2,1,0:T(8,128)(2,1)S(1)}, bf16[2,2,2,48,512]{4,3,2,1,0:T(8,128)(2,1)S(1)}, u32[]{:S(2)}, u32[]{:S(2)}) collective-permute-start(bf16[2,2,2,48,512]{4,3,2,1,0:T(8,128)(2,1)S(1)} %get-tuple-element.269), channel_id=1, source_target_pairs={{0,8},{1,9},{2,10},{3,11},{4,12},{5,13},{6,14},{7,15},{8,0},{9,1},... | collective-permute-start | bytes 1179656 | tf_op jit(solution)/shard_map/ppermute | solution.py:45
  180.9 9.0 %collective-permute-start.49 = (bf16[144,512]{1,0:T(8,128)(2,1)S(1)}, bf16[144,512]{1,0:T(8,128)(2,1)S(1)}, u32[]{:S(2)}, u32[]{:S(2)}) collective-permute-start(bf16[144,512]{1,0:T(8,128)(2,1)S(1)} %get-tuple-element.289), channel_id=1, source_target_pairs={{0,4},{1,5},{2,6},{3,7},{4,0},{5,1},{6,2},{7,3},{8,12},{9,13},{10,... | collective-permute-start | bytes 442376 | tf_op jit(solution)/shard_map/ppermute | solution.py:45
  (31 other events, 206.9 us)

commit v2 on v1

--- a/solution.py
+++ b/solution.py
@@ -17,6 +17,7 @@
 PAIR = 2 * HEAD_DIM
 RIM = 8
 MASKED = -1e30
+LEAST_ITEM = 501
 F32 = jnp.float32
 BF16 = jnp.bfloat16
 TN = ((0,), (0,))
@@ -459,17 +460,27 @@
     return jnp.where(lower, values[:half], values[half:])
 
 
-def memory_pair(memory, m, pair, micro):
+def reach(blocks, each):
+    row = blocks * each
+    size = (row - 2 - LEAST_ITEM) // each + 1
+    size = min(size + size % 2, blocks)
+    skipped = (LEAST_ITEM + 3) // 3 // (each // 3)
+    return size if blocks - size <= skipped else blocks
+
+
+def memory_pair(memory, first, size, m, pair, micro):
     slots = memory.shape[1] // micro
-    rows = memory[:, slots * m : slots * (m + 1), PAIR * pair : PAIR * (pair + 1)]
-    return rows.reshape(memory.shape[0] * slots, PAIR)
+    rows, cols = slice(slots * m, slots * (m + 1)), slice(PAIR * pair, PAIR * (pair + 1))
+    return memory[pl.ds(first, size), rows, cols].reshape(size * slots, PAIR)
 
 
 def attend_kernel(info, query, keys, values, memory_keys, memory_values, attended, stats):
     micro = info.shape[0]
     count, width = query.shape
     each = count // micro
-    slots = memory_keys.shape[0] * memory_keys.shape[1] // micro
+    blocks, share = memory_keys.shape[0], memory_keys.shape[1] // micro
+    size = reach(blocks, each)
+    slots = size * share
     pairs = width // PAIR
     lower = iota((each, PAIR), 1) < HEAD_DIM
     lane = iota((2 * each, 128), 1)
@@ -478,7 +489,8 @@
         rows = slice(each * m, each * (m + 1))
         place = info[m, 4] + iota((each, 1), 0)
         start = segment_start(info, m, place)
-        end = 3 * iota((each, slots), 1)
+        begin = jnp.where(info[m, 4] < info[m, 1], 0, blocks - size)
+        end = 3 * (share * begin + iota((each, slots), 1))
         bias = jnp.where((end <= place) & (end >= start), 0.0, MASKED).astype(F32)
         bias = jnp.concatenate([bias, bias], axis=0)
         for pair in range(pairs):
@@ -487,8 +499,8 @@
             value = values[rows, cols].astype(F32)
             queries = stacked(query[rows, cols].astype(F32) * SCALE, lower)
             own = jnp.sum(queries * jnp.concatenate([key, key], axis=0), axis=1, keepdims=True)
-            memory_key = memory_pair(memory_keys, m, pair, micro)
-            memory_value = memory_pair(memory_values, m, pair, micro)
+            memory_key = memory_pair(memory_keys, begin, size, m, pair, micro)
+            memory_value = memory_pair(memory_values, begin, size, m, pair, micro)
             scores = dot(queries.astype(BF16), memory_key, NT) + bias
             top = jnp.maximum(jnp.max(scores, axis=1, keepdims=True), own)
             expos = jnp.exp(scores - top)
@@ -587,10 +599,10 @@
     vec_grad[...] = jnp.concatenate(rows, axis=0)
 
 
-def memory_turned(flag, memory, m, pair, micro):
+def memory_turned(flag, memory, first, size, m, pair, micro):
     slots = memory.shape[2] // micro
     rows, cols = slice(slots * m, slots * (m + 1)), slice(PAIR * pair, PAIR * (pair + 1))
-    halves = [memory[:, pl.ds(at, 1), rows, cols] for at in (flag, 1 - flag)]
+    halves = [memory[pl.ds(first, size), pl.ds(at, 1), rows, cols] for at in (flag, 1 - flag)]
     return jnp.concatenate([h.reshape(-1, PAIR) for h in halves], axis=0)
 
 
@@ -617,7 +629,8 @@
     each = count // micro
     chips = memory_keys.shape[0]
     share = memory_keys.shape[2] // micro
-    slots = 2 * chips * share
+    size = reach(2 * chips, each) // 2
+    slots = 2 * size * share
     flag = info[0, 6]
     pairs = width // PAIR
     lower = iota((each, PAIR), 1) < HEAD_DIM
@@ -641,14 +654,21 @@
         place = info[m, 4] + jnp.where(lanes >= each, lanes - each, lanes)
         start = segment_start(info, m, place)
         row = iota((slots, 1), 0)
-        late = row >= chips * share
-        row = jnp.where(late, row - chips * share, row)
-        block = jnp.zeros((slots, 1), jnp.int32)
-        for chip in range(1, chips):
+        late = row >= size * share
+        row = jnp.where(late, row - size * share, row)
+        front = info[m, 4] < info[m, 1]
+        begin = jnp.where(front, 0, chips - size)
+        block = jnp.zeros((slots, 1), jnp.int32) + 2 * begin
+        for chip in range(1, size):
             block = block + jnp.where(row >= share * chip, 1, 0)
         core = jnp.where(late, 1 - flag, flag)
         end = 3 * (row + share * (block + core))
         bias = jnp.where((end <= place) & (end >= start), 0.0, MASKED).astype(F32)
+        if size < chips:
+            empty = pl.ds(jnp.where(front, size, 0), chips - size)
+            zeros = jnp.zeros((chips - size, share, width), BF16)
+            for half in (key_keep, key_send, value_keep, value_send):
+                half[empty, share * m : share * (m + 1), :] = zeros
         for pair in range(pairs):
             cols = slice(PAIR * pair, PAIR * (pair + 1))
             at = m * pairs + pair
@@ -665,8 +685,8 @@
             )
             grad_own = (own * (grad_own - parts[m, pair])).astype(BF16).astype(F32)
             queries, grads = queries.astype(BF16), grads.astype(BF16)
-            memory_key = memory_turned(flag, memory_keys, m, pair, micro)
-            memory_value = memory_turned(flag, memory_values, m, pair, micro)
+            memory_key = memory_turned(flag, memory_keys, begin, size, m, pair, micro)
+            memory_value = memory_turned(flag, memory_values, begin, size, m, pair, micro)
             scores = dot(memory_key, queries, NT) + bias
             probs = jnp.exp(scores - found_t[at : at + 1, :])
             grad_probs = dot(memory_value, grads, NT)
@@ -676,9 +696,10 @@
                 (dot(probs.astype(BF16), grads), value_keep, value_send),
             )
             for grad, keep, send in sides:
-                halves = grad.astype(BF16).reshape(2, chips, share, PAIR)
-                keep[:, share * m : share * (m + 1), cols] = halves[0]
-                send[:, share * m : share * (m + 1), cols] = halves[1]
+                halves = grad.astype(BF16).reshape(2, size, share, PAIR)
+                into = (pl.ds(begin, size), slice(share * m, share * (m + 1)), cols)
+                keep[into] = halves[0]
+                send[into] = halves[1]
             turned = dot(memory_key.T, grad_scores).T
             own_grad = merged(jnp.broadcast_to(grad_own, (2 * each, PAIR)), lower)
             own_weight = merged(jnp.broadcast_to(own, (2 * each, PAIR)), lower)
@@ -841,14 +862,6 @@
     along = powers(2, seq)[::-1]
     back = along[::-1]
     order = Order()
-    lengths = lengths[:, 0]
-    first_pad = 3 * ((lengths[:, 0] + 2) // 3)
-    second_pad = 3 * ((lengths[:, 1] + 2) // 3)
-    start = 1 + first_pad
-    seats = [lax.axis_index("seq") * each, upper_half(1) if whole else 0, upper_half(1)]
-    seats = [jnp.full_like(start, seat) for seat in seats]
-    info = [1 + lengths[:, 0], start, start + lengths[:, 1], start + second_pad]
-    info = jnp.stack(info + seats, axis=1).astype(jnp.int32)
     if whole:
         moves = [(kind, None, kind, 0, UNIT) for kind in range(2)]
         moves += [(2 + k, tap, k, UNIT * (1 + tap), UNIT) for k in range(2) for tap in range(3)]
@@ -876,6 +889,15 @@
     halo = halo.reshape(micro * RIM, width)
     for at in range(1, len(along)):
         one.place()
+        if at == 1:
+            lengths = order.turn(lengths[:, 0])
+            first_pad = 3 * ((lengths[:, 0] + 2) // 3)
+            second_pad = 3 * ((lengths[:, 1] + 2) // 3)
+            start = 1 + first_pad
+            seats = [lax.axis_index("seq") * each, upper_half(1) if whole else 0, upper_half(1)]
+            seats = [jnp.full_like(start, seat) for seat in seats]
+            info = [1 + lengths[:, 0], start, start + lengths[:, 1], start + second_pad]
+            info = jnp.stack(info + seats, axis=1).astype(jnp.int32)
         one.go(along[at])
         two.place()
         two.go(back[at])
@@ -1115,12 +1137,19 @@
         if at < len(cross):
             inputs.add((line[at],))
             inputs.go(line[at])
+    rest_total = feeds.total()
     for at in range(len(along)):
+        if at == len(along) - 1:
+            ups = [rest_total[share * c : share * (c + 1)] for c in range(1, 1 + wide)]
+            rest_outs = (rest_total[:share], jnp.concatenate(ups, axis=1))
+            rest_outs = rest_outs + (rest_total[share * (1 + wide) :],)
+            rest_outs = lax.optimization_barrier(rest_outs)
+            order.done(rest_outs)
         convs.add((back[at],), 7 * share)
         convs.go(back[at])
         inputs.add((along[at],))
         inputs.go(along[at])
-    feeds, convs, late_inputs = feeds.total(), convs.total(), inputs.total()
+    convs, late_inputs = convs.total(), inputs.total()
     conv_keys = convs[: 3 * share].reshape(3, share, width)
     conv_values = convs[4 * share :].reshape(3, share, width)
 
@@ -1142,12 +1171,12 @@
         own(late_inputs, 1),
         conv_keys,
         conv_values,
-        own(feeds, 0),
+        rest_outs[0],
         own_vector(2),
         own_vector(3),
-        jnp.concatenate([own(feeds, 1 + c) for c in range(wide)], axis=1),
+        rest_outs[1],
         own_vector(VECTORS, ff // count),
-        feeds[share * (1 + wide) :],
+        rest_outs[2],
         own_vector(4),
     )
 

time: 210 us -> 209 us (level)
  transfers between devices with their start and end apart: 50 -> 50, of which waited for: 35 -> 33; matrix products, arithmetic and copies ran while one was open for 3% -> 3% of each run, Pallas kernels for 14% -> 14%
where the time goes in v2:
time: 209 us
  waiting for transfers between devices  93.1 us (45%)
  starting transfers between devices  55.5 us (27%)
  Pallas kernels  47.8 us (23%)
  local copies, waits for them, and re-layouts  7.21 us (3%)
  other arithmetic  3.89 us (2%)
    ppermute x48, waiting for transfers between devices, swap(): lax.ppermute(array, AXES, [(i, i ^ mask) for i in range(device_count())])  90.7 us
    ppermute x48, starting transfers between devices, swap(): lax.ppermute(array, AXES, [(i, i ^ mask) for i in range(device_count())])  52.6 us
    pallas_call x35, Pallas kernels, kernel(): pl.pallas_call(body, in_specs=[pl.BlockSpec(memory_space=spec.get(a.dtype...  45.9 us
  transfers between devices with their start and end apart: 50, of which 33 were waited for; matrix products, arithmetic and copies ran while one was open for 3% of the time, Pallas kernels for 14%

profile of v2, /device:TPU:0, one launch (start us, length us, event | category | flops | bytes accessed | tf_op | source)
XLA Modules:
  0.0 208.5 jit_solution(6736933217048210744)
XLA Ops:
  4.0 4.1 %collective-permute-start = (bf16[80,512]{1,0:T(8,128)(2,1)}, bf16[80,512]{1,0:T(8,128)(2,1)S(1)}, u32[]{:S(2)}, u32[]{:S(2)}) collective-permute-start(bf16[80,512]{1,0:T(8,128)(2,1)} %get-tuple-element.157.refs_0_), channel_id=1, source_target_pairs={{0,4},{1,5},{2,6},{3,7},{4,0},{5,1},{6,2},{7,3},{8,12},{9,13},{10,... | collective-permute-start | bytes 245768 | tf_op jit(solution)/shard_map/ppermute | solution.py:46
  17.3 3.3 %collective-permute-start.4 = (bf16[2,80,512]{2,1,0:T(8,128)(2,1)S(1)}, bf16[2,80,512]{2,1,0:T(8,128)(2,1)S(1)}, u32[]{:S(2)}, u32[]{:S(2)}) collective-permute-start(bf16[2,80,512]{2,1,0:T(8,128)(2,1)S(1)} %shard_map.291.refs_0_), channel_id=1, source_target_pairs={{0,4},{1,5},{2,6},{3,7},{4,0},{5,1},{6,2},{7,3},{8,12},{9,13},{10,... | collective-permute-start | bytes 491528 | tf_op jit(solution)/shard_map/ppermute | solution.py:46
  23.7 4.7 %collective-permute-done.4.refs_1_ = bf16[2,80,512]{2,1,0:T(8,128)(2,1)S(1)} collective-permute-done((bf16[2,80,512]{2,1,0:T(8,128)(2,1)S(1)}, bf16[2,80,512]{2,1,0:T(8,128)(2,1)S(1)}, u32[]{:S(2)}, u32[]{:S(2)}) %collective-permute-start.4) | collective-permute-done | bytes 163872 | tf_op jit(solution)/shard_map/ppermute | solution.py:46
  33.1 5.3 %collective-permute-done.7.refs_3_ = bf16[144,512]{1,0:T(8,128)(2,1)S(1)} collective-permute-done((bf16[144,512]{1,0:T(8,128)(2,1)}, bf16[144,512]{1,0:T(8,128)(2,1)S(1)}, u32[]{:S(2)}, u32[]{:S(2)}) %collective-permute-start.7) | collective-permute-done | bytes 147488 | tf_op jit(solution)/shard_map/ppermute | solution.py:46
  41.8 10.6 %collective-permute-done.8.refs_1_ = bf16[2,2,2,80,512]{4,3,2,1,0:T(8,128)(2,1)S(1)} collective-permute-done((bf16[2,2,2,80,512]{4,3,2,1,0:T(8,128)(2,1)S(1)}, bf16[2,2,2,80,512]{4,3,2,1,0:T(8,128)(2,1)S(1)}, u32[]{:S(2)}, u32[]{:S(2)}) %collective-permute-start.8) | collective-permute-done | bytes 655392 | tf_op jit(solution)/shard_map/ppermute | solution.py:46
  63.2 3.5 %collective-permute-start.14 = (bf16[128,512]{1,0:T(8,128)(2,1)S(1)}, bf16[128,512]{1,0:T(8,128)(2,1)S(1)}, u32[]{:S(2)}, u32[]{:S(2)}) collective-permute-start(bf16[128,512]{1,0:T(8,128)(2,1)S(1)} %get-tuple-element.182.refs_2_), channel_id=1, source_target_pairs={{0,2},{1,3},{2,0},{3,1},{4,6},{5,7},{6,4},{7,5},{8,10},{9,11},{10,... | collective-permute-start | bytes 393224 | tf_op jit(solution)/shard_map/ppermute | solution.py:46
  66.6 3.3 %collective-permute-done.13.refs_1_ = bf16[128,512]{1,0:T(8,128)(2,1)S(1)} collective-permute-done((bf16[128,512]{1,0:T(8,128)(2,1)S(1)}, bf16[128,512]{1,0:T(8,128)(2,1)S(1)}, u32[]{:S(2)}, u32[]{:S(2)}) %collective-permute-start.13) | collective-permute-done | bytes 131104 | tf_op jit(solution)/shard_map/ppermute | solution.py:46
  70.0 2.4 %collective-permute-done.14.refs_3_ = bf16[128,512]{1,0:T(8,128)(2,1)S(1)} collective-permute-done((bf16[128,512]{1,0:T(8,128)(2,1)S(1)}, bf16[128,512]{1,0:T(8,128)(2,1)S(1)}, u32[]{:S(2)}, u32[]{:S(2)}) %collective-permute-start.14) | collective-permute-done | bytes 131104 | tf_op jit(solution)/shard_map/ppermute | solution.py:46
  76.9 11.1 %collective-permute-done.18.refs_3_ = bf16[2,128,512]{2,1,0:T(8,128)(2,1)S(1)} collective-permute-done((bf16[2,128,512]{2,1,0:T(8,128)(2,1)S(1)}, bf16[2,128,512]{2,1,0:T(8,128)(2,1)S(1)}, u32[]{:S(2)}, u32[]{:S(2)}) %collective-permute-start.18) | collective-permute-done | bytes 262176 | tf_op jit(solution)/shard_map/ppermute | solution.py:46
  90.9 4.7 %collective-permute-done.21.refs_1_ = bf16[2,2,128,512]{3,2,1,0:T(8,128)(2,1)S(1)} collective-permute-done((bf16[2,2,128,512]{3,2,1,0:T(8,128)(2,1)S(1)}, bf16[2,2,128,512]{3,2,1,0:T(8,128)(2,1)S(1)}, u32[]{:S(2)}, u32[]{:S(2)}) %collective-permute-start.21) | collective-permute-done | bytes 524320 | tf_op jit(solution)/shard_map/ppermute | solution.py:46
  97.0 3.8 %shard_map.305 = (f32[384,512]{1,0:T(8,128)S(1)}, f32[384,128]{1,0:T(8,128)S(1)}) custom-call(s32[2,7]{1,0:T(2,128)S(1)} %stack.47.info, bf16[384,512]{1,0:T(8,128)(2,1)S(1)} %get-tuple-element.210.query, bf16[384,512]{1,0:T(8,128)(2,1)S(1)} %get-tuple-element.202.keys, bf16[384,512]{1,0:T(8,128)(2,1)S(1)} %get-tuple-element.203.values, ...), custom_call_target="tpu_custom_call" | custom-call | flops 805306368 | bytes 3276856 | tf_op jit(solution)/shard_map/pallas_call | solution.py:327
  101.8 9.7 %shard_map.307 = (bf16[384,512]{1,0:T(8,128)(2,1)}, f32[384,512]{1,0:T(8,128)S(1)}, bf16[384,512]{1,0:T(8,128)(2,1)S(1)}, bf16[16,144,512]{2,1,0:T(8,128)(2,1)S(...) custom-call(s32[2,7]{1,0:T(2,128)S(1)} %stack.47.info, bf16[384,512]{1,0:T(8,128)(2,1)S(1)} %bitcast.68, ...), custom_call_target="tpu_custom_call" | custom-call | flops 5435817984 | bytes 6324280 | tf_op jit(solution)/shard_map/pallas_call | solution.py:327
  111.7 5.6 %shard_map.308 = (bf16[384,512]{1,0:T(8,128)(2,1)S(1)}, bf16[4,128,512]{2,1,0:T(8,128)(2,1)S(1)}, bf16[4,128,512]{2,1,0:T(8,128)(2,1)S(1)}, bf16[4,128,512]{2,1,...) custom-call(s32[2,7]{1,0:T(2,128)S(1)} %stack.47.info, ...), custom_call_target="tpu_custom_call" | custom-call | flops 2013265920 | bytes 4653112 | tf_op jit(solution)/shard_map/pallas_call | solution.py:327
  122.7 2.3 %collective-permute-start.29 = (bf16[2,128,512]{2,1,0:T(8,128)(2,1)S(1)}, bf16[2,128,512]{2,1,0:T(8,128)(2,1)S(1)}, u32[]{:S(2)}, u32[]{:S(2)}) collective-permute-start(bf16[2,128,512]{2,1,0:T(8,128)(2,1)S(1)} %get-tuple-element.229), channel_id=1, source_target_pairs={{0,4},{1,5},{2,6},{3,7},{4,0},{5,1},{6,2},{7,3},{8,12},{9,13},{10,... | collective-permute-start | bytes 786440 | tf_op jit(solution)/shard_map/ppermute | solution.py:46
  125.0 10.5 %collective-permute-done.27.refs_1_ = bf16[2,128,512]{2,1,0:T(8,128)(2,1)S(1)} collective-permute-done((bf16[2,128,512]{2,1,0:T(8,128)(2,1)S(1)}, bf16[2,128,512]{2,1,0:T(8,128)(2,1)S(1)}, u32[]{:S(2)}, u32[]{:S(2)}) %collective-permute-start.27) | collective-permute-done | bytes 262176 | tf_op jit(solution)/shard_map/ppermute | solution.py:46
  143.9 2.3 %collective-permute-done.34 = bf16[128,512]{1,0:T(8,128)(2,1)S(1)} collective-permute-done((bf16[128,512]{1,0:T(8,128)(2,1)S(1)}, bf16[128,512]{1,0:T(8,128)(2,1)S(1)}, u32[]{:S(2)}, u32[]{:S(2)}) %collective-permute-start.34) | collective-permute-done | bytes 131104 | tf_op jit(solution)/shard_map/ppermute | solution.py:46
  146.5 2.3 %collective-permute-done.32.refs_1_ = bf16[2,2,80,512]{3,2,1,0:T(8,128)(2,1)S(1)} collective-permute-done((bf16[2,2,80,512]{3,2,1,0:T(8,128)(2,1)S(1)}, bf16[2,2,80,512]{3,2,1,0:T(8,128)(2,1)S(1)}, u32[]{:S(2)}, u32[]{:S(2)}) %collective-permute-start.32) | collective-permute-done | bytes 327712 | tf_op jit(solution)/shard_map/ppermute | solution.py:46
  149.5 2.7 %shard_map.314 = (f32[384,512]{1,0:T(8,128)S(1)}, f32[384,512]{1,0:T(8,128)S(1)}, f32[16,1024]{1,0:T(8,128)S(1)}, bf16[16,112,512]{2,1,0:T(8,128)(2,1)S(1)}, bf16[16,112,512]{2,1,0:T(8,128)(2,1)S(1)}) custom-call(s32[2,7]{1,0:T(2,128)S(1)} %stack.47.info, bf16[128,512]{1,0:T(8,128)(2,1)S(1)} %add_convert_fusion.1.key_memory, ...), custom_call_target="tpu_custom_call" | custom-call | flops 1006632960 | bytes 7094328 | tf_op jit(solution)/shard_map/pallas_call | solution.py:327
  153.8 2.3 %collective-permute-done.35.rims = f32[16,1024]{1,0:T(8,128)S(1)} collective-permute-done((f32[16,1024]{1,0:T(8,128)S(1)}, f32[16,1024]{1,0:T(8,128)S(1)}, u32[]{:S(2)}, u32[]{:S(2)}) %collective-permute-start.35) | collective-permute-done | bytes 65568 | tf_op jit(solution)/shard_map/ppermute | solution.py:1082
  156.1 2.9 %shard_map.315 = (bf16[384,512]{1,0:T(8,128)(2,1)}, bf16[16,48,512]{2,1,0:T(8,128)(2,1)S(1)}, bf16[16,48,512]{2,1,0:T(8,128)(2,1)S(1)}) custom-call(s32[2,7]{1,0:T(2,128)S(1)} %stack.47.info, bf16[384,512]{1,0:T(8,128)(2,1)S(1)} %bitcast.69, bf16[400,512]{1,0:T(8,128)(2,1)S(1)} %get-tuple-element.178.normed, ...), custom_call_target="tpu_custom_call" | custom-call | flops 1207959552 | bytes 10502200 | tf_op jit(solution)/shard_map/pallas_call | solution.py:327
  167.3 4.2 %collective-permute-done.40.refs_5_ = bf16[2,144,512]{2,1,0:T(8,128)(2,1)S(1)} collective-permute-done((bf16[2,144,512]{2,1,0:T(8,128)(2,1)S(1)}, bf16[2,144,512]{2,1,0:T(8,128)(2,1)S(1)}, u32[]{:S(2)}, u32[]{:S(2)}) %collective-permute-start.40) | collective-permute-done | bytes 294944 | tf_op jit(solution)/shard_map/ppermute | solution.py:46
  173.8 4.9 %collective-permute-done.38.refs_1_ = bf16[2,2,2,80,512]{4,3,2,1,0:T(8,128)(2,1)S(1)} collective-permute-done((bf16[2,2,2,80,512]{4,3,2,1,0:T(8,128)(2,1)S(1)}, bf16[2,2,2,80,512]{4,3,2,1,0:T(8,128)(2,1)S(1)}, u32[]{:S(2)}, u32[]{:S(2)}) %collective-permute-start.38) | collective-permute-done | bytes 655392 | tf_op jit(solution)/shard_map/ppermute | solution.py:46
  184.6 3.8 %collective-permute-done.45 = bf16[144,512]{1,0:T(8,128)(2,1)S(1)} collective-permute-done((bf16[144,512]{1,0:T(8,128)(2,1)S(1)}, bf16[144,512]{1,0:T(8,128)(2,1)S(1)}, u32[]{:S(2)}, u32[]{:S(2)}) %collective-permute-start.45) | collective-permute-done | bytes 147488 | tf_op jit(solution)/shard_map/ppermute | solution.py:46
  195.8 2.7 %collective-permute-done.46.refs_1_ = bf16[2,112,512]{2,1,0:T(8,128)(2,1)S(1)} collective-permute-done((bf16[2,112,512]{2,1,0:T(8,128)(2,1)S(1)}, bf16[2,112,512]{2,1,0:T(8,128)(2,1)S(1)}, u32[]{:S(2)}, u32[]{:S(2)}) %collective-permute-start.46) | collective-permute-done | bytes 229408 | tf_op jit(solution)/shard_map/ppermute | solution.py:46
  (143 shorter events, 94.3 us)
Async XLA Ops:
  8.8 12.8 %collective-permute-start.1 = (bf16[2,8,512]{2,1,0:T(8,128)(2,1)S(1)}, bf16[2,8,512]{2,1,0:T(8,128)(2,1)S(1)}, u32[]{:S(2)}, u32[]{:S(2)}) collective-permute-start(bf16[2,8,512]{2,1,0:T(8,128)(2,1)S(1)} %slice_bitcast_fusion), channel_id=1, source_target_pairs={{0,1},{1,2},{2,3},{3,4},{4,5},{5,6},{6,7},{8,9},{9,10},{10,11},{11... | collective-permute-start | bytes 49160 | tf_op jit(solution)/shard_map/ppermute | solution.py:888
  17.3 11.1 %collective-permute-start.4 = (bf16[2,80,512]{2,1,0:T(8,128)(2,1)S(1)}, bf16[2,80,512]{2,1,0:T(8,128)(2,1)S(1)}, u32[]{:S(2)}, u32[]{:S(2)}) collective-permute-start(bf16[2,80,512]{2,1,0:T(8,128)(2,1)S(1)} %shard_map.291.refs_0_), channel_id=1, source_target_pairs={{0,4},{1,5},{2,6},{3,7},{4,0},{5,1},{6,2},{7,3},{8,12},{9,13},{10,... | collective-permute-start | bytes 491528 | tf_op jit(solution)/shard_map/ppermute | solution.py:46
  29.0 10.7 %collective-permute-start.6 = (bf16[2,2,80,512]{3,2,1,0:T(8,128)(2,1)S(1)}, bf16[2,2,80,512]{3,2,1,0:T(8,128)(2,1)S(1)}, u32[]{:S(2)}, u32[]{:S(2)}) collective-permute-start(bf16[2,2,80,512]{3,2,1,0:T(8,128)(2,1)S(1)} %shard_map.292.refs_0_), channel_id=1, source_target_pairs={{0,16},{1,17},{2,18},{3,19},{4,20},{5,21},{6,22},{7,23},{8,24},{9,... | collective-permute-start | bytes 983048 | tf_op jit(solution)/shard_map/ppermute | solution.py:46
  31.5 20.9 %collective-permute-start.8 = (bf16[2,2,2,80,512]{4,3,2,1,0:T(8,128)(2,1)S(1)}, bf16[2,2,2,80,512]{4,3,2,1,0:T(8,128)(2,1)S(1)}, u32[]{:S(2)}, u32[]{:S(2)}) collective-permute-start(bf16[2,2,2,80,512]{4,3,2,1,0:T(8,128)(2,1)S(1)} %shard_map.293.refs_0_), channel_id=1, source_target_pairs={{0,16},{1,17},{2,18},{3,19},{4,20},{5,21},{6,22},{7,23},{8,24},{9,... | collective-permute-start | bytes 1966088 | tf_op jit(solution)/shard_map/ppermute | solution.py:46
  40.3 14.9 %collective-permute-start.9 = (bf16[2,2,2,80,512]{4,3,2,1,0:T(8,128)(2,1)S(1)}, bf16[2,2,2,80,512]{4,3,2,1,0:T(8,128)(2,1)S(1)}, u32[]{:S(2)}, u32[]{:S(2)}) collective-permute-start(bf16[2,2,2,80,512]{4,3,2,1,0:T(8,128)(2,1)S(1)} %get-tuple-element.171.refs_0_), channel_id=1, source_target_pairs={{0,8},{1,9},{2,10},{3,11},{4,12},{5,13},{6,14},{7,15},{8,0},{9,1},... | collective-permute-start | bytes 1966088 | tf_op jit(solution)/shard_map/ppermute | solution.py:46
  41.8 11.3 %collective-permute-start.10 = (bf16[2,144,512]{2,1,0:T(8,128)(2,1)S(1)}, bf16[2,144,512]{2,1,0:T(8,128)(2,1)S(1)}, u32[]{:S(2)}, u32[]{:S(2)}) collective-permute-start(bf16[2,144,512]{2,1,0:T(8,128)(2,1)S(1)} %get-tuple-element.173.refs_2_), channel_id=1, source_target_pairs={{0,2},{1,3},{2,0},{3,1},{4,6},{5,7},{6,4},{7,5},{8,10},{9,11},{10,... | collective-permute-start | bytes 884744 | tf_op jit(solution)/shard_map/ppermute | solution.py:46
  55.9 10.7 %collective-permute-start.15 = (bf16[2,2,80,512]{3,2,1,0:T(8,128)(2,1)S(1)}, bf16[2,2,80,512]{3,2,1,0:T(8,128)(2,1)S(1)}, u32[]{:S(2)}, u32[]{:S(2)}) collective-permute-start(bf16[2,2,80,512]{3,2,1,0:T(8,128)(2,1)S(1)} %get-tuple-element.184.refs_4_), channel_id=1, source_target_pairs={{0,8},{1,9},{2,10},{3,11},{4,12},{5,13},{6,14},{7,15},{8,0},{9,1},... | collective-permute-start | bytes 983048 | tf_op jit(solution)/shard_map/ppermute | solution.py:46
  57.5 9.1 %collective-permute-start.16 = (bf16[2,2,64,512]{3,2,1,0:T(8,128)(2,1)S(1)}, bf16[2,2,64,512]{3,2,1,0:T(8,128)(2,1)S(1)}, u32[]{:S(2)}, u32[]{:S(2)}) collective-permute-start(bf16[2,2,64,512]{3,2,1,0:T(8,128)(2,1)S(1)} %get-tuple-element.186.refs_6_), channel_id=1, source_target_pairs={{0,16},{1,17},{2,18},{3,19},{4,20},{5,21},{6,22},{7,23},{8,24},{9,... | collective-permute-start | bytes 786440 | tf_op jit(solution)/shard_map/ppermute | solution.py:46
  60.8 9.2 %collective-permute-start.13 = (bf16[128,512]{1,0:T(8,128)(2,1)S(1)}, bf16[128,512]{1,0:T(8,128)(2,1)S(1)}, u32[]{:S(2)}, u32[]{:S(2)}) collective-permute-start(bf16[128,512]{1,0:T(8,128)(2,1)S(1)} %get-tuple-element.181.refs_0_), channel_id=1, source_target_pairs={{0,4},{1,5},{2,6},{3,7},{4,0},{5,1},{6,2},{7,3},{8,12},{9,13},{10,... | collective-permute-start | bytes 393224 | tf_op jit(solution)/shard_map/ppermute | solution.py:46
  63.2 9.2 %collective-permute-start.14 = (bf16[128,512]{1,0:T(8,128)(2,1)S(1)}, bf16[128,512]{1,0:T(8,128)(2,1)S(1)}, u32[]{:S(2)}, u32[]{:S(2)}) collective-permute-start(bf16[128,512]{1,0:T(8,128)(2,1)S(1)} %get-tuple-element.182.refs_2_), channel_id=1, source_target_pairs={{0,2},{1,3},{2,0},{3,1},{4,6},{5,7},{6,4},{7,5},{8,10},{9,11},{10,... | collective-permute-start | bytes 393224 | tf_op jit(solution)/shard_map/ppermute | solution.py:46
  73.0 16.4 %collective-permute-start.19 = (bf16[2,2,2,80,512]{4,3,2,1,0:T(8,128)(2,1)S(1)}, bf16[2,2,2,80,512]{4,3,2,1,0:T(8,128)(2,1)S(1)}, u32[]{:S(2)}, u32[]{:S(2)}) collective-permute-start(bf16[2,2,2,80,512]{4,3,2,1,0:T(8,128)(2,1)S(1)} %get-tuple-element.192.refs_4_), channel_id=1, source_target_pairs={{0,16},{1,17},{2,18},{3,19},{4,20},{5,21},{6,22},{7,23},{8,24},{9,... | collective-permute-start | bytes 1966088 | tf_op jit(solution)/shard_map/ppermute | solution.py:46
  74.3 13.8 %collective-permute-start.20 = (bf16[2,2,2,64,512]{4,3,2,1,0:T(8,128)(2,1)S(1)}, bf16[2,2,2,64,512]{4,3,2,1,0:T(8,128)(2,1)S(1)}, u32[]{:S(2)}, u32[]{:S(2)}) collective-permute-start(bf16[2,2,2,64,512]{4,3,2,1,0:T(8,128)(2,1)S(1)} %get-tuple-element.194.refs_6_), channel_id=1, source_target_pairs={{0,8},{1,9},{2,10},{3,11},{4,12},{5,13},{6,14},{7,15},{8,0},{9,1},... | collective-permute-start | bytes 1572872 | tf_op jit(solution)/shard_map/ppermute | solution.py:46
  74.9 13.1 %collective-permute-start.18 = (bf16[2,128,512]{2,1,0:T(8,128)(2,1)S(1)}, bf16[2,128,512]{2,1,0:T(8,128)(2,1)S(1)}, u32[]{:S(2)}, u32[]{:S(2)}) collective-permute-start(bf16[2,128,512]{2,1,0:T(8,128)(2,1)S(1)} %get-tuple-element.190.refs_2_), channel_id=1, source_target_pairs={{0,4},{1,5},{2,6},{3,7},{4,0},{5,1},{6,2},{7,3},{8,12},{9,13},{10,... | collective-permute-start | bytes 786440 | tf_op jit(solution)/shard_map/ppermute | solution.py:46
  74.9 13.3 %collective-permute-start.17 = (bf16[2,128,512]{2,1,0:T(8,128)(2,1)S(1)}, bf16[2,128,512]{2,1,0:T(8,128)(2,1)S(1)}, u32[]{:S(2)}, u32[]{:S(2)}) collective-permute-start(bf16[2,128,512]{2,1,0:T(8,128)(2,1)S(1)} %get-tuple-element.188.refs_0_), channel_id=1, source_target_pairs={{0,2},{1,3},{2,0},{3,1},{4,6},{5,7},{6,4},{7,5},{8,10},{9,11},{10,... | collective-permute-start | bytes 786440 | tf_op jit(solution)/shard_map/ppermute | solution.py:46
  90.2 10.5 %collective-permute-start.23 = (bf16[2,2,2,2,144,512]{5,4,3,2,1,0:T(8,128)(2,1)S(1)}, bf16[2,2,2,2,144,512]{5,4,3,2,1,0:T(8,128)(2,1)S(1)}, u32[]{:S(2)}, u32[]{:S(2)}) collective-permute-start(bf16[2,2,2,2,144,512]{5,4,3,2,1,0:T(8,128)(2,1)S(1)} %get-tuple-element.205.refs_0_), channel_id=1, source_target_pairs={{0,1},{1,0},{2,3},{3,2},{4,5},{5,4},{6,7},{7,6},{8,9},{9,8},{10,11... | collective-permute-start | bytes 7077896 | tf_op jit(solution)/shard_map/ppermute | solution.py:46
  120.9 17.1 %collective-permute-start.30 = (bf16[2,2,2,80,512]{4,3,2,1,0:T(8,128)(2,1)S(1)}, bf16[2,2,2,80,512]{4,3,2,1,0:T(8,128)(2,1)S(1)}, u32[]{:S(2)}, u32[]{:S(2)}) collective-permute-start(bf16[2,2,2,80,512]{4,3,2,1,0:T(8,128)(2,1)S(1)} %get-tuple-element.232), channel_id=1, source_target_pairs={{0,16},{1,17},{2,18},{3,19},{4,20},{5,21},{6,22},{7,23},{8,24},{9,... | collective-permute-start | bytes 1966088 | tf_op jit(solution)/shard_map/ppermute | solution.py:46
  122.2 15.1 %collective-permute-start.31 = (bf16[2,2,2,64,512]{4,3,2,1,0:T(8,128)(2,1)S(1)}, bf16[2,2,2,64,512]{4,3,2,1,0:T(8,128)(2,1)S(1)}, u32[]{:S(2)}, u32[]{:S(2)}) collective-permute-start(bf16[2,2,2,64,512]{4,3,2,1,0:T(8,128)(2,1)S(1)} %get-tuple-element.235), channel_id=1, source_target_pairs={{0,8},{1,9},{2,10},{3,11},{4,12},{5,13},{6,14},{7,15},{8,0},{9,1},... | collective-permute-start | bytes 1572872 | tf_op jit(solution)/shard_map/ppermute | solution.py:46
  122.7 12.8 %collective-permute-start.27 = (bf16[2,128,512]{2,1,0:T(8,128)(2,1)S(1)}, bf16[2,128,512]{2,1,0:T(8,128)(2,1)S(1)}, u32[]{:S(2)}, u32[]{:S(2)}) collective-permute-start(bf16[2,128,512]{2,1,0:T(8,128)(2,1)S(1)} %get-tuple-element.225), channel_id=1, source_target_pairs={{0,2},{1,3},{2,0},{3,1},{4,6},{5,7},{6,4},{7,5},{8,10},{9,11},{10,... | collective-permute-start | bytes 786440 | tf_op jit(solution)/shard_map/ppermute | solution.py:46
  122.7 14.6 %collective-permute-start.29 = (bf16[2,128,512]{2,1,0:T(8,128)(2,1)S(1)}, bf16[2,128,512]{2,1,0:T(8,128)(2,1)S(1)}, u32[]{:S(2)}, u32[]{:S(2)}) collective-permute-start(bf16[2,128,512]{2,1,0:T(8,128)(2,1)S(1)} %get-tuple-element.229), channel_id=1, source_target_pairs={{0,4},{1,5},{2,6},{3,7},{4,0},{5,1},{6,2},{7,3},{8,12},{9,13},{10,... | collective-permute-start | bytes 786440 | tf_op jit(solution)/shard_map/ppermute | solution.py:46
  152.2 9.1 %collective-permute-start.36 = (bf16[2,2,2,2,112,512]{5,4,3,2,1,0:T(8,128)(2,1)S(1)}, bf16[2,2,2,2,112,512]{5,4,3,2,1,0:T(8,128)(2,1)S(1)}, u32[]{:S(2)}, u32[]{:S(2)}) collective-permute-start(bf16[2,2,2,2,112,512]{5,4,3,2,1,0:T(8,128)(2,1)S(1)} %bitcast.75), channel_id=1, source_target_pairs={{0,1},{1,0},{2,3},{3,2},{4,5},{5,4},{6,7},{7,6},{8,9},{9,8},{10,11... | collective-permute-start | bytes 5505032 | tf_op jit(solution)/shard_map/ppermute | solution.py:46
  162.0 16.7 %collective-permute-start.38 = (bf16[2,2,2,80,512]{4,3,2,1,0:T(8,128)(2,1)S(1)}, bf16[2,2,2,80,512]{4,3,2,1,0:T(8,128)(2,1)S(1)}, u32[]{:S(2)}, u32[]{:S(2)}) collective-permute-start(bf16[2,2,2,80,512]{4,3,2,1,0:T(8,128)(2,1)S(1)} %get-tuple-element.266), channel_id=1, source_target_pairs={{0,16},{1,17},{2,18},{3,19},{4,20},{5,21},{6,22},{7,23},{8,24},{9,... | collective-permute-start | bytes 1966088 | tf_op jit(solution)/shard_map/ppermute | solution.py:46
  164.5 9.2 %collective-permute-start.39 = (bf16[2,2,2,32,512]{4,3,2,1,0:T(8,128)(2,1)S(1)}, bf16[2,2,2,32,512]{4,3,2,1,0:T(8,128)(2,1)S(1)}, u32[]{:S(2)}, u32[]{:S(2)}) collective-permute-start(bf16[2,2,2,32,512]{4,3,2,1,0:T(8,128)(2,1)S(1)} %get-tuple-element.269), channel_id=1, source_target_pairs={{0,8},{1,9},{2,10},{3,11},{4,12},{5,13},{6,14},{7,15},{8,0},{9,1},... | collective-permute-start | bytes 786440 | tf_op jit(solution)/shard_map/ppermute | solution.py:46
  165.7 16.2 %collective-permute-start.41 = (bf16[2,2,2,48,512]{4,3,2,1,0:T(8,128)(2,1)S(1)}, bf16[2,2,2,48,512]{4,3,2,1,0:T(8,128)(2,1)S(1)}, u32[]{:S(2)}, u32[]{:S(2)}) collective-permute-start(bf16[2,2,2,48,512]{4,3,2,1,0:T(8,128)(2,1)S(1)} %get-tuple-element.274), channel_id=1, source_target_pairs={{0,8},{1,9},{2,10},{3,11},{4,12},{5,13},{6,14},{7,15},{8,0},{9,1},... | collective-permute-start | bytes 1179656 | tf_op jit(solution)/shard_map/ppermute | solution.py:46
  179.4 9.0 %collective-permute-start.45 = (bf16[144,512]{1,0:T(8,128)(2,1)S(1)}, bf16[144,512]{1,0:T(8,128)(2,1)S(1)}, u32[]{:S(2)}, u32[]{:S(2)}) collective-permute-start(bf16[144,512]{1,0:T(8,128)(2,1)S(1)} %get-tuple-element.286), channel_id=1, source_target_pairs={{0,4},{1,5},{2,6},{3,7},{4,0},{5,1},{6,2},{7,3},{8,12},{9,13},{10,... | collective-permute-start | bytes 442376 | tf_op jit(solution)/shard_map/ppermute | solution.py:46
  (31 other events, 210.8 us)

commit v3 on v2

--- a/solution.py
+++ b/solution.py
@@ -73,11 +73,20 @@
     return (2,) * len(bits) + tuple(rows)
 
 
-def at_bit(rank, axis, index, rows):
-    where = [slice(None)] * rank
+def cut_of(rank, cut):
+    by_lanes, part = cut
+    last = (slice(None), part) if by_lanes else (part, slice(None))
+    return (slice(None),) * (rank - 2) + last
+
+
+def at_bit(rank, axis, index, cut):
+    where = list(cut_of(rank, cut))
     where[axis] = pl.ds(index, 1)
-    where[-2] = rows
     return tuple(where)
+
+
+def cut_shape(shape, by_lanes, size):
+    return (shape[0], size) if by_lanes else (size, shape[1])
 
 
 def overlaps(lefts, rights):
@@ -101,7 +110,7 @@
     for i, j, inside, outside in cuts:
         mine, other, out = refs[2 * i], refs[2 * i + 1], refs[2 * count + j]
         rank, axis, at = len(out.shape), axes[i], uppers[masks[i].bit_length() - 1]
-        source = (slice(None),) * (rank - 3) + (inside, slice(None))
+        source = cut_of(rank - 1, inside)
         out[at_bit(rank, axis, at, outside)] = jnp.expand_dims(mine[source], axis)
         out[at_bit(rank, axis, 1 - at, outside)] = jnp.expand_dims(other[source], axis)
 
@@ -111,7 +120,7 @@
         keep, other = refs[2 * i], refs[2 * i + 1]
         next_keep, next_send = refs[2 * count + 2 * j], refs[2 * count + 2 * j + 1]
         rank, axis, at = len(keep.shape), axes[j], uppers[masks[j].bit_length() - 1]
-        into = (slice(None),) * (rank - 3) + (outside, slice(None))
+        into = cut_of(rank - 1, outside)
         here, there = at_bit(rank, axis, at, inside), at_bit(rank, axis, 1 - at, inside)
         next_send[into] = jnp.squeeze(keep[there] + other[there], axis)
         next_keep[into] = jnp.squeeze(keep[here] + other[here], axis)
@@ -120,20 +129,21 @@
 def place(order, *jobs):
     axes, masks, cuts, args, outs, plans = [], [], [], [], [], []
     for gather, sizes in jobs:
-        olds = [p.shape[-2] for p in gather.parts]
+        lanes = gather.by_lanes
+        whole = (gather.rows, gather.width)
+        olds = [p.shape[-1 if lanes else -2] for p in gather.parts]
         sizes = sizes or olds
         bits = [sorted(b + [m], reverse=True) for b, m in zip(gather.bits, gather.masks)]
         own_axes = [axis_of(b, m) for b, m in zip(gather.bits, gather.masks)]
         bits = [bits[min(j, len(bits) - 1)] for j in range(len(sizes))]
         found = overlaps(olds, sizes)
         plans.append((gather, olds, sizes, bits, own_axes, len(outs)))
-        cuts += [(len(axes) + i, len(outs) + j, x, y) for i, j, x, y in found]
+        cuts += [(len(axes) + i, len(outs) + j, (lanes, x), (lanes, y)) for i, j, x, y in found]
         axes += own_axes
         masks += gather.masks
         for mine, other in zip(gather.parts, gather.others):
             args += [order.turn(mine), other]
-        width = gather.parts[0].shape[-1]
-        outs += [(bit_shape(b, (r, width)), BF16) for b, r in zip(bits, sizes)]
+        outs += [(bit_shape(b, cut_shape(whole, lanes, r)), BF16) for b, r in zip(bits, sizes)]
     if device_count() == GROUPS:
         body = functools.partial(place_kernel, axes, masks, cuts)
         placed = kernel(body, (order.uppers, *args), outs, 0, 24)
@@ -148,28 +158,30 @@
                 up = upper_half(mask)
                 low, high = jnp.where(up, other, mine), jnp.where(up, mine, other)
                 held.append(jnp.stack([low, high], axis=axis))
-            parts = cut_rows(held, olds, sizes)
+            parts = cut_parts(held, olds, sizes, gather.by_lanes)
         gather.parts, gather.bits = parts, bits
 
 
 def add(order, *jobs):
     axes, all_masks, cuts, args, outs, plans, count = [], [], [], [], [], [], 0
     for chain, masks, sizes in jobs:
-        olds = [p.shape[-2] for p in chain.keeps]
+        lanes = chain.by_lanes
+        whole = (chain.rows, chain.width)
+        olds = [p.shape[-1 if lanes else -2] for p in chain.keeps]
         sizes = sizes or olds
         bits = [chain.bits[min(j, len(olds) - 1)] for j in range(len(sizes))]
         own_axes = [axis_of(b, m) for b, m in zip(bits, masks)]
         left = [[b for b in old if b != m] for old, m in zip(bits, masks)]
         plans.append((chain, masks, olds, sizes, own_axes, left, len(axes)))
-        cuts += [(count + i, len(axes) + j, x, y) for i, j, x, y in overlaps(olds, sizes)]
+        found = overlaps(olds, sizes)
+        cuts += [(count + i, len(axes) + j, (lanes, x), (lanes, y)) for i, j, x, y in found]
         axes += own_axes
         all_masks += masks
         count += len(olds)
         for keep, other in zip(chain.keeps, chain.others):
             args += [order.turn(keep), other]
-        width = chain.keeps[0].shape[-1]
         for b, r in zip(left, sizes):
-            outs += [(bit_shape(b, (r, width)), BF16)] * 2
+            outs += [(bit_shape(b, cut_shape(whole, lanes, r)), BF16)] * 2
     if device_count() == GROUPS:
         body = functools.partial(add_kernel, axes, all_masks, cuts, count)
         both = kernel(body, (order.uppers, *args), outs, 0, 24)
@@ -183,7 +195,7 @@
                 (k.astype(F32) + o.astype(F32)).astype(BF16)
                 for k, o in zip(chain.keeps, chain.others)
             ]
-            sums = cut_rows(sums, olds, sizes)
+            sums = cut_parts(sums, olds, sizes, chain.by_lanes)
             sides = list(zip(sums, [upper_half(m) for m in masks], own_axes))
             take = lax.dynamic_index_in_dim
             chain.keeps = [take(t, u, axis, False) for t, u, axis in sides]
@@ -192,8 +204,9 @@
 
 
 class Gather:
-    def __init__(self, order, *parts):
-        self.order, self.parts, self.bits = order, list(parts), [[] for _ in parts]
+    def __init__(self, order, part, by_lanes=False):
+        self.order, self.parts, self.bits = order, [part], [[]]
+        self.by_lanes, (self.rows, self.width) = by_lanes, part.shape
 
     def go(self, *masks, wait=False):
         self.masks = masks
@@ -209,18 +222,20 @@
         return held.reshape((-1,) + held.shape[-2:])
 
 
-def cut_rows(arrays, olds, sizes):
+def cut_parts(arrays, olds, sizes, by_lanes):
     if list(olds) == list(sizes):
         return arrays
-    joint = jnp.concatenate(arrays, axis=-2)
+    axis = -1 if by_lanes else -2
+    joint = jnp.concatenate(arrays, axis=axis)
     ends = [sum(sizes[: j + 1]) for j in range(len(sizes) - 1)]
-    return jnp.split(joint, ends, axis=-2)
+    return jnp.split(joint, ends, axis=axis)
 
 
 class Reduce:
-    def __init__(self, order, keep, send, bits):
+    def __init__(self, order, keep, send, bits, by_lanes=False):
         shape = bit_shape(bits, keep.shape[-2:])
         self.order, self.bits = order, [bits]
+        self.by_lanes, (self.rows, self.width) = by_lanes, keep.shape[-2:]
         self.keeps, self.sends = [keep.reshape(shape)], [send.reshape(shape)]
 
     def go(self, *masks, wait=False):
@@ -879,29 +894,19 @@
         second = jnp.concatenate([w_value, *conv_value, w_query], axis=0)
         ups = [w_up[:, width * c : width * (c + 1)] for c in range(wide)]
         rest = jnp.concatenate([w_out] + ups + [w_down], axis=0)
-    rest_rows = rest.shape[0]
-    upper_rows = share * (1 + wide)
-    one, two, both = Gather(order, first), Gather(order, second), Gather(order, rest)
+    one, two, both = Gather(order, first), Gather(order, second), Gather(order, rest, True)
     one.go(along[0])
     two.go(back[0])
-    last_rows = lax.optimization_barrier((tokens[:, 0, each - RIM :], first))[0]
-    halo = lax.ppermute(last_rows, "seq", [(i, i + 1) for i in range(seq - 1)])
-    halo = halo.reshape(micro * RIM, width)
     for at in range(1, len(along)):
         one.place()
         if at == 1:
-            lengths = order.turn(lengths[:, 0])
-            first_pad = 3 * ((lengths[:, 0] + 2) // 3)
-            second_pad = 3 * ((lengths[:, 1] + 2) // 3)
-            start = 1 + first_pad
-            seats = [lax.axis_index("seq") * each, upper_half(1) if whole else 0, upper_half(1)]
-            seats = [jnp.full_like(start, seat) for seat in seats]
-            info = [1 + lengths[:, 0], start, start + lengths[:, 1], start + second_pad]
-            info = jnp.stack(info + seats, axis=1).astype(jnp.int32)
+            last_rows = order.turn(tokens[:, 0, each - RIM :])
+            halo = lax.ppermute(last_rows, "seq", [(i, i + 1) for i in range(seq - 1)])
+            halo = halo.reshape(micro * RIM, width)
         one.go(along[at])
         two.place()
         two.go(back[at])
-    order.done((halo, info, rest))
+    order.done((halo, rest))
     one.place()
     one.go(across[0])
     two.place()
@@ -920,9 +925,18 @@
             two.go(across[-1 - at])
         if at < len(along):
             both.go(along[at])
+    lengths = order.turn(lengths[:, 0])
+    first_pad = 3 * ((lengths[:, 0] + 2) // 3)
+    second_pad = 3 * ((lengths[:, 1] + 2) // 3)
+    start = 1 + first_pad
+    seats = [lax.axis_index("seq") * each, upper_half(1) if whole else 0, upper_half(1)]
+    seats = [jnp.full_like(start, seat) for seat in seats]
+    info = [1 + lengths[:, 0], start, start + lengths[:, 1], start + second_pad]
+    info = jnp.stack(info + seats, axis=1).astype(jnp.int32)
+    order.done((order.last, info))
     one.place()
     one.go(1)
-    place(order, (two, ()), (both, (upper_rows, rest_rows - upper_rows)))
+    place(order, (two, ()), (both, (width // 2, width // 2)))
     two.go(1)
     both.go(across[0], across[-1])
     first = one.place().whole()
@@ -978,7 +992,7 @@
             values_side.go(back[at])
         if at < len(across):
             both.go(across[at], across[-1 - at])
-    place(order, (keys_side, ()), (values_side, ()), (both, (rest_rows,)))
+    place(order, (keys_side, ()), (values_side, ()), (both, (width,)))
     keys_side.go(1)
     values_side.go(1)
     both.go(1)
@@ -1007,12 +1021,12 @@
     order.done(halves[0])
     all_bits = powers(2, count)[::-1]
 
-    def begin(keep, send, size):
+    def begin(keep, send, size, by_lanes=False):
         if not whole:
             keep, send = split_cores(scattered(joined(keep, send), size))
-        return Reduce(order, keep, send, all_bits)
-
-    feeds = begin(*halves, rest_sizes)
+        return Reduce(order, keep, send, all_bits, by_lanes)
+
+    feeds = begin(*halves, rest_sizes, True)
     feeds.go(1)
     memory_half = ((seq // 2, slots, width), BF16)
     chips = (seq // 2, 2, slots, width)
@@ -1041,7 +1055,7 @@
     cross = [(across[-1 - at], across[at]) for at in range(len(across))]
     keys_side.add((back[0],))
     keys_side.go(back[0])
-    cuts = (upper_rows, rest_rows - upper_rows)
+    cuts = (width // 2, width // 2)
     add(order, (values_side, (along[0],), ()), (feeds, cross[0], cuts))
     values_side.go(along[0])
     feeds.go(*cross[0])
@@ -1058,7 +1072,7 @@
             values_side.go(along[at])
         if at < len(cross):
             feeds.go(*cross[at])
-    feeds.add((back[0],), rest_rows)
+    feeds.add((back[0],), width)
     key_grad, value_grad = (held.total().astype(BF16) for held in (keys_side, values_side))
     key_kept, value_kept, rims, *halves = kernel(
         compress_back_kernel,

time: 209 us -> 205 us (0.981)
  waiting for transfers between devices: 93.1 us -> 90.8 us
    ppermute x48, waiting for transfers between devices: 90.7 us -> 87.7 us  [swap(): lax.ppermute(array, AXES, [(i, i ^ mask) for i in range(device_count())])]
  transfers between devices with their start and end apart: 50 -> 50, of which waited for: 33 -> 34; matrix products, arithmetic and copies ran while one was open for 3% -> 2% of each run, Pallas kernels for 14% -> 14%
where the time goes in v3:
time: 205 us
  waiting for transfers between devices  90.8 us (44%)
  starting transfers between devices  55.5 us (27%)
  Pallas kernels  47.8 us (23%)
  local copies, waits for them, and re-layouts  7.22 us (4%)
  other arithmetic  2.39 us (1%)
    ppermute x48, waiting for transfers between devices, swap(): lax.ppermute(array, AXES, [(i, i ^ mask) for i in range(device_count())])  87.7 us
    ppermute x48, starting transfers between devices, swap(): lax.ppermute(array, AXES, [(i, i ^ mask) for i in range(device_count())])  52.7 us
    pallas_call x35, Pallas kernels, kernel(): pl.pallas_call(body, in_specs=[pl.BlockSpec(memory_space=spec.get(a.dtype...  46 us
  transfers between devices with their start and end apart: 50, of which 34 were waited for; matrix products, arithmetic and copies ran while one was open for 2% of the time, Pallas kernels for 14%

profile of v3, /device:TPU:0, one launch (start us, length us, event | category | flops | bytes accessed | tf_op | source)
XLA Modules:
  0.0 204.9 jit_solution(7589009725428795109)
XLA Ops:
  4.0 4.1 %collective-permute-start = (bf16[80,512]{1,0:T(8,128)(2,1)}, bf16[80,512]{1,0:T(8,128)(2,1)S(1)}, u32[]{:S(2)}, u32[]{:S(2)}) collective-permute-start(bf16[80,512]{1,0:T(8,128)(2,1)} %get-tuple-element.158.refs_0_), channel_id=1, source_target_pairs={{0,4},{1,5},{2,6},{3,7},{4,0},{5,1},{6,2},{7,3},{8,12},{9,13},{10,... | collective-permute-start | bytes 245768 | tf_op jit(solution)/shard_map/ppermute | solution.py:46
  9.7 2.3 %collective-permute-done.refs_1_ = bf16[80,512]{1,0:T(8,128)(2,1)S(1)} collective-permute-done((bf16[80,512]{1,0:T(8,128)(2,1)}, bf16[80,512]{1,0:T(8,128)(2,1)S(1)}, u32[]{:S(2)}, u32[]{:S(2)}) %collective-permute-start) | collective-permute-done | bytes 81952 | tf_op jit(solution)/shard_map/ppermute | solution.py:46
  16.3 3.3 %collective-permute-start.4 = (bf16[2,80,512]{2,1,0:T(8,128)(2,1)S(1)}, bf16[2,80,512]{2,1,0:T(8,128)(2,1)S(1)}, u32[]{:S(2)}, u32[]{:S(2)}) collective-permute-start(bf16[2,80,512]{2,1,0:T(8,128)(2,1)S(1)} %shard_map.290.refs_0_), channel_id=1, source_target_pairs={{0,4},{1,5},{2,6},{3,7},{4,0},{5,1},{6,2},{7,3},{8,12},{9,13},{10,... | collective-permute-start | bytes 491528 | tf_op jit(solution)/shard_map/ppermute | solution.py:46
  24.6 2.5 %collective-permute-done.4.refs_1_ = bf16[2,80,512]{2,1,0:T(8,128)(2,1)S(1)} collective-permute-done((bf16[2,80,512]{2,1,0:T(8,128)(2,1)S(1)}, bf16[2,80,512]{2,1,0:T(8,128)(2,1)S(1)}, u32[]{:S(2)}, u32[]{:S(2)}) %collective-permute-start.4) | collective-permute-done | bytes 163872 | tf_op jit(solution)/shard_map/ppermute | solution.py:46
  29.2 2.9 %collective-permute-start.7 = (bf16[144,512]{1,0:T(8,128)(2,1)}, bf16[144,512]{1,0:T(8,128)(2,1)S(1)}, u32[]{:S(2)}, u32[]{:S(2)}) collective-permute-start(bf16[144,512]{1,0:T(8,128)(2,1)} %get-tuple-element.167.refs_2_), channel_id=1, source_target_pairs={{0,4},{1,5},{2,6},{3,7},{4,0},{5,1},{6,2},{7,3},{8,12},{9,13},{10,... | collective-permute-start | bytes 442376 | tf_op jit(solution)/shard_map/ppermute | solution.py:46
  35.7 2.4 %collective-permute-done.7.refs_3_ = bf16[144,512]{1,0:T(8,128)(2,1)S(1)} collective-permute-done((bf16[144,512]{1,0:T(8,128)(2,1)}, bf16[144,512]{1,0:T(8,128)(2,1)S(1)}, u32[]{:S(2)}, u32[]{:S(2)}) %collective-permute-start.7) | collective-permute-done | bytes 147488 | tf_op jit(solution)/shard_map/ppermute | solution.py:46
  41.0 9.8 %collective-permute-done.8.refs_1_ = bf16[2,2,2,80,512]{4,3,2,1,0:T(8,128)(2,1)S(1)} collective-permute-done((bf16[2,2,2,80,512]{4,3,2,1,0:T(8,128)(2,1)S(1)}, bf16[2,2,2,80,512]{4,3,2,1,0:T(8,128)(2,1)S(1)}, u32[]{:S(2)}, u32[]{:S(2)}) %collective-permute-start.8) | collective-permute-done | bytes 655392 | tf_op jit(solution)/shard_map/ppermute | solution.py:46
  51.5 3.4 %collective-permute-done.9.refs_1_ = bf16[2,2,2,80,512]{4,3,2,1,0:T(8,128)(2,1)S(1)} collective-permute-done((bf16[2,2,2,80,512]{4,3,2,1,0:T(8,128)(2,1)S(1)}, bf16[2,2,2,80,512]{4,3,2,1,0:T(8,128)(2,1)S(1)}, u32[]{:S(2)}, u32[]{:S(2)}) %collective-permute-start.9) | collective-permute-done | bytes 655392 | tf_op jit(solution)/shard_map/ppermute | solution.py:46
  66.6 2.7 %collective-permute-done.13.refs_1_ = bf16[128,512]{1,0:T(8,128)(2,1)S(1)} collective-permute-done((bf16[128,512]{1,0:T(8,128)(2,1)S(1)}, bf16[128,512]{1,0:T(8,128)(2,1)S(1)}, u32[]{:S(2)}, u32[]{:S(2)}) %collective-permute-start.13) | collective-permute-done | bytes 131104 | tf_op jit(solution)/shard_map/ppermute | solution.py:46
  73.4 2.4 %collective-permute-start.17 = (bf16[2,128,512]{2,1,0:T(8,128)(2,1)S(1)}, bf16[2,128,512]{2,1,0:T(8,128)(2,1)S(1)}, u32[]{:S(2)}, u32[]{:S(2)}) collective-permute-start(bf16[2,128,512]{2,1,0:T(8,128)(2,1)S(1)} %get-tuple-element.188.refs_0_), channel_id=1, source_target_pairs={{0,2},{1,3},{2,0},{3,1},{4,6},{5,7},{6,4},{7,5},{8,10},{9,11},{10,... | collective-permute-start | bytes 786440 | tf_op jit(solution)/shard_map/ppermute | solution.py:46
  75.8 11.0 %collective-permute-done.18.refs_3_ = bf16[2,128,512]{2,1,0:T(8,128)(2,1)S(1)} collective-permute-done((bf16[2,128,512]{2,1,0:T(8,128)(2,1)S(1)}, bf16[2,128,512]{2,1,0:T(8,128)(2,1)S(1)}, u32[]{:S(2)}, u32[]{:S(2)}) %collective-permute-start.18) | collective-permute-done | bytes 262176 | tf_op jit(solution)/shard_map/ppermute | solution.py:46
  88.6 4.7 %collective-permute-done.21.refs_1_ = bf16[2,2,128,512]{3,2,1,0:T(8,128)(2,1)S(1)} collective-permute-done((bf16[2,2,128,512]{3,2,1,0:T(8,128)(2,1)S(1)}, bf16[2,2,128,512]{3,2,1,0:T(8,128)(2,1)S(1)}, u32[]{:S(2)}, u32[]{:S(2)}) %collective-permute-start.21) | collective-permute-done | bytes 524320 | tf_op jit(solution)/shard_map/ppermute | solution.py:46
  94.7 3.8 %shard_map.305 = (f32[384,512]{1,0:T(8,128)S(1)}, f32[384,128]{1,0:T(8,128)S(1)}) custom-call(s32[2,7]{1,0:T(2,128)S(1)} %stack.47.info, bf16[384,512]{1,0:T(8,128)(2,1)S(1)} %get-tuple-element.210.query, bf16[384,512]{1,0:T(8,128)(2,1)S(1)} %get-tuple-element.202.keys, bf16[384,512]{1,0:T(8,128)(2,1)S(1)} %get-tuple-element.203.values, ...), custom_call_target="tpu_custom_call" | custom-call | flops 805306368 | bytes 3276856 | tf_op jit(solution)/shard_map/pallas_call | solution.py:342
  99.5 9.7 %shard_map.307 = (bf16[384,512]{1,0:T(8,128)(2,1)}, f32[384,512]{1,0:T(8,128)S(1)}, bf16[384,512]{1,0:T(8,128)(2,1)S(1)}, bf16[16,144,512]{2,1,0:T(8,128)(2,1)S(...) custom-call(s32[2,7]{1,0:T(2,128)S(1)} %stack.47.info, bf16[384,512]{1,0:T(8,128)(2,1)S(1)} %bitcast.68, ...), custom_call_target="tpu_custom_call" | custom-call | flops 5435817984 | bytes 6324280 | tf_op jit(solution)/shard_map/pallas_call | solution.py:342
  109.4 5.6 %shard_map.308 = (bf16[384,512]{1,0:T(8,128)(2,1)S(1)}, bf16[4,128,512]{2,1,0:T(8,128)(2,1)S(1)}, bf16[4,128,512]{2,1,0:T(8,128)(2,1)S(1)}, bf16[4,128,512]{2,1,...) custom-call(s32[2,7]{1,0:T(2,128)S(1)} %stack.47.info, ...), custom_call_target="tpu_custom_call" | custom-call | flops 2013265920 | bytes 4653112 | tf_op jit(solution)/shard_map/pallas_call | solution.py:342
  120.0 3.3 %collective-permute-start.29 = (bf16[2,128,512]{2,1,0:T(8,128)(2,1)S(1)}, bf16[2,128,512]{2,1,0:T(8,128)(2,1)S(1)}, u32[]{:S(2)}, u32[]{:S(2)}) collective-permute-start(bf16[2,128,512]{2,1,0:T(8,128)(2,1)S(1)} %get-tuple-element.229), channel_id=1, source_target_pairs={{0,4},{1,5},{2,6},{3,7},{4,0},{5,1},{6,2},{7,3},{8,12},{9,13},{10,... | collective-permute-start | bytes 786440 | tf_op jit(solution)/shard_map/ppermute | solution.py:46
  123.3 10.0 %collective-permute-done.27.refs_1_ = bf16[2,128,512]{2,1,0:T(8,128)(2,1)S(1)} collective-permute-done((bf16[2,128,512]{2,1,0:T(8,128)(2,1)S(1)}, bf16[2,128,512]{2,1,0:T(8,128)(2,1)S(1)}, u32[]{:S(2)}, u32[]{:S(2)}) %collective-permute-start.27) | collective-permute-done | bytes 262176 | tf_op jit(solution)/shard_map/ppermute | solution.py:46
  145.9 2.7 %shard_map.314 = (f32[384,512]{1,0:T(8,128)S(1)}, f32[384,512]{1,0:T(8,128)S(1)}, f32[16,1024]{1,0:T(8,128)S(1)}, bf16[16,112,512]{2,1,0:T(8,128)(2,1)S(1)}, bf16[16,112,512]{2,1,0:T(8,128)(2,1)S(1)}) custom-call(s32[2,7]{1,0:T(2,128)S(1)} %stack.47.info, bf16[128,512]{1,0:T(8,128)(2,1)S(1)} %add_convert_fusion.1.key_memory, ...), custom_call_target="tpu_custom_call" | custom-call | flops 1006632960 | bytes 7094328 | tf_op jit(solution)/shard_map/pallas_call | solution.py:342
  150.1 2.3 %collective-permute-done.35.rims = f32[16,1024]{1,0:T(8,128)S(1)} collective-permute-done((f32[16,1024]{1,0:T(8,128)S(1)}, f32[16,1024]{1,0:T(8,128)S(1)}, u32[]{:S(2)}, u32[]{:S(2)}) %collective-permute-start.35) | collective-permute-done | bytes 65568 | tf_op jit(solution)/shard_map/ppermute | solution.py:1096
  152.5 2.9 %shard_map.315 = (bf16[384,512]{1,0:T(8,128)(2,1)}, bf16[16,48,512]{2,1,0:T(8,128)(2,1)S(1)}, bf16[16,48,512]{2,1,0:T(8,128)(2,1)S(1)}) custom-call(s32[2,7]{1,0:T(2,128)S(1)} %stack.47.info, bf16[384,512]{1,0:T(8,128)(2,1)S(1)} %bitcast.69, bf16[400,512]{1,0:T(8,128)(2,1)S(1)} %get-tuple-element.178.normed, ...), custom_call_target="tpu_custom_call" | custom-call | flops 1207959552 | bytes 10502200 | tf_op jit(solution)/shard_map/pallas_call | solution.py:342
  163.1 5.5 %collective-permute-done.40.refs_5_ = bf16[2,144,512]{2,1,0:T(8,128)(2,1)S(1)} collective-permute-done((bf16[2,144,512]{2,1,0:T(8,128)(2,1)S(1)}, bf16[2,144,512]{2,1,0:T(8,128)(2,1)S(1)}, u32[]{:S(2)}, u32[]{:S(2)}) %collective-permute-start.40) | collective-permute-done | bytes 294944 | tf_op jit(solution)/shard_map/ppermute | solution.py:46
  169.6 5.5 %collective-permute-done.38.refs_1_ = bf16[2,2,2,80,512]{4,3,2,1,0:T(8,128)(2,1)S(1)} collective-permute-done((bf16[2,2,2,80,512]{4,3,2,1,0:T(8,128)(2,1)S(1)}, bf16[2,2,2,80,512]{4,3,2,1,0:T(8,128)(2,1)S(1)}, u32[]{:S(2)}, u32[]{:S(2)}) %collective-permute-start.38) | collective-permute-done | bytes 655392 | tf_op jit(solution)/shard_map/ppermute | solution.py:46
  181.2 3.3 %collective-permute-done.45 = bf16[144,512]{1,0:T(8,128)(2,1)S(1)} collective-permute-done((bf16[144,512]{1,0:T(8,128)(2,1)S(1)}, bf16[144,512]{1,0:T(8,128)(2,1)S(1)}, u32[]{:S(2)}, u32[]{:S(2)}) %collective-permute-start.45) | collective-permute-done | bytes 147488 | tf_op jit(solution)/shard_map/ppermute | solution.py:46
  190.8 3.9 %collective-permute-done.46.refs_1_ = bf16[2,112,512]{2,1,0:T(8,128)(2,1)S(1)} collective-permute-done((bf16[2,112,512]{2,1,0:T(8,128)(2,1)S(1)}, bf16[2,112,512]{2,1,0:T(8,128)(2,1)S(1)}, u32[]{:S(2)}, u32[]{:S(2)}) %collective-permute-start.46) | collective-permute-done | bytes 229408 | tf_op jit(solution)/shard_map/ppermute | solution.py:46
  (145 shorter events, 93.6 us)
Async XLA Ops:
  13.5 9.0 %collective-permute-start.3 = (bf16[2,80,512]{2,1,0:T(8,128)(2,1)S(1)}, bf16[2,80,512]{2,1,0:T(8,128)(2,1)S(1)}, u32[]{:S(2)}, u32[]{:S(2)}) collective-permute-start(bf16[2,80,512]{2,1,0:T(8,128)(2,1)S(1)} %shard_map.289.refs_0_), channel_id=1, source_target_pairs={{0,2},{1,3},{2,0},{3,1},{4,6},{5,7},{6,4},{7,5},{8,10},{9,11},{10,... | collective-permute-start | bytes 491528 | tf_op jit(solution)/shard_map/ppermute | solution.py:46
  16.3 10.8 %collective-permute-start.4 = (bf16[2,80,512]{2,1,0:T(8,128)(2,1)S(1)}, bf16[2,80,512]{2,1,0:T(8,128)(2,1)S(1)}, u32[]{:S(2)}, u32[]{:S(2)}) collective-permute-start(bf16[2,80,512]{2,1,0:T(8,128)(2,1)S(1)} %shard_map.290.refs_0_), channel_id=1, source_target_pairs={{0,4},{1,5},{2,6},{3,7},{4,0},{5,1},{6,2},{7,3},{8,12},{9,13},{10,... | collective-permute-start | bytes 491528 | tf_op jit(solution)/shard_map/ppermute | solution.py:46
  23.0 10.5 %collective-permute-start.5 = (bf16[2,2,80,512]{3,2,1,0:T(8,128)(2,1)S(1)}, bf16[2,2,80,512]{3,2,1,0:T(8,128)(2,1)S(1)}, u32[]{:S(2)}, u32[]{:S(2)}) collective-permute-start(bf16[2,2,80,512]{3,2,1,0:T(8,128)(2,1)S(1)} %shard_map.291.refs_0_), channel_id=1, source_target_pairs={{0,8},{1,9},{2,10},{3,11},{4,12},{5,13},{6,14},{7,15},{8,0},{9,1},... | collective-permute-start | bytes 983048 | tf_op jit(solution)/shard_map/ppermute | solution.py:46
  27.6 10.4 %collective-permute-start.6 = (bf16[2,2,80,512]{3,2,1,0:T(8,128)(2,1)S(1)}, bf16[2,2,80,512]{3,2,1,0:T(8,128)(2,1)S(1)}, u32[]{:S(2)}, u32[]{:S(2)}) collective-permute-start(bf16[2,2,80,512]{3,2,1,0:T(8,128)(2,1)S(1)} %shard_map.292.refs_0_), channel_id=1, source_target_pairs={{0,16},{1,17},{2,18},{3,19},{4,20},{5,21},{6,22},{7,23},{8,24},{9,... | collective-permute-start | bytes 983048 | tf_op jit(solution)/shard_map/ppermute | solution.py:46
  29.2 8.8 %collective-permute-start.7 = (bf16[144,512]{1,0:T(8,128)(2,1)}, bf16[144,512]{1,0:T(8,128)(2,1)S(1)}, u32[]{:S(2)}, u32[]{:S(2)}) collective-permute-start(bf16[144,512]{1,0:T(8,128)(2,1)} %get-tuple-element.167.refs_2_), channel_id=1, source_target_pairs={{0,4},{1,5},{2,6},{3,7},{4,0},{5,1},{6,2},{7,3},{8,12},{9,13},{10,... | collective-permute-start | bytes 442376 | tf_op jit(solution)/shard_map/ppermute | solution.py:46
  34.1 16.6 %collective-permute-start.8 = (bf16[2,2,2,80,512]{4,3,2,1,0:T(8,128)(2,1)S(1)}, bf16[2,2,2,80,512]{4,3,2,1,0:T(8,128)(2,1)S(1)}, u32[]{:S(2)}, u32[]{:S(2)}) collective-permute-start(bf16[2,2,2,80,512]{4,3,2,1,0:T(8,128)(2,1)S(1)} %shard_map.293.refs_0_), channel_id=1, source_target_pairs={{0,16},{1,17},{2,18},{3,19},{4,20},{5,21},{6,22},{7,23},{8,24},{9,... | collective-permute-start | bytes 1966088 | tf_op jit(solution)/shard_map/ppermute | solution.py:46
  38.7 16.2 %collective-permute-start.9 = (bf16[2,2,2,80,512]{4,3,2,1,0:T(8,128)(2,1)S(1)}, bf16[2,2,2,80,512]{4,3,2,1,0:T(8,128)(2,1)S(1)}, u32[]{:S(2)}, u32[]{:S(2)}) collective-permute-start(bf16[2,2,2,80,512]{4,3,2,1,0:T(8,128)(2,1)S(1)} %get-tuple-element.171.refs_0_), channel_id=1, source_target_pairs={{0,8},{1,9},{2,10},{3,11},{4,12},{5,13},{6,14},{7,15},{8,0},{9,1},... | collective-permute-start | bytes 1966088 | tf_op jit(solution)/shard_map/ppermute | solution.py:46
  40.2 11.2 %collective-permute-start.10 = (bf16[2,144,512]{2,1,0:T(8,128)(2,1)S(1)}, bf16[2,144,512]{2,1,0:T(8,128)(2,1)S(1)}, u32[]{:S(2)}, u32[]{:S(2)}) collective-permute-start(bf16[2,144,512]{2,1,0:T(8,128)(2,1)S(1)} %get-tuple-element.173.refs_2_), channel_id=1, source_target_pairs={{0,2},{1,3},{2,0},{3,1},{4,6},{5,7},{6,4},{7,5},{8,10},{9,11},{10,... | collective-permute-start | bytes 884744 | tf_op jit(solution)/shard_map/ppermute | solution.py:46
  55.7 9.4 %collective-permute-start.15 = (bf16[2,2,144,256]{3,2,1,0:T(8,128)(2,1)S(1)}, bf16[2,2,144,256]{3,2,1,0:T(8,128)(2,1)S(1)}, u32[]{:S(2)}, u32[]{:S(2)}) collective-permute-start(bf16[2,2,144,256]{3,2,1,0:T(8,128)(2,1)S(1)} %get-tuple-element.184.refs_4_), channel_id=1, source_target_pairs={{0,8},{1,9},{2,10},{3,11},{4,12},{5,13},{6,14},{7,15},{8,0},{9,1},... | collective-permute-start | bytes 884744 | tf_op jit(solution)/shard_map/ppermute | solution.py:46
  57.5 9.1 %collective-permute-start.16 = (bf16[2,2,144,256]{3,2,1,0:T(8,128)(2,1)S(1)}, bf16[2,2,144,256]{3,2,1,0:T(8,128)(2,1)S(1)}, u32[]{:S(2)}, u32[]{:S(2)}) collective-permute-start(bf16[2,2,144,256]{3,2,1,0:T(8,128)(2,1)S(1)} %get-tuple-element.186.refs_6_), channel_id=1, source_target_pairs={{0,16},{1,17},{2,18},{3,19},{4,20},{5,21},{6,22},{7,23},{8,24},{9,... | collective-permute-start | bytes 884744 | tf_op jit(solution)/shard_map/ppermute | solution.py:46
  71.6 15.2 %collective-permute-start.19 = (bf16[2,2,2,144,256]{4,3,2,1,0:T(8,128)(2,1)S(1)}, bf16[2,2,2,144,256]{4,3,2,1,0:T(8,128)(2,1)S(1)}, u32[]{:S(2)}, u32[]{:S(2)}) collective-permute-start(bf16[2,2,2,144,256]{4,3,2,1,0:T(8,128)(2,1)S(1)} %get-tuple-element.192.refs_4_), channel_id=1, source_target_pairs={{0,16},{1,17},{2,18},{3,19},{4,20},{5,21},{6,22},{7,23},{8,24},{9,... | collective-permute-start | bytes 1769480 | tf_op jit(solution)/shard_map/ppermute | solution.py:46
  73.2 14.0 %collective-permute-start.20 = (bf16[2,2,2,144,256]{4,3,2,1,0:T(8,128)(2,1)S(1)}, bf16[2,2,2,144,256]{4,3,2,1,0:T(8,128)(2,1)S(1)}, u32[]{:S(2)}, u32[]{:S(2)}) collective-permute-start(bf16[2,2,2,144,256]{4,3,2,1,0:T(8,128)(2,1)S(1)} %get-tuple-element.194.refs_6_), channel_id=1, source_target_pairs={{0,8},{1,9},{2,10},{3,11},{4,12},{5,13},{6,14},{7,15},{8,0},{9,1},... | collective-permute-start | bytes 1769480 | tf_op jit(solution)/shard_map/ppermute | solution.py:46
  73.4 13.3 %collective-permute-start.18 = (bf16[2,128,512]{2,1,0:T(8,128)(2,1)S(1)}, bf16[2,128,512]{2,1,0:T(8,128)(2,1)S(1)}, u32[]{:S(2)}, u32[]{:S(2)}) collective-permute-start(bf16[2,128,512]{2,1,0:T(8,128)(2,1)S(1)} %get-tuple-element.190.refs_2_), channel_id=1, source_target_pairs={{0,4},{1,5},{2,6},{3,7},{4,0},{5,1},{6,2},{7,3},{8,12},{9,13},{10,... | collective-permute-start | bytes 786440 | tf_op jit(solution)/shard_map/ppermute | solution.py:46
  73.4 13.4 %collective-permute-start.17 = (bf16[2,128,512]{2,1,0:T(8,128)(2,1)S(1)}, bf16[2,128,512]{2,1,0:T(8,128)(2,1)S(1)}, u32[]{:S(2)}, u32[]{:S(2)}) collective-permute-start(bf16[2,128,512]{2,1,0:T(8,128)(2,1)S(1)} %get-tuple-element.188.refs_0_), channel_id=1, source_target_pairs={{0,2},{1,3},{2,0},{3,1},{4,6},{5,7},{6,4},{7,5},{8,10},{9,11},{10,... | collective-permute-start | bytes 786440 | tf_op jit(solution)/shard_map/ppermute | solution.py:46
  88.0 10.5 %collective-permute-start.23 = (bf16[2,2,2,2,144,512]{5,4,3,2,1,0:T(8,128)(2,1)S(1)}, bf16[2,2,2,2,144,512]{5,4,3,2,1,0:T(8,128)(2,1)S(1)}, u32[]{:S(2)}, u32[]{:S(2)}) collective-permute-start(bf16[2,2,2,2,144,512]{5,4,3,2,1,0:T(8,128)(2,1)S(1)} %get-tuple-element.205.refs_0_), channel_id=1, source_target_pairs={{0,1},{1,0},{2,3},{3,2},{4,5},{5,4},{6,7},{7,6},{8,9},{9,8},{10,11... | collective-permute-start | bytes 7077896 | tf_op jit(solution)/shard_map/ppermute | solution.py:46
  118.7 16.3 %collective-permute-start.30 = (bf16[2,2,2,144,256]{4,3,2,1,0:T(8,128)(2,1)S(1)}, bf16[2,2,2,144,256]{4,3,2,1,0:T(8,128)(2,1)S(1)}, u32[]{:S(2)}, u32[]{:S(2)}) collective-permute-start(bf16[2,2,2,144,256]{4,3,2,1,0:T(8,128)(2,1)S(1)} %get-tuple-element.232), channel_id=1, source_target_pairs={{0,16},{1,17},{2,18},{3,19},{4,20},{5,21},{6,22},{7,23},{8,24},{9,... | collective-permute-start | bytes 1769480 | tf_op jit(solution)/shard_map/ppermute | solution.py:46
  119.3 15.6 %collective-permute-start.31 = (bf16[2,2,2,144,256]{4,3,2,1,0:T(8,128)(2,1)S(1)}, bf16[2,2,2,144,256]{4,3,2,1,0:T(8,128)(2,1)S(1)}, u32[]{:S(2)}, u32[]{:S(2)}) collective-permute-start(bf16[2,2,2,144,256]{4,3,2,1,0:T(8,128)(2,1)S(1)} %get-tuple-element.235), channel_id=1, source_target_pairs={{0,8},{1,9},{2,10},{3,11},{4,12},{5,13},{6,14},{7,15},{8,0},{9,1},... | collective-permute-start | bytes 1769480 | tf_op jit(solution)/shard_map/ppermute | solution.py:46
  119.9 13.4 %collective-permute-start.27 = (bf16[2,128,512]{2,1,0:T(8,128)(2,1)S(1)}, bf16[2,128,512]{2,1,0:T(8,128)(2,1)S(1)}, u32[]{:S(2)}, u32[]{:S(2)}) collective-permute-start(bf16[2,128,512]{2,1,0:T(8,128)(2,1)S(1)} %get-tuple-element.225), channel_id=1, source_target_pairs={{0,2},{1,3},{2,0},{3,1},{4,6},{5,7},{6,4},{7,5},{8,10},{9,11},{10,... | collective-permute-start | bytes 786440 | tf_op jit(solution)/shard_map/ppermute | solution.py:46
  120.0 15.0 %collective-permute-start.29 = (bf16[2,128,512]{2,1,0:T(8,128)(2,1)S(1)}, bf16[2,128,512]{2,1,0:T(8,128)(2,1)S(1)}, u32[]{:S(2)}, u32[]{:S(2)}) collective-permute-start(bf16[2,128,512]{2,1,0:T(8,128)(2,1)S(1)} %get-tuple-element.229), channel_id=1, source_target_pairs={{0,4},{1,5},{2,6},{3,7},{4,0},{5,1},{6,2},{7,3},{8,12},{9,13},{10,... | collective-permute-start | bytes 786440 | tf_op jit(solution)/shard_map/ppermute | solution.py:46
  148.5 9.1 %collective-permute-start.36 = (bf16[2,2,2,2,112,512]{5,4,3,2,1,0:T(8,128)(2,1)S(1)}, bf16[2,2,2,2,112,512]{5,4,3,2,1,0:T(8,128)(2,1)S(1)}, u32[]{:S(2)}, u32[]{:S(2)}) collective-permute-start(bf16[2,2,2,2,112,512]{5,4,3,2,1,0:T(8,128)(2,1)S(1)} %bitcast.75), channel_id=1, source_target_pairs={{0,1},{1,0},{2,3},{3,2},{4,5},{5,4},{6,7},{7,6},{8,9},{9,8},{10,11... | collective-permute-start | bytes 5505032 | tf_op jit(solution)/shard_map/ppermute | solution.py:46
  158.4 16.7 %collective-permute-start.38 = (bf16[2,2,2,80,512]{4,3,2,1,0:T(8,128)(2,1)S(1)}, bf16[2,2,2,80,512]{4,3,2,1,0:T(8,128)(2,1)S(1)}, u32[]{:S(2)}, u32[]{:S(2)}) collective-permute-start(bf16[2,2,2,80,512]{4,3,2,1,0:T(8,128)(2,1)S(1)} %get-tuple-element.266), channel_id=1, source_target_pairs={{0,16},{1,17},{2,18},{3,19},{4,20},{5,21},{6,22},{7,23},{8,24},{9,... | collective-permute-start | bytes 1966088 | tf_op jit(solution)/shard_map/ppermute | solution.py:46
  160.3 9.2 %collective-permute-start.39 = (bf16[2,2,2,32,512]{4,3,2,1,0:T(8,128)(2,1)S(1)}, bf16[2,2,2,32,512]{4,3,2,1,0:T(8,128)(2,1)S(1)}, u32[]{:S(2)}, u32[]{:S(2)}) collective-permute-start(bf16[2,2,2,32,512]{4,3,2,1,0:T(8,128)(2,1)S(1)} %get-tuple-element.269), channel_id=1, source_target_pairs={{0,8},{1,9},{2,10},{3,11},{4,12},{5,13},{6,14},{7,15},{8,0},{9,1},... | collective-permute-start | bytes 786440 | tf_op jit(solution)/shard_map/ppermute | solution.py:46
  162.3 16.2 %collective-permute-start.41 = (bf16[2,2,2,48,512]{4,3,2,1,0:T(8,128)(2,1)S(1)}, bf16[2,2,2,48,512]{4,3,2,1,0:T(8,128)(2,1)S(1)}, u32[]{:S(2)}, u32[]{:S(2)}) collective-permute-start(bf16[2,2,2,48,512]{4,3,2,1,0:T(8,128)(2,1)S(1)} %get-tuple-element.274), channel_id=1, source_target_pairs={{0,8},{1,9},{2,10},{3,11},{4,12},{5,13},{6,14},{7,15},{8,0},{9,1},... | collective-permute-start | bytes 1179656 | tf_op jit(solution)/shard_map/ppermute | solution.py:46
  175.7 8.8 %collective-permute-start.45 = (bf16[144,512]{1,0:T(8,128)(2,1)S(1)}, bf16[144,512]{1,0:T(8,128)(2,1)S(1)}, u32[]{:S(2)}, u32[]{:S(2)}) collective-permute-start(bf16[144,512]{1,0:T(8,128)(2,1)S(1)} %get-tuple-element.286), channel_id=1, source_target_pairs={{0,4},{1,5},{2,6},{3,7},{4,0},{5,1},{6,2},{7,3},{8,12},{9,13},{10,... | collective-permute-start | bytes 442376 | tf_op jit(solution)/shard_map/ppermute | solution.py:46
  (32 other events, 242.9 us)

commit v4 on v3

--- a/solution.py
+++ b/solution.py
@@ -500,6 +500,7 @@
     lower = iota((each, PAIR), 1) < HEAD_DIM
     lane = iota((2 * each, 128), 1)
     found = jnp.zeros((2 * each, 128), F32)
+    ones = jnp.ones((slots, PAIR), BF16)
     for m in range(micro):
         rows = slice(each * m, each * (m + 1))
         place = info[m, 4] + iota((each, 1), 0)
@@ -520,10 +521,12 @@
             top = jnp.maximum(jnp.max(scores, axis=1, keepdims=True), own)
             expos = jnp.exp(scores - top)
             own = jnp.exp(own - top)
-            total = jnp.sum(expos, axis=1, keepdims=True) + own
+            beside = jnp.concatenate([memory_value, ones], axis=1)
+            mixed = dot(expos.astype(BF16), beside)
+            total = mixed[:, PAIR:] + own
             inverse = 1.0 / total
-            mixed = dot(expos.astype(BF16), memory_value) * inverse
-            weight = jnp.broadcast_to(own * inverse, mixed.shape)
+            weight = own * inverse
+            mixed = mixed[:, :PAIR] * inverse
             attended[rows, cols] = merged(mixed, lower) + merged(weight, lower) * value
             found = jnp.where(lane == m * pairs + pair, top + jnp.log(total), found)
     stats[...] = found

time: 205 us -> 205 us (level)
  no operation moved by 1% of the time
where the time goes in v4:
time: 205 us; the launch traced here: 204 us
  waiting for transfers between devices  90.8 us (44%)
  starting transfers between devices  55.5 us (27%)
  Pallas kernels  47.5 us (23%)
  local copies, waits for them, and re-layouts  7.22 us (4%)
  other arithmetic  2.39 us (1%)
    ppermute x48, waiting for transfers between devices, swap(): lax.ppermute(array, AXES, [(i, i ^ mask) for i in range(device_count())])  87.6 us
    ppermute x48, starting transfers between devices, swap(): lax.ppermute(array, AXES, [(i, i ^ mask) for i in range(device_count())])  52.8 us
    pallas_call x35, Pallas kernels, kernel(): pl.pallas_call(body, in_specs=[pl.BlockSpec(memory_space=spec.get(a.dtype...  45.6 us
  transfers between devices with their start and end apart: 50, of which 34 were waited for; matrix products, arithmetic and copies ran while one was open for 2% of the time, Pallas kernels for 14%

profile of v4, /device:TPU:0, one launch (start us, length us, event | category | flops | bytes accessed | tf_op | source)
XLA Modules:
  0.0 204.5 jit_solution(231131719707509849)
XLA Ops:
  4.0 4.1 %collective-permute-start = (bf16[80,512]{1,0:T(8,128)(2,1)}, bf16[80,512]{1,0:T(8,128)(2,1)S(1)}, u32[]{:S(2)}, u32[]{:S(2)}) collective-permute-start(bf16[80,512]{1,0:T(8,128)(2,1)} %get-tuple-element.158.refs_0_), channel_id=1, source_target_pairs={{0,4},{1,5},{2,6},{3,7},{4,0},{5,1},{6,2},{7,3},{8,12},{9,13},{10,... | collective-permute-start | bytes 245768 | tf_op jit(solution)/shard_map/ppermute | solution.py:46
  9.7 2.3 %collective-permute-done.refs_1_ = bf16[80,512]{1,0:T(8,128)(2,1)S(1)} collective-permute-done((bf16[80,512]{1,0:T(8,128)(2,1)}, bf16[80,512]{1,0:T(8,128)(2,1)S(1)}, u32[]{:S(2)}, u32[]{:S(2)}) %collective-permute-start) | collective-permute-done | bytes 81952 | tf_op jit(solution)/shard_map/ppermute | solution.py:46
  16.3 3.3 %collective-permute-start.4 = (bf16[2,80,512]{2,1,0:T(8,128)(2,1)S(1)}, bf16[2,80,512]{2,1,0:T(8,128)(2,1)S(1)}, u32[]{:S(2)}, u32[]{:S(2)}) collective-permute-start(bf16[2,80,512]{2,1,0:T(8,128)(2,1)S(1)} %shard_map.290.refs_0_), channel_id=1, source_target_pairs={{0,4},{1,5},{2,6},{3,7},{4,0},{5,1},{6,2},{7,3},{8,12},{9,13},{10,... | collective-permute-start | bytes 491528 | tf_op jit(solution)/shard_map/ppermute | solution.py:46
  24.6 2.5 %collective-permute-done.4.refs_1_ = bf16[2,80,512]{2,1,0:T(8,128)(2,1)S(1)} collective-permute-done((bf16[2,80,512]{2,1,0:T(8,128)(2,1)S(1)}, bf16[2,80,512]{2,1,0:T(8,128)(2,1)S(1)}, u32[]{:S(2)}, u32[]{:S(2)}) %collective-permute-start.4) | collective-permute-done | bytes 163872 | tf_op jit(solution)/shard_map/ppermute | solution.py:46
  29.2 2.9 %collective-permute-start.7 = (bf16[144,512]{1,0:T(8,128)(2,1)}, bf16[144,512]{1,0:T(8,128)(2,1)S(1)}, u32[]{:S(2)}, u32[]{:S(2)}) collective-permute-start(bf16[144,512]{1,0:T(8,128)(2,1)} %get-tuple-element.167.refs_2_), channel_id=1, source_target_pairs={{0,4},{1,5},{2,6},{3,7},{4,0},{5,1},{6,2},{7,3},{8,12},{9,13},{10,... | collective-permute-start | bytes 442376 | tf_op jit(solution)/shard_map/ppermute | solution.py:46
  35.7 2.4 %collective-permute-done.7.refs_3_ = bf16[144,512]{1,0:T(8,128)(2,1)S(1)} collective-permute-done((bf16[144,512]{1,0:T(8,128)(2,1)}, bf16[144,512]{1,0:T(8,128)(2,1)S(1)}, u32[]{:S(2)}, u32[]{:S(2)}) %collective-permute-start.7) | collective-permute-done | bytes 147488 | tf_op jit(solution)/shard_map/ppermute | solution.py:46
  41.0 9.8 %collective-permute-done.8.refs_1_ = bf16[2,2,2,80,512]{4,3,2,1,0:T(8,128)(2,1)S(1)} collective-permute-done((bf16[2,2,2,80,512]{4,3,2,1,0:T(8,128)(2,1)S(1)}, bf16[2,2,2,80,512]{4,3,2,1,0:T(8,128)(2,1)S(1)}, u32[]{:S(2)}, u32[]{:S(2)}) %collective-permute-start.8) | collective-permute-done | bytes 655392 | tf_op jit(solution)/shard_map/ppermute | solution.py:46
  51.5 3.4 %collective-permute-done.9.refs_1_ = bf16[2,2,2,80,512]{4,3,2,1,0:T(8,128)(2,1)S(1)} collective-permute-done((bf16[2,2,2,80,512]{4,3,2,1,0:T(8,128)(2,1)S(1)}, bf16[2,2,2,80,512]{4,3,2,1,0:T(8,128)(2,1)S(1)}, u32[]{:S(2)}, u32[]{:S(2)}) %collective-permute-start.9) | collective-permute-done | bytes 655392 | tf_op jit(solution)/shard_map/ppermute | solution.py:46
  66.6 2.7 %collective-permute-done.13.refs_1_ = bf16[128,512]{1,0:T(8,128)(2,1)S(1)} collective-permute-done((bf16[128,512]{1,0:T(8,128)(2,1)S(1)}, bf16[128,512]{1,0:T(8,128)(2,1)S(1)}, u32[]{:S(2)}, u32[]{:S(2)}) %collective-permute-start.13) | collective-permute-done | bytes 131104 | tf_op jit(solution)/shard_map/ppermute | solution.py:46
  73.4 2.4 %collective-permute-start.17 = (bf16[2,128,512]{2,1,0:T(8,128)(2,1)S(1)}, bf16[2,128,512]{2,1,0:T(8,128)(2,1)S(1)}, u32[]{:S(2)}, u32[]{:S(2)}) collective-permute-start(bf16[2,128,512]{2,1,0:T(8,128)(2,1)S(1)} %get-tuple-element.188.refs_0_), channel_id=1, source_target_pairs={{0,2},{1,3},{2,0},{3,1},{4,6},{5,7},{6,4},{7,5},{8,10},{9,11},{10,... | collective-permute-start | bytes 786440 | tf_op jit(solution)/shard_map/ppermute | solution.py:46
  75.8 11.0 %collective-permute-done.18.refs_3_ = bf16[2,128,512]{2,1,0:T(8,128)(2,1)S(1)} collective-permute-done((bf16[2,128,512]{2,1,0:T(8,128)(2,1)S(1)}, bf16[2,128,512]{2,1,0:T(8,128)(2,1)S(1)}, u32[]{:S(2)}, u32[]{:S(2)}) %collective-permute-start.18) | collective-permute-done | bytes 262176 | tf_op jit(solution)/shard_map/ppermute | solution.py:46
  88.6 4.7 %collective-permute-done.21.refs_1_ = bf16[2,2,128,512]{3,2,1,0:T(8,128)(2,1)S(1)} collective-permute-done((bf16[2,2,128,512]{3,2,1,0:T(8,128)(2,1)S(1)}, bf16[2,2,128,512]{3,2,1,0:T(8,128)(2,1)S(1)}, u32[]{:S(2)}, u32[]{:S(2)}) %collective-permute-start.21) | collective-permute-done | bytes 524320 | tf_op jit(solution)/shard_map/ppermute | solution.py:46
  94.7 3.4 %shard_map.305 = (f32[384,512]{1,0:T(8,128)S(1)}, f32[384,128]{1,0:T(8,128)S(1)}) custom-call(s32[2,7]{1,0:T(2,128)S(1)} %stack.47.info, bf16[384,512]{1,0:T(8,128)(2,1)S(1)} %get-tuple-element.210.query, bf16[384,512]{1,0:T(8,128)(2,1)S(1)} %get-tuple-element.202.keys, bf16[384,512]{1,0:T(8,128)(2,1)S(1)} %get-tuple-element.203.values, ...), custom_call_target="tpu_custom_call" | custom-call | flops 805306368 | bytes 3276856 | tf_op jit(solution)/shard_map/pallas_call | solution.py:342
  99.1 9.7 %shard_map.307 = (bf16[384,512]{1,0:T(8,128)(2,1)}, f32[384,512]{1,0:T(8,128)S(1)}, bf16[384,512]{1,0:T(8,128)(2,1)S(1)}, bf16[16,144,512]{2,1,0:T(8,128)(2,1)S(...) custom-call(s32[2,7]{1,0:T(2,128)S(1)} %stack.47.info, bf16[384,512]{1,0:T(8,128)(2,1)S(1)} %bitcast.68, ...), custom_call_target="tpu_custom_call" | custom-call | flops 5435817984 | bytes 6324280 | tf_op jit(solution)/shard_map/pallas_call | solution.py:342
  109.0 5.6 %shard_map.308 = (bf16[384,512]{1,0:T(8,128)(2,1)S(1)}, bf16[4,128,512]{2,1,0:T(8,128)(2,1)S(1)}, bf16[4,128,512]{2,1,0:T(8,128)(2,1)S(1)}, bf16[4,128,512]{2,1,...) custom-call(s32[2,7]{1,0:T(2,128)S(1)} %stack.47.info, ...), custom_call_target="tpu_custom_call" | custom-call | flops 2013265920 | bytes 4653112 | tf_op jit(solution)/shard_map/pallas_call | solution.py:342
  119.6 3.3 %collective-permute-start.29 = (bf16[2,128,512]{2,1,0:T(8,128)(2,1)S(1)}, bf16[2,128,512]{2,1,0:T(8,128)(2,1)S(1)}, u32[]{:S(2)}, u32[]{:S(2)}) collective-permute-start(bf16[2,128,512]{2,1,0:T(8,128)(2,1)S(1)} %get-tuple-element.229), channel_id=1, source_target_pairs={{0,4},{1,5},{2,6},{3,7},{4,0},{5,1},{6,2},{7,3},{8,12},{9,13},{10,... | collective-permute-start | bytes 786440 | tf_op jit(solution)/shard_map/ppermute | solution.py:46
  122.9 10.0 %collective-permute-done.27.refs_1_ = bf16[2,128,512]{2,1,0:T(8,128)(2,1)S(1)} collective-permute-done((bf16[2,128,512]{2,1,0:T(8,128)(2,1)S(1)}, bf16[2,128,512]{2,1,0:T(8,128)(2,1)S(1)}, u32[]{:S(2)}, u32[]{:S(2)}) %collective-permute-start.27) | collective-permute-done | bytes 262176 | tf_op jit(solution)/shard_map/ppermute | solution.py:46
  145.4 2.7 %shard_map.314 = (f32[384,512]{1,0:T(8,128)S(1)}, f32[384,512]{1,0:T(8,128)S(1)}, f32[16,1024]{1,0:T(8,128)S(1)}, bf16[16,112,512]{2,1,0:T(8,128)(2,1)S(1)}, bf16[16,112,512]{2,1,0:T(8,128)(2,1)S(1)}) custom-call(s32[2,7]{1,0:T(2,128)S(1)} %stack.47.info, bf16[128,512]{1,0:T(8,128)(2,1)S(1)} %add_convert_fusion.1.key_memory, ...), custom_call_target="tpu_custom_call" | custom-call | flops 1006632960 | bytes 7094328 | tf_op jit(solution)/shard_map/pallas_call | solution.py:342
  149.7 2.3 %collective-permute-done.35.rims = f32[16,1024]{1,0:T(8,128)S(1)} collective-permute-done((f32[16,1024]{1,0:T(8,128)S(1)}, f32[16,1024]{1,0:T(8,128)S(1)}, u32[]{:S(2)}, u32[]{:S(2)}) %collective-permute-start.35) | collective-permute-done | bytes 65568 | tf_op jit(solution)/shard_map/ppermute | solution.py:1099
  152.1 2.9 %shard_map.315 = (bf16[384,512]{1,0:T(8,128)(2,1)}, bf16[16,48,512]{2,1,0:T(8,128)(2,1)S(1)}, bf16[16,48,512]{2,1,0:T(8,128)(2,1)S(1)}) custom-call(s32[2,7]{1,0:T(2,128)S(1)} %stack.47.info, bf16[384,512]{1,0:T(8,128)(2,1)S(1)} %bitcast.69, bf16[400,512]{1,0:T(8,128)(2,1)S(1)} %get-tuple-element.178.normed, ...), custom_call_target="tpu_custom_call" | custom-call | flops 1207959552 | bytes 10502200 | tf_op jit(solution)/shard_map/pallas_call | solution.py:342
  162.7 5.5 %collective-permute-done.40.refs_5_ = bf16[2,144,512]{2,1,0:T(8,128)(2,1)S(1)} collective-permute-done((bf16[2,144,512]{2,1,0:T(8,128)(2,1)S(1)}, bf16[2,144,512]{2,1,0:T(8,128)(2,1)S(1)}, u32[]{:S(2)}, u32[]{:S(2)}) %collective-permute-start.40) | collective-permute-done | bytes 294944 | tf_op jit(solution)/shard_map/ppermute | solution.py:46
  169.2 5.5 %collective-permute-done.38.refs_1_ = bf16[2,2,2,80,512]{4,3,2,1,0:T(8,128)(2,1)S(1)} collective-permute-done((bf16[2,2,2,80,512]{4,3,2,1,0:T(8,128)(2,1)S(1)}, bf16[2,2,2,80,512]{4,3,2,1,0:T(8,128)(2,1)S(1)}, u32[]{:S(2)}, u32[]{:S(2)}) %collective-permute-start.38) | collective-permute-done | bytes 655392 | tf_op jit(solution)/shard_map/ppermute | solution.py:46
  180.8 3.3 %collective-permute-done.45 = bf16[144,512]{1,0:T(8,128)(2,1)S(1)} collective-permute-done((bf16[144,512]{1,0:T(8,128)(2,1)S(1)}, bf16[144,512]{1,0:T(8,128)(2,1)S(1)}, u32[]{:S(2)}, u32[]{:S(2)}) %collective-permute-start.45) | collective-permute-done | bytes 147488 | tf_op jit(solution)/shard_map/ppermute | solution.py:46
  190.4 3.9 %collective-permute-done.46.refs_1_ = bf16[2,112,512]{2,1,0:T(8,128)(2,1)S(1)} collective-permute-done((bf16[2,112,512]{2,1,0:T(8,128)(2,1)S(1)}, bf16[2,112,512]{2,1,0:T(8,128)(2,1)S(1)}, u32[]{:S(2)}, u32[]{:S(2)}) %collective-permute-start.46) | collective-permute-done | bytes 229408 | tf_op jit(solution)/shard_map/ppermute | solution.py:46
  (145 shorter events, 93.6 us)
Async XLA Ops:
  13.5 9.0 %collective-permute-start.3 = (bf16[2,80,512]{2,1,0:T(8,128)(2,1)S(1)}, bf16[2,80,512]{2,1,0:T(8,128)(2,1)S(1)}, u32[]{:S(2)}, u32[]{:S(2)}) collective-permute-start(bf16[2,80,512]{2,1,0:T(8,128)(2,1)S(1)} %shard_map.289.refs_0_), channel_id=1, source_target_pairs={{0,2},{1,3},{2,0},{3,1},{4,6},{5,7},{6,4},{7,5},{8,10},{9,11},{10,... | collective-permute-start | bytes 491528 | tf_op jit(solution)/shard_map/ppermute | solution.py:46
  16.3 10.8 %collective-permute-start.4 = (bf16[2,80,512]{2,1,0:T(8,128)(2,1)S(1)}, bf16[2,80,512]{2,1,0:T(8,128)(2,1)S(1)}, u32[]{:S(2)}, u32[]{:S(2)}) collective-permute-start(bf16[2,80,512]{2,1,0:T(8,128)(2,1)S(1)} %shard_map.290.refs_0_), channel_id=1, source_target_pairs={{0,4},{1,5},{2,6},{3,7},{4,0},{5,1},{6,2},{7,3},{8,12},{9,13},{10,... | collective-permute-start | bytes 491528 | tf_op jit(solution)/shard_map/ppermute | solution.py:46
  23.0 10.5 %collective-permute-start.5 = (bf16[2,2,80,512]{3,2,1,0:T(8,128)(2,1)S(1)}, bf16[2,2,80,512]{3,2,1,0:T(8,128)(2,1)S(1)}, u32[]{:S(2)}, u32[]{:S(2)}) collective-permute-start(bf16[2,2,80,512]{3,2,1,0:T(8,128)(2,1)S(1)} %shard_map.291.refs_0_), channel_id=1, source_target_pairs={{0,8},{1,9},{2,10},{3,11},{4,12},{5,13},{6,14},{7,15},{8,0},{9,1},... | collective-permute-start | bytes 983048 | tf_op jit(solution)/shard_map/ppermute | solution.py:46
  27.6 10.4 %collective-permute-start.6 = (bf16[2,2,80,512]{3,2,1,0:T(8,128)(2,1)S(1)}, bf16[2,2,80,512]{3,2,1,0:T(8,128)(2,1)S(1)}, u32[]{:S(2)}, u32[]{:S(2)}) collective-permute-start(bf16[2,2,80,512]{3,2,1,0:T(8,128)(2,1)S(1)} %shard_map.292.refs_0_), channel_id=1, source_target_pairs={{0,16},{1,17},{2,18},{3,19},{4,20},{5,21},{6,22},{7,23},{8,24},{9,... | collective-permute-start | bytes 983048 | tf_op jit(solution)/shard_map/ppermute | solution.py:46
  29.2 8.8 %collective-permute-start.7 = (bf16[144,512]{1,0:T(8,128)(2,1)}, bf16[144,512]{1,0:T(8,128)(2,1)S(1)}, u32[]{:S(2)}, u32[]{:S(2)}) collective-permute-start(bf16[144,512]{1,0:T(8,128)(2,1)} %get-tuple-element.167.refs_2_), channel_id=1, source_target_pairs={{0,4},{1,5},{2,6},{3,7},{4,0},{5,1},{6,2},{7,3},{8,12},{9,13},{10,... | collective-permute-start | bytes 442376 | tf_op jit(solution)/shard_map/ppermute | solution.py:46
  34.1 16.6 %collective-permute-start.8 = (bf16[2,2,2,80,512]{4,3,2,1,0:T(8,128)(2,1)S(1)}, bf16[2,2,2,80,512]{4,3,2,1,0:T(8,128)(2,1)S(1)}, u32[]{:S(2)}, u32[]{:S(2)}) collective-permute-start(bf16[2,2,2,80,512]{4,3,2,1,0:T(8,128)(2,1)S(1)} %shard_map.293.refs_0_), channel_id=1, source_target_pairs={{0,16},{1,17},{2,18},{3,19},{4,20},{5,21},{6,22},{7,23},{8,24},{9,... | collective-permute-start | bytes 1966088 | tf_op jit(solution)/shard_map/ppermute | solution.py:46
  38.7 16.2 %collective-permute-start.9 = (bf16[2,2,2,80,512]{4,3,2,1,0:T(8,128)(2,1)S(1)}, bf16[2,2,2,80,512]{4,3,2,1,0:T(8,128)(2,1)S(1)}, u32[]{:S(2)}, u32[]{:S(2)}) collective-permute-start(bf16[2,2,2,80,512]{4,3,2,1,0:T(8,128)(2,1)S(1)} %get-tuple-element.171.refs_0_), channel_id=1, source_target_pairs={{0,8},{1,9},{2,10},{3,11},{4,12},{5,13},{6,14},{7,15},{8,0},{9,1},... | collective-permute-start | bytes 1966088 | tf_op jit(solution)/shard_map/ppermute | solution.py:46
  40.2 11.2 %collective-permute-start.10 = (bf16[2,144,512]{2,1,0:T(8,128)(2,1)S(1)}, bf16[2,144,512]{2,1,0:T(8,128)(2,1)S(1)}, u32[]{:S(2)}, u32[]{:S(2)}) collective-permute-start(bf16[2,144,512]{2,1,0:T(8,128)(2,1)S(1)} %get-tuple-element.173.refs_2_), channel_id=1, source_target_pairs={{0,2},{1,3},{2,0},{3,1},{4,6},{5,7},{6,4},{7,5},{8,10},{9,11},{10,... | collective-permute-start | bytes 884744 | tf_op jit(solution)/shard_map/ppermute | solution.py:46
  55.7 9.4 %collective-permute-start.15 = (bf16[2,2,144,256]{3,2,1,0:T(8,128)(2,1)S(1)}, bf16[2,2,144,256]{3,2,1,0:T(8,128)(2,1)S(1)}, u32[]{:S(2)}, u32[]{:S(2)}) collective-permute-start(bf16[2,2,144,256]{3,2,1,0:T(8,128)(2,1)S(1)} %get-tuple-element.184.refs_4_), channel_id=1, source_target_pairs={{0,8},{1,9},{2,10},{3,11},{4,12},{5,13},{6,14},{7,15},{8,0},{9,1},... | collective-permute-start | bytes 884744 | tf_op jit(solution)/shard_map/ppermute | solution.py:46
  57.5 9.1 %collective-permute-start.16 = (bf16[2,2,144,256]{3,2,1,0:T(8,128)(2,1)S(1)}, bf16[2,2,144,256]{3,2,1,0:T(8,128)(2,1)S(1)}, u32[]{:S(2)}, u32[]{:S(2)}) collective-permute-start(bf16[2,2,144,256]{3,2,1,0:T(8,128)(2,1)S(1)} %get-tuple-element.186.refs_6_), channel_id=1, source_target_pairs={{0,16},{1,17},{2,18},{3,19},{4,20},{5,21},{6,22},{7,23},{8,24},{9,... | collective-permute-start | bytes 884744 | tf_op jit(solution)/shard_map/ppermute | solution.py:46
  71.6 15.2 %collective-permute-start.19 = (bf16[2,2,2,144,256]{4,3,2,1,0:T(8,128)(2,1)S(1)}, bf16[2,2,2,144,256]{4,3,2,1,0:T(8,128)(2,1)S(1)}, u32[]{:S(2)}, u32[]{:S(2)}) collective-permute-start(bf16[2,2,2,144,256]{4,3,2,1,0:T(8,128)(2,1)S(1)} %get-tuple-element.192.refs_4_), channel_id=1, source_target_pairs={{0,16},{1,17},{2,18},{3,19},{4,20},{5,21},{6,22},{7,23},{8,24},{9,... | collective-permute-start | bytes 1769480 | tf_op jit(solution)/shard_map/ppermute | solution.py:46
  73.2 14.0 %collective-permute-start.20 = (bf16[2,2,2,144,256]{4,3,2,1,0:T(8,128)(2,1)S(1)}, bf16[2,2,2,144,256]{4,3,2,1,0:T(8,128)(2,1)S(1)}, u32[]{:S(2)}, u32[]{:S(2)}) collective-permute-start(bf16[2,2,2,144,256]{4,3,2,1,0:T(8,128)(2,1)S(1)} %get-tuple-element.194.refs_6_), channel_id=1, source_target_pairs={{0,8},{1,9},{2,10},{3,11},{4,12},{5,13},{6,14},{7,15},{8,0},{9,1},... | collective-permute-start | bytes 1769480 | tf_op jit(solution)/shard_map/ppermute | solution.py:46
  73.4 13.3 %collective-permute-start.18 = (bf16[2,128,512]{2,1,0:T(8,128)(2,1)S(1)}, bf16[2,128,512]{2,1,0:T(8,128)(2,1)S(1)}, u32[]{:S(2)}, u32[]{:S(2)}) collective-permute-start(bf16[2,128,512]{2,1,0:T(8,128)(2,1)S(1)} %get-tuple-element.190.refs_2_), channel_id=1, source_target_pairs={{0,4},{1,5},{2,6},{3,7},{4,0},{5,1},{6,2},{7,3},{8,12},{9,13},{10,... | collective-permute-start | bytes 786440 | tf_op jit(solution)/shard_map/ppermute | solution.py:46
  73.4 13.4 %collective-permute-start.17 = (bf16[2,128,512]{2,1,0:T(8,128)(2,1)S(1)}, bf16[2,128,512]{2,1,0:T(8,128)(2,1)S(1)}, u32[]{:S(2)}, u32[]{:S(2)}) collective-permute-start(bf16[2,128,512]{2,1,0:T(8,128)(2,1)S(1)} %get-tuple-element.188.refs_0_), channel_id=1, source_target_pairs={{0,2},{1,3},{2,0},{3,1},{4,6},{5,7},{6,4},{7,5},{8,10},{9,11},{10,... | collective-permute-start | bytes 786440 | tf_op jit(solution)/shard_map/ppermute | solution.py:46
  88.0 10.2 %collective-permute-start.23 = (bf16[2,2,2,2,144,512]{5,4,3,2,1,0:T(8,128)(2,1)S(1)}, bf16[2,2,2,2,144,512]{5,4,3,2,1,0:T(8,128)(2,1)S(1)}, u32[]{:S(2)}, u32[]{:S(2)}) collective-permute-start(bf16[2,2,2,2,144,512]{5,4,3,2,1,0:T(8,128)(2,1)S(1)} %get-tuple-element.205.refs_0_), channel_id=1, source_target_pairs={{0,1},{1,0},{2,3},{3,2},{4,5},{5,4},{6,7},{7,6},{8,9},{9,8},{10,11... | collective-permute-start | bytes 7077896 | tf_op jit(solution)/shard_map/ppermute | solution.py:46
  118.3 16.3 %collective-permute-start.30 = (bf16[2,2,2,144,256]{4,3,2,1,0:T(8,128)(2,1)S(1)}, bf16[2,2,2,144,256]{4,3,2,1,0:T(8,128)(2,1)S(1)}, u32[]{:S(2)}, u32[]{:S(2)}) collective-permute-start(bf16[2,2,2,144,256]{4,3,2,1,0:T(8,128)(2,1)S(1)} %get-tuple-element.232), channel_id=1, source_target_pairs={{0,16},{1,17},{2,18},{3,19},{4,20},{5,21},{6,22},{7,23},{8,24},{9,... | collective-permute-start | bytes 1769480 | tf_op jit(solution)/shard_map/ppermute | solution.py:46
  118.9 15.6 %collective-permute-start.31 = (bf16[2,2,2,144,256]{4,3,2,1,0:T(8,128)(2,1)S(1)}, bf16[2,2,2,144,256]{4,3,2,1,0:T(8,128)(2,1)S(1)}, u32[]{:S(2)}, u32[]{:S(2)}) collective-permute-start(bf16[2,2,2,144,256]{4,3,2,1,0:T(8,128)(2,1)S(1)} %get-tuple-element.235), channel_id=1, source_target_pairs={{0,8},{1,9},{2,10},{3,11},{4,12},{5,13},{6,14},{7,15},{8,0},{9,1},... | collective-permute-start | bytes 1769480 | tf_op jit(solution)/shard_map/ppermute | solution.py:46
  119.5 13.4 %collective-permute-start.27 = (bf16[2,128,512]{2,1,0:T(8,128)(2,1)S(1)}, bf16[2,128,512]{2,1,0:T(8,128)(2,1)S(1)}, u32[]{:S(2)}, u32[]{:S(2)}) collective-permute-start(bf16[2,128,512]{2,1,0:T(8,128)(2,1)S(1)} %get-tuple-element.225), channel_id=1, source_target_pairs={{0,2},{1,3},{2,0},{3,1},{4,6},{5,7},{6,4},{7,5},{8,10},{9,11},{10,... | collective-permute-start | bytes 786440 | tf_op jit(solution)/shard_map/ppermute | solution.py:46
  119.6 14.9 %collective-permute-start.29 = (bf16[2,128,512]{2,1,0:T(8,128)(2,1)S(1)}, bf16[2,128,512]{2,1,0:T(8,128)(2,1)S(1)}, u32[]{:S(2)}, u32[]{:S(2)}) collective-permute-start(bf16[2,128,512]{2,1,0:T(8,128)(2,1)S(1)} %get-tuple-element.229), channel_id=1, source_target_pairs={{0,4},{1,5},{2,6},{3,7},{4,0},{5,1},{6,2},{7,3},{8,12},{9,13},{10,... | collective-permute-start | bytes 786440 | tf_op jit(solution)/shard_map/ppermute | solution.py:46
  148.1 9.1 %collective-permute-start.36 = (bf16[2,2,2,2,112,512]{5,4,3,2,1,0:T(8,128)(2,1)S(1)}, bf16[2,2,2,2,112,512]{5,4,3,2,1,0:T(8,128)(2,1)S(1)}, u32[]{:S(2)}, u32[]{:S(2)}) collective-permute-start(bf16[2,2,2,2,112,512]{5,4,3,2,1,0:T(8,128)(2,1)S(1)} %bitcast.75), channel_id=1, source_target_pairs={{0,1},{1,0},{2,3},{3,2},{4,5},{5,4},{6,7},{7,6},{8,9},{9,8},{10,11... | collective-permute-start | bytes 5505032 | tf_op jit(solution)/shard_map/ppermute | solution.py:46
  157.9 16.7 %collective-permute-start.38 = (bf16[2,2,2,80,512]{4,3,2,1,0:T(8,128)(2,1)S(1)}, bf16[2,2,2,80,512]{4,3,2,1,0:T(8,128)(2,1)S(1)}, u32[]{:S(2)}, u32[]{:S(2)}) collective-permute-start(bf16[2,2,2,80,512]{4,3,2,1,0:T(8,128)(2,1)S(1)} %get-tuple-element.266), channel_id=1, source_target_pairs={{0,16},{1,17},{2,18},{3,19},{4,20},{5,21},{6,22},{7,23},{8,24},{9,... | collective-permute-start | bytes 1966088 | tf_op jit(solution)/shard_map/ppermute | solution.py:46
  159.9 9.2 %collective-permute-start.39 = (bf16[2,2,2,32,512]{4,3,2,1,0:T(8,128)(2,1)S(1)}, bf16[2,2,2,32,512]{4,3,2,1,0:T(8,128)(2,1)S(1)}, u32[]{:S(2)}, u32[]{:S(2)}) collective-permute-start(bf16[2,2,2,32,512]{4,3,2,1,0:T(8,128)(2,1)S(1)} %get-tuple-element.269), channel_id=1, source_target_pairs={{0,8},{1,9},{2,10},{3,11},{4,12},{5,13},{6,14},{7,15},{8,0},{9,1},... | collective-permute-start | bytes 786440 | tf_op jit(solution)/shard_map/ppermute | solution.py:46
  161.9 16.2 %collective-permute-start.41 = (bf16[2,2,2,48,512]{4,3,2,1,0:T(8,128)(2,1)S(1)}, bf16[2,2,2,48,512]{4,3,2,1,0:T(8,128)(2,1)S(1)}, u32[]{:S(2)}, u32[]{:S(2)}) collective-permute-start(bf16[2,2,2,48,512]{4,3,2,1,0:T(8,128)(2,1)S(1)} %get-tuple-element.274), channel_id=1, source_target_pairs={{0,8},{1,9},{2,10},{3,11},{4,12},{5,13},{6,14},{7,15},{8,0},{9,1},... | collective-permute-start | bytes 1179656 | tf_op jit(solution)/shard_map/ppermute | solution.py:46
  175.3 8.8 %collective-permute-start.45 = (bf16[144,512]{1,0:T(8,128)(2,1)S(1)}, bf16[144,512]{1,0:T(8,128)(2,1)S(1)}, u32[]{:S(2)}, u32[]{:S(2)}) collective-permute-start(bf16[144,512]{1,0:T(8,128)(2,1)S(1)} %get-tuple-element.286), channel_id=1, source_target_pairs={{0,4},{1,5},{2,6},{3,7},{4,0},{5,1},{6,2},{7,3},{8,12},{9,13},{10,... | collective-permute-start | bytes 442376 | tf_op jit(solution)/shard_map/ppermute | solution.py:46
  (32 other events, 242.9 us)

commit v5 on v4

--- a/solution.py
+++ b/solution.py
@@ -1056,22 +1056,16 @@
     keys_side.go(1)
     values_side.go(1)
     cross = [(across[-1 - at], across[at]) for at in range(len(across))]
-    keys_side.add((back[0],))
-    keys_side.go(back[0])
     cuts = (width // 2, width // 2)
-    add(order, (values_side, (along[0],), ()), (feeds, cross[0], cuts))
-    values_side.go(along[0])
-    feeds.go(*cross[0])
-    for at in range(1, max(len(along), len(cross))):
+    for at in range(max(len(along), len(cross))):
         jobs = []
         if at < len(along):
-            keys_side.add((back[at],))
-            keys_side.go(back[at])
-            jobs.append((values_side, (along[at],), ()))
+            jobs = [(keys_side, (back[at],), ()), (values_side, (along[at],), ())]
         if at < len(cross):
-            jobs.append((feeds, cross[at], ()))
+            jobs.append((feeds, cross[at], () if at else cuts))
         add(order, *jobs)
         if at < len(along):
+            keys_side.go(back[at])
             values_side.go(along[at])
         if at < len(cross):
             feeds.go(*cross[at])

time: 205 us -> 207 us (level)
  waiting for transfers between devices: 90.8 us -> 93.6 us
    ppermute x48, waiting for transfers between devices: 87.6 us -> 90.4 us  [swap(): lax.ppermute(array, AXES, [(i, i ^ mask) for i in range(device_count())])]
    pallas_call x35 -> x33, Pallas kernels: 45.6 us -> 44.5 us  [kernel(): pl.pallas_call(body, in_specs=[pl.BlockSpec(memory_space=spec.get(a.dtype...]
  transfers between devices with their start and end apart: 50 -> 50, of which waited for: 34 -> 31; matrix products, arithmetic and copies ran while one was open for 2% -> 2% of each run, Pallas kernels for 14% -> 13%
where the time goes in v5:
time: 207 us; the launch traced here: 206 us
  waiting for transfers between devices  93.6 us (45%)
  starting transfers between devices  55.9 us (27%)
  Pallas kernels  46.4 us (22%)
  local copies, waits for them, and re-layouts  7.22 us (3%)
  other arithmetic  2.39 us (1%)
    ppermute x48, waiting for transfers between devices, swap(): lax.ppermute(array, AXES, [(i, i ^ mask) for i in range(device_count())])  90.4 us
    ppermute x48, starting transfers between devices, swap(): lax.ppermute(array, AXES, [(i, i ^ mask) for i in range(device_count())])  53.1 us
    pallas_call x33, Pallas kernels, kernel(): pl.pallas_call(body, in_specs=[pl.BlockSpec(memory_space=spec.get(a.dtype...  44.5 us
  transfers between devices with their start and end apart: 50, of which 31 were waited for; matrix products, arithmetic and copies ran while one was open for 2% of the time, Pallas kernels for 13%

profile of v5, /device:TPU:0, one launch (start us, length us, event | category | flops | bytes accessed | tf_op | source)
XLA Modules:
  0.0 206.5 jit_solution(15422043717685843849)
XLA Ops:
  4.0 4.1 %collective-permute-start = (bf16[80,512]{1,0:T(8,128)(2,1)}, bf16[80,512]{1,0:T(8,128)(2,1)S(1)}, u32[]{:S(2)}, u32[]{:S(2)}) collective-permute-start(bf16[80,512]{1,0:T(8,128)(2,1)} %get-tuple-element.158.refs_0_), channel_id=1, source_target_pairs={{0,4},{1,5},{2,6},{3,7},{4,0},{5,1},{6,2},{7,3},{8,12},{9,13},{10,... | collective-permute-start | bytes 245768 | tf_op jit(solution)/shard_map/ppermute | solution.py:46
  16.3 3.3 %collective-permute-start.4 = (bf16[2,80,512]{2,1,0:T(8,128)(2,1)S(1)}, bf16[2,80,512]{2,1,0:T(8,128)(2,1)S(1)}, u32[]{:S(2)}, u32[]{:S(2)}) collective-permute-start(bf16[2,80,512]{2,1,0:T(8,128)(2,1)S(1)} %shard_map.290.refs_0_), channel_id=1, source_target_pairs={{0,4},{1,5},{2,6},{3,7},{4,0},{5,1},{6,2},{7,3},{8,12},{9,13},{10,... | collective-permute-start | bytes 491528 | tf_op jit(solution)/shard_map/ppermute | solution.py:46
  24.6 2.5 %collective-permute-done.4.refs_1_ = bf16[2,80,512]{2,1,0:T(8,128)(2,1)S(1)} collective-permute-done((bf16[2,80,512]{2,1,0:T(8,128)(2,1)S(1)}, bf16[2,80,512]{2,1,0:T(8,128)(2,1)S(1)}, u32[]{:S(2)}, u32[]{:S(2)}) %collective-permute-start.4) | collective-permute-done | bytes 163872 | tf_op jit(solution)/shard_map/ppermute | solution.py:46
  29.2 2.9 %collective-permute-start.7 = (bf16[144,512]{1,0:T(8,128)(2,1)}, bf16[144,512]{1,0:T(8,128)(2,1)S(1)}, u32[]{:S(2)}, u32[]{:S(2)}) collective-permute-start(bf16[144,512]{1,0:T(8,128)(2,1)} %get-tuple-element.167.refs_2_), channel_id=1, source_target_pairs={{0,4},{1,5},{2,6},{3,7},{4,0},{5,1},{6,2},{7,3},{8,12},{9,13},{10,... | collective-permute-start | bytes 442376 | tf_op jit(solution)/shard_map/ppermute | solution.py:46
  35.7 2.4 %collective-permute-done.7.refs_3_ = bf16[144,512]{1,0:T(8,128)(2,1)S(1)} collective-permute-done((bf16[144,512]{1,0:T(8,128)(2,1)}, bf16[144,512]{1,0:T(8,128)(2,1)S(1)}, u32[]{:S(2)}, u32[]{:S(2)}) %collective-permute-start.7) | collective-permute-done | bytes 147488 | tf_op jit(solution)/shard_map/ppermute | solution.py:46
  41.0 9.8 %collective-permute-done.8.refs_1_ = bf16[2,2,2,80,512]{4,3,2,1,0:T(8,128)(2,1)S(1)} collective-permute-done((bf16[2,2,2,80,512]{4,3,2,1,0:T(8,128)(2,1)S(1)}, bf16[2,2,2,80,512]{4,3,2,1,0:T(8,128)(2,1)S(1)}, u32[]{:S(2)}, u32[]{:S(2)}) %collective-permute-start.8) | collective-permute-done | bytes 655392 | tf_op jit(solution)/shard_map/ppermute | solution.py:46
  51.5 3.4 %collective-permute-done.9.refs_1_ = bf16[2,2,2,80,512]{4,3,2,1,0:T(8,128)(2,1)S(1)} collective-permute-done((bf16[2,2,2,80,512]{4,3,2,1,0:T(8,128)(2,1)S(1)}, bf16[2,2,2,80,512]{4,3,2,1,0:T(8,128)(2,1)S(1)}, u32[]{:S(2)}, u32[]{:S(2)}) %collective-permute-start.9) | collective-permute-done | bytes 655392 | tf_op jit(solution)/shard_map/ppermute | solution.py:46
  66.6 2.7 %collective-permute-done.13.refs_1_ = bf16[128,512]{1,0:T(8,128)(2,1)S(1)} collective-permute-done((bf16[128,512]{1,0:T(8,128)(2,1)S(1)}, bf16[128,512]{1,0:T(8,128)(2,1)S(1)}, u32[]{:S(2)}, u32[]{:S(2)}) %collective-permute-start.13) | collective-permute-done | bytes 131104 | tf_op jit(solution)/shard_map/ppermute | solution.py:46
  73.4 2.4 %collective-permute-start.17 = (bf16[2,128,512]{2,1,0:T(8,128)(2,1)S(1)}, bf16[2,128,512]{2,1,0:T(8,128)(2,1)S(1)}, u32[]{:S(2)}, u32[]{:S(2)}) collective-permute-start(bf16[2,128,512]{2,1,0:T(8,128)(2,1)S(1)} %get-tuple-element.188.refs_0_), channel_id=1, source_target_pairs={{0,2},{1,3},{2,0},{3,1},{4,6},{5,7},{6,4},{7,5},{8,10},{9,11},{10,... | collective-permute-start | bytes 786440 | tf_op jit(solution)/shard_map/ppermute | solution.py:46
  75.8 11.0 %collective-permute-done.18.refs_3_ = bf16[2,128,512]{2,1,0:T(8,128)(2,1)S(1)} collective-permute-done((bf16[2,128,512]{2,1,0:T(8,128)(2,1)S(1)}, bf16[2,128,512]{2,1,0:T(8,128)(2,1)S(1)}, u32[]{:S(2)}, u32[]{:S(2)}) %collective-permute-start.18) | collective-permute-done | bytes 262176 | tf_op jit(solution)/shard_map/ppermute | solution.py:46
  88.6 4.7 %collective-permute-done.21.refs_1_ = bf16[2,2,128,512]{3,2,1,0:T(8,128)(2,1)S(1)} collective-permute-done((bf16[2,2,128,512]{3,2,1,0:T(8,128)(2,1)S(1)}, bf16[2,2,128,512]{3,2,1,0:T(8,128)(2,1)S(1)}, u32[]{:S(2)}, u32[]{:S(2)}) %collective-permute-start.21) | collective-permute-done | bytes 524320 | tf_op jit(solution)/shard_map/ppermute | solution.py:46
  94.7 3.4 %shard_map.305 = (f32[384,512]{1,0:T(8,128)S(1)}, f32[384,128]{1,0:T(8,128)S(1)}) custom-call(s32[2,7]{1,0:T(2,128)S(1)} %stack.47.info, bf16[384,512]{1,0:T(8,128)(2,1)S(1)} %get-tuple-element.210.query, bf16[384,512]{1,0:T(8,128)(2,1)S(1)} %get-tuple-element.202.keys, bf16[384,512]{1,0:T(8,128)(2,1)S(1)} %get-tuple-element.203.values, ...), custom_call_target="tpu_custom_call" | custom-call | flops 805306368 | bytes 3276856 | tf_op jit(solution)/shard_map/pallas_call | solution.py:342
  99.1 9.7 %shard_map.307 = (bf16[384,512]{1,0:T(8,128)(2,1)}, f32[384,512]{1,0:T(8,128)S(1)}, bf16[384,512]{1,0:T(8,128)(2,1)S(1)}, bf16[16,144,512]{2,1,0:T(8,128)(2,1)S(...) custom-call(s32[2,7]{1,0:T(2,128)S(1)} %stack.47.info, bf16[384,512]{1,0:T(8,128)(2,1)S(1)} %bitcast.68, ...), custom_call_target="tpu_custom_call" | custom-call | flops 5435817984 | bytes 6324280 | tf_op jit(solution)/shard_map/pallas_call | solution.py:342
  109.0 5.6 %shard_map.308 = (bf16[384,512]{1,0:T(8,128)(2,1)S(1)}, bf16[4,128,512]{2,1,0:T(8,128)(2,1)S(1)}, bf16[4,128,512]{2,1,0:T(8,128)(2,1)S(1)}, bf16[4,128,512]{2,1,...) custom-call(s32[2,7]{1,0:T(2,128)S(1)} %stack.47.info, ...), custom_call_target="tpu_custom_call" | custom-call | flops 2013265920 | bytes 4653112 | tf_op jit(solution)/shard_map/pallas_call | solution.py:342
  119.6 3.3 %collective-permute-start.28 = (bf16[2,128,512]{2,1,0:T(8,128)(2,1)S(1)}, bf16[2,128,512]{2,1,0:T(8,128)(2,1)S(1)}, u32[]{:S(2)}, u32[]{:S(2)}) collective-permute-start(bf16[2,128,512]{2,1,0:T(8,128)(2,1)S(1)} %get-tuple-element.227), channel_id=1, source_target_pairs={{0,4},{1,5},{2,6},{3,7},{4,0},{5,1},{6,2},{7,3},{8,12},{9,13},{10,... | collective-permute-start | bytes 786440 | tf_op jit(solution)/shard_map/ppermute | solution.py:46
  122.9 10.0 %collective-permute-done.27.refs_1_ = bf16[2,128,512]{2,1,0:T(8,128)(2,1)S(1)} collective-permute-done((bf16[2,128,512]{2,1,0:T(8,128)(2,1)S(1)}, bf16[2,128,512]{2,1,0:T(8,128)(2,1)S(1)}, u32[]{:S(2)}, u32[]{:S(2)}) %collective-permute-start.27) | collective-permute-done | bytes 262176 | tf_op jit(solution)/shard_map/ppermute | solution.py:46
  135.7 2.6 %collective-permute-start.34 = (bf16[128,512]{1,0:T(8,128)(2,1)S(1)}, bf16[128,512]{1,0:T(8,128)(2,1)S(1)}, u32[]{:S(2)}, u32[]{:S(2)}) collective-permute-start(bf16[128,512]{1,0:T(8,128)(2,1)S(1)} %get-tuple-element.245), channel_id=1, source_target_pairs={{0,2},{1,3},{2,0},{3,1},{4,6},{5,7},{6,4},{7,5},{8,10},{9,11},{10,... | collective-permute-start | bytes 393224 | tf_op jit(solution)/shard_map/ppermute | solution.py:46
  140.1 3.4 %collective-permute-done.31 = bf16[128,512]{1,0:T(8,128)(2,1)S(1)} collective-permute-done((bf16[128,512]{1,0:T(8,128)(2,1)S(1)}, bf16[128,512]{1,0:T(8,128)(2,1)S(1)}, u32[]{:S(2)}, u32[]{:S(2)}) %collective-permute-start.31) | collective-permute-done | bytes 131104 | tf_op jit(solution)/shard_map/ppermute | solution.py:46
  146.9 2.7 %shard_map.312 = (f32[384,512]{1,0:T(8,128)S(1)}, f32[384,512]{1,0:T(8,128)S(1)}, f32[16,1024]{1,0:T(8,128)S(1)}, bf16[16,112,512]{2,1,0:T(8,128)(2,1)S(1)}, bf16[16,112,512]{2,1,0:T(8,128)(2,1)S(1)}) custom-call(s32[2,7]{1,0:T(2,128)S(1)} %stack.47.info, bf16[128,512]{1,0:T(8,128)(2,1)S(1)} %add_convert_fusion.1.key_memory, ...), custom_call_target="tpu_custom_call" | custom-call | flops 1006632960 | bytes 7094328 | tf_op jit(solution)/shard_map/pallas_call | solution.py:342
  153.6 2.9 %shard_map.313 = (bf16[384,512]{1,0:T(8,128)(2,1)}, bf16[16,48,512]{2,1,0:T(8,128)(2,1)S(1)}, bf16[16,48,512]{2,1,0:T(8,128)(2,1)S(1)}) custom-call(s32[2,7]{1,0:T(2,128)S(1)} %stack.47.info, bf16[384,512]{1,0:T(8,128)(2,1)S(1)} %bitcast.69, bf16[400,512]{1,0:T(8,128)(2,1)S(1)} %get-tuple-element.178.normed, ...), custom_call_target="tpu_custom_call" | custom-call | flops 1207959552 | bytes 10502200 | tf_op jit(solution)/shard_map/pallas_call | solution.py:342
  163.6 5.6 %collective-permute-done.40.refs_5_ = bf16[2,144,512]{2,1,0:T(8,128)(2,1)S(1)} collective-permute-done((bf16[2,144,512]{2,1,0:T(8,128)(2,1)S(1)}, bf16[2,144,512]{2,1,0:T(8,128)(2,1)S(1)}, u32[]{:S(2)}, u32[]{:S(2)}) %collective-permute-start.40) | collective-permute-done | bytes 294944 | tf_op jit(solution)/shard_map/ppermute | solution.py:46
  170.1 6.1 %collective-permute-done.38.refs_1_ = bf16[2,2,2,80,512]{4,3,2,1,0:T(8,128)(2,1)S(1)} collective-permute-done((bf16[2,2,2,80,512]{4,3,2,1,0:T(8,128)(2,1)S(1)}, bf16[2,2,2,80,512]{4,3,2,1,0:T(8,128)(2,1)S(1)}, u32[]{:S(2)}, u32[]{:S(2)}) %collective-permute-start.38) | collective-permute-done | bytes 655392 | tf_op jit(solution)/shard_map/ppermute | solution.py:46
  181.2 4.6 %collective-permute-done.45 = bf16[144,512]{1,0:T(8,128)(2,1)S(1)} collective-permute-done((bf16[144,512]{1,0:T(8,128)(2,1)S(1)}, bf16[144,512]{1,0:T(8,128)(2,1)S(1)}, u32[]{:S(2)}, u32[]{:S(2)}) %collective-permute-start.45) | collective-permute-done | bytes 147488 | tf_op jit(solution)/shard_map/ppermute | solution.py:46
  192.0 4.0 %collective-permute-done.46.refs_1_ = bf16[2,112,512]{2,1,0:T(8,128)(2,1)S(1)} collective-permute-done((bf16[2,112,512]{2,1,0:T(8,128)(2,1)S(1)}, bf16[2,112,512]{2,1,0:T(8,128)(2,1)S(1)}, u32[]{:S(2)}, u32[]{:S(2)}) %collective-permute-start.46) | collective-permute-done | bytes 229408 | tf_op jit(solution)/shard_map/ppermute | solution.py:46
  (143 shorter events, 92.2 us)
Async XLA Ops:
  13.5 9.0 %collective-permute-start.3 = (bf16[2,80,512]{2,1,0:T(8,128)(2,1)S(1)}, bf16[2,80,512]{2,1,0:T(8,128)(2,1)S(1)}, u32[]{:S(2)}, u32[]{:S(2)}) collective-permute-start(bf16[2,80,512]{2,1,0:T(8,128)(2,1)S(1)} %shard_map.289.refs_0_), channel_id=1, source_target_pairs={{0,2},{1,3},{2,0},{3,1},{4,6},{5,7},{6,4},{7,5},{8,10},{9,11},{10,... | collective-permute-start | bytes 491528 | tf_op jit(solution)/shard_map/ppermute | solution.py:46
  16.3 10.8 %collective-permute-start.4 = (bf16[2,80,512]{2,1,0:T(8,128)(2,1)S(1)}, bf16[2,80,512]{2,1,0:T(8,128)(2,1)S(1)}, u32[]{:S(2)}, u32[]{:S(2)}) collective-permute-start(bf16[2,80,512]{2,1,0:T(8,128)(2,1)S(1)} %shard_map.290.refs_0_), channel_id=1, source_target_pairs={{0,4},{1,5},{2,6},{3,7},{4,0},{5,1},{6,2},{7,3},{8,12},{9,13},{10,... | collective-permute-start | bytes 491528 | tf_op jit(solution)/shard_map/ppermute | solution.py:46
  23.0 10.5 %collective-permute-start.5 = (bf16[2,2,80,512]{3,2,1,0:T(8,128)(2,1)S(1)}, bf16[2,2,80,512]{3,2,1,0:T(8,128)(2,1)S(1)}, u32[]{:S(2)}, u32[]{:S(2)}) collective-permute-start(bf16[2,2,80,512]{3,2,1,0:T(8,128)(2,1)S(1)} %shard_map.291.refs_0_), channel_id=1, source_target_pairs={{0,8},{1,9},{2,10},{3,11},{4,12},{5,13},{6,14},{7,15},{8,0},{9,1},... | collective-permute-start | bytes 983048 | tf_op jit(solution)/shard_map/ppermute | solution.py:46
  27.6 10.4 %collective-permute-start.6 = (bf16[2,2,80,512]{3,2,1,0:T(8,128)(2,1)S(1)}, bf16[2,2,80,512]{3,2,1,0:T(8,128)(2,1)S(1)}, u32[]{:S(2)}, u32[]{:S(2)}) collective-permute-start(bf16[2,2,80,512]{3,2,1,0:T(8,128)(2,1)S(1)} %shard_map.292.refs_0_), channel_id=1, source_target_pairs={{0,16},{1,17},{2,18},{3,19},{4,20},{5,21},{6,22},{7,23},{8,24},{9,... | collective-permute-start | bytes 983048 | tf_op jit(solution)/shard_map/ppermute | solution.py:46
  34.1 16.6 %collective-permute-start.8 = (bf16[2,2,2,80,512]{4,3,2,1,0:T(8,128)(2,1)S(1)}, bf16[2,2,2,80,512]{4,3,2,1,0:T(8,128)(2,1)S(1)}, u32[]{:S(2)}, u32[]{:S(2)}) collective-permute-start(bf16[2,2,2,80,512]{4,3,2,1,0:T(8,128)(2,1)S(1)} %shard_map.293.refs_0_), channel_id=1, source_target_pairs={{0,16},{1,17},{2,18},{3,19},{4,20},{5,21},{6,22},{7,23},{8,24},{9,... | collective-permute-start | bytes 1966088 | tf_op jit(solution)/shard_map/ppermute | solution.py:46
  38.7 16.2 %collective-permute-start.9 = (bf16[2,2,2,80,512]{4,3,2,1,0:T(8,128)(2,1)S(1)}, bf16[2,2,2,80,512]{4,3,2,1,0:T(8,128)(2,1)S(1)}, u32[]{:S(2)}, u32[]{:S(2)}) collective-permute-start(bf16[2,2,2,80,512]{4,3,2,1,0:T(8,128)(2,1)S(1)} %get-tuple-element.171.refs_0_), channel_id=1, source_target_pairs={{0,8},{1,9},{2,10},{3,11},{4,12},{5,13},{6,14},{7,15},{8,0},{9,1},... | collective-permute-start | bytes 1966088 | tf_op jit(solution)/shard_map/ppermute | solution.py:46
  40.2 11.2 %collective-permute-start.10 = (bf16[2,144,512]{2,1,0:T(8,128)(2,1)S(1)}, bf16[2,144,512]{2,1,0:T(8,128)(2,1)S(1)}, u32[]{:S(2)}, u32[]{:S(2)}) collective-permute-start(bf16[2,144,512]{2,1,0:T(8,128)(2,1)S(1)} %get-tuple-element.173.refs_2_), channel_id=1, source_target_pairs={{0,2},{1,3},{2,0},{3,1},{4,6},{5,7},{6,4},{7,5},{8,10},{9,11},{10,... | collective-permute-start | bytes 884744 | tf_op jit(solution)/shard_map/ppermute | solution.py:46
  55.7 9.4 %collective-permute-start.15 = (bf16[2,2,144,256]{3,2,1,0:T(8,128)(2,1)S(1)}, bf16[2,2,144,256]{3,2,1,0:T(8,128)(2,1)S(1)}, u32[]{:S(2)}, u32[]{:S(2)}) collective-permute-start(bf16[2,2,144,256]{3,2,1,0:T(8,128)(2,1)S(1)} %get-tuple-element.184.refs_4_), channel_id=1, source_target_pairs={{0,8},{1,9},{2,10},{3,11},{4,12},{5,13},{6,14},{7,15},{8,0},{9,1},... | collective-permute-start | bytes 884744 | tf_op jit(solution)/shard_map/ppermute | solution.py:46
  57.5 9.1 %collective-permute-start.16 = (bf16[2,2,144,256]{3,2,1,0:T(8,128)(2,1)S(1)}, bf16[2,2,144,256]{3,2,1,0:T(8,128)(2,1)S(1)}, u32[]{:S(2)}, u32[]{:S(2)}) collective-permute-start(bf16[2,2,144,256]{3,2,1,0:T(8,128)(2,1)S(1)} %get-tuple-element.186.refs_6_), channel_id=1, source_target_pairs={{0,16},{1,17},{2,18},{3,19},{4,20},{5,21},{6,22},{7,23},{8,24},{9,... | collective-permute-start | bytes 884744 | tf_op jit(solution)/shard_map/ppermute | solution.py:46
  71.6 15.2 %collective-permute-start.19 = (bf16[2,2,2,144,256]{4,3,2,1,0:T(8,128)(2,1)S(1)}, bf16[2,2,2,144,256]{4,3,2,1,0:T(8,128)(2,1)S(1)}, u32[]{:S(2)}, u32[]{:S(2)}) collective-permute-start(bf16[2,2,2,144,256]{4,3,2,1,0:T(8,128)(2,1)S(1)} %get-tuple-element.192.refs_4_), channel_id=1, source_target_pairs={{0,16},{1,17},{2,18},{3,19},{4,20},{5,21},{6,22},{7,23},{8,24},{9,... | collective-permute-start | bytes 1769480 | tf_op jit(solution)/shard_map/ppermute | solution.py:46
  73.2 14.0 %collective-permute-start.20 = (bf16[2,2,2,144,256]{4,3,2,1,0:T(8,128)(2,1)S(1)}, bf16[2,2,2,144,256]{4,3,2,1,0:T(8,128)(2,1)S(1)}, u32[]{:S(2)}, u32[]{:S(2)}) collective-permute-start(bf16[2,2,2,144,256]{4,3,2,1,0:T(8,128)(2,1)S(1)} %get-tuple-element.194.refs_6_), channel_id=1, source_target_pairs={{0,8},{1,9},{2,10},{3,11},{4,12},{5,13},{6,14},{7,15},{8,0},{9,1},... | collective-permute-start | bytes 1769480 | tf_op jit(solution)/shard_map/ppermute | solution.py:46
  73.4 13.3 %collective-permute-start.18 = (bf16[2,128,512]{2,1,0:T(8,128)(2,1)S(1)}, bf16[2,128,512]{2,1,0:T(8,128)(2,1)S(1)}, u32[]{:S(2)}, u32[]{:S(2)}) collective-permute-start(bf16[2,128,512]{2,1,0:T(8,128)(2,1)S(1)} %get-tuple-element.190.refs_2_), channel_id=1, source_target_pairs={{0,4},{1,5},{2,6},{3,7},{4,0},{5,1},{6,2},{7,3},{8,12},{9,13},{10,... | collective-permute-start | bytes 786440 | tf_op jit(solution)/shard_map/ppermute | solution.py:46
  73.4 13.4 %collective-permute-start.17 = (bf16[2,128,512]{2,1,0:T(8,128)(2,1)S(1)}, bf16[2,128,512]{2,1,0:T(8,128)(2,1)S(1)}, u32[]{:S(2)}, u32[]{:S(2)}) collective-permute-start(bf16[2,128,512]{2,1,0:T(8,128)(2,1)S(1)} %get-tuple-element.188.refs_0_), channel_id=1, source_target_pairs={{0,2},{1,3},{2,0},{3,1},{4,6},{5,7},{6,4},{7,5},{8,10},{9,11},{10,... | collective-permute-start | bytes 786440 | tf_op jit(solution)/shard_map/ppermute | solution.py:46
  88.0 10.2 %collective-permute-start.23 = (bf16[2,2,2,2,144,512]{5,4,3,2,1,0:T(8,128)(2,1)S(1)}, bf16[2,2,2,2,144,512]{5,4,3,2,1,0:T(8,128)(2,1)S(1)}, u32[]{:S(2)}, u32[]{:S(2)}) collective-permute-start(bf16[2,2,2,2,144,512]{5,4,3,2,1,0:T(8,128)(2,1)S(1)} %get-tuple-element.205.refs_0_), channel_id=1, source_target_pairs={{0,1},{1,0},{2,3},{3,2},{4,5},{5,4},{6,7},{7,6},{8,9},{9,8},{10,11... | collective-permute-start | bytes 7077896 | tf_op jit(solution)/shard_map/ppermute | solution.py:46
  118.3 16.3 %collective-permute-start.29 = (bf16[2,2,2,144,256]{4,3,2,1,0:T(8,128)(2,1)S(1)}, bf16[2,2,2,144,256]{4,3,2,1,0:T(8,128)(2,1)S(1)}, u32[]{:S(2)}, u32[]{:S(2)}) collective-permute-start(bf16[2,2,2,144,256]{4,3,2,1,0:T(8,128)(2,1)S(1)} %get-tuple-element.230), channel_id=1, source_target_pairs={{0,16},{1,17},{2,18},{3,19},{4,20},{5,21},{6,22},{7,23},{8,24},{9,... | collective-permute-start | bytes 1769480 | tf_op jit(solution)/shard_map/ppermute | solution.py:46
  118.9 15.6 %collective-permute-start.30 = (bf16[2,2,2,144,256]{4,3,2,1,0:T(8,128)(2,1)S(1)}, bf16[2,2,2,144,256]{4,3,2,1,0:T(8,128)(2,1)S(1)}, u32[]{:S(2)}, u32[]{:S(2)}) collective-permute-start(bf16[2,2,2,144,256]{4,3,2,1,0:T(8,128)(2,1)S(1)} %get-tuple-element.233), channel_id=1, source_target_pairs={{0,8},{1,9},{2,10},{3,11},{4,12},{5,13},{6,14},{7,15},{8,0},{9,1},... | collective-permute-start | bytes 1769480 | tf_op jit(solution)/shard_map/ppermute | solution.py:46
  119.5 13.4 %collective-permute-start.27 = (bf16[2,128,512]{2,1,0:T(8,128)(2,1)S(1)}, bf16[2,128,512]{2,1,0:T(8,128)(2,1)S(1)}, u32[]{:S(2)}, u32[]{:S(2)}) collective-permute-start(bf16[2,128,512]{2,1,0:T(8,128)(2,1)S(1)} %get-tuple-element.224), channel_id=1, source_target_pairs={{0,2},{1,3},{2,0},{3,1},{4,6},{5,7},{6,4},{7,5},{8,10},{9,11},{10,... | collective-permute-start | bytes 786440 | tf_op jit(solution)/shard_map/ppermute | solution.py:46
  119.6 14.9 %collective-permute-start.28 = (bf16[2,128,512]{2,1,0:T(8,128)(2,1)S(1)}, bf16[2,128,512]{2,1,0:T(8,128)(2,1)S(1)}, u32[]{:S(2)}, u32[]{:S(2)}) collective-permute-start(bf16[2,128,512]{2,1,0:T(8,128)(2,1)S(1)} %get-tuple-element.227), channel_id=1, source_target_pairs={{0,4},{1,5},{2,6},{3,7},{4,0},{5,1},{6,2},{7,3},{8,12},{9,13},{10,... | collective-permute-start | bytes 786440 | tf_op jit(solution)/shard_map/ppermute | solution.py:46
  149.6 9.1 %collective-permute-start.36 = (bf16[2,2,2,2,112,512]{5,4,3,2,1,0:T(8,128)(2,1)S(1)}, bf16[2,2,2,2,112,512]{5,4,3,2,1,0:T(8,128)(2,1)S(1)}, u32[]{:S(2)}, u32[]{:S(2)}) collective-permute-start(bf16[2,2,2,2,112,512]{5,4,3,2,1,0:T(8,128)(2,1)S(1)} %bitcast.75), channel_id=1, source_target_pairs={{0,1},{1,0},{2,3},{3,2},{4,5},{5,4},{6,7},{7,6},{8,9},{9,8},{10,11... | collective-permute-start | bytes 5505032 | tf_op jit(solution)/shard_map/ppermute | solution.py:46
  159.4 16.7 %collective-permute-start.38 = (bf16[2,2,2,80,512]{4,3,2,1,0:T(8,128)(2,1)S(1)}, bf16[2,2,2,80,512]{4,3,2,1,0:T(8,128)(2,1)S(1)}, u32[]{:S(2)}, u32[]{:S(2)}) collective-permute-start(bf16[2,2,2,80,512]{4,3,2,1,0:T(8,128)(2,1)S(1)} %get-tuple-element.266), channel_id=1, source_target_pairs={{0,16},{1,17},{2,18},{3,19},{4,20},{5,21},{6,22},{7,23},{8,24},{9,... | collective-permute-start | bytes 1966088 | tf_op jit(solution)/shard_map/ppermute | solution.py:46
  160.8 9.2 %collective-permute-start.39 = (bf16[2,2,2,32,512]{4,3,2,1,0:T(8,128)(2,1)S(1)}, bf16[2,2,2,32,512]{4,3,2,1,0:T(8,128)(2,1)S(1)}, u32[]{:S(2)}, u32[]{:S(2)}) collective-permute-start(bf16[2,2,2,32,512]{4,3,2,1,0:T(8,128)(2,1)S(1)} %get-tuple-element.269), channel_id=1, source_target_pairs={{0,8},{1,9},{2,10},{3,11},{4,12},{5,13},{6,14},{7,15},{8,0},{9,1},... | collective-permute-start | bytes 786440 | tf_op jit(solution)/shard_map/ppermute | solution.py:46
  162.5 15.9 %collective-permute-start.41 = (bf16[2,2,2,48,512]{4,3,2,1,0:T(8,128)(2,1)S(1)}, bf16[2,2,2,48,512]{4,3,2,1,0:T(8,128)(2,1)S(1)}, u32[]{:S(2)}, u32[]{:S(2)}) collective-permute-start(bf16[2,2,2,48,512]{4,3,2,1,0:T(8,128)(2,1)S(1)} %get-tuple-element.274), channel_id=1, source_target_pairs={{0,8},{1,9},{2,10},{3,11},{4,12},{5,13},{6,14},{7,15},{8,0},{9,1},... | collective-permute-start | bytes 1179656 | tf_op jit(solution)/shard_map/ppermute | solution.py:46
  176.8 8.9 %collective-permute-start.45 = (bf16[144,512]{1,0:T(8,128)(2,1)S(1)}, bf16[144,512]{1,0:T(8,128)(2,1)S(1)}, u32[]{:S(2)}, u32[]{:S(2)}) collective-permute-start(bf16[144,512]{1,0:T(8,128)(2,1)S(1)} %get-tuple-element.286), channel_id=1, source_target_pairs={{0,4},{1,5},{2,6},{3,7},{4,0},{5,1},{6,2},{7,3},{8,12},{9,13},{10,... | collective-permute-start | bytes 442376 | tf_op jit(solution)/shard_map/ppermute | solution.py:46
  186.4 9.6 %collective-permute-start.46 = (bf16[2,112,512]{2,1,0:T(8,128)(2,1)S(1)}, bf16[2,112,512]{2,1,0:T(8,128)(2,1)S(1)}, u32[]{:S(2)}, u32[]{:S(2)}) collective-permute-start(bf16[2,112,512]{2,1,0:T(8,128)(2,1)S(1)} %get-tuple-element.291), channel_id=1, source_target_pairs={{0,2},{1,3},{2,0},{3,1},{4,6},{5,7},{6,4},{7,5},{8,10},{9,11},{10,... | collective-permute-start | bytes 688136 | tf_op jit(solution)/shard_map/ppermute | solution.py:46
  (32 other events, 247.5 us)

commit v6 on v4

--- a/solution.py
+++ b/solution.py
@@ -457,10 +457,13 @@
     keep_and_compress(info, low, weights, kept, window, memory, line)
 
 
-def value_kernel(info, normed, weights, query, kept, window, memory, line):
+def query_kernel(normed, weights, query):
+    query[...] = dot(normed[: query.shape[0], :], tile(weights, 4)).astype(BF16)
+
+
+def value_kernel(info, normed, weights, kept, window, memory, line):
     low = normed[...]
     keep_and_compress(info, low, weights, kept, window, memory, line)
-    query[...] = dot(low[: query.shape[0]], tile(weights, 4)).astype(BF16)
 
 
 def stacked(values, lower):
@@ -972,10 +975,10 @@
     keys_side = Gather(order, memory_key)
     keys_side.go(along[0])
     second = grouped(two.place().whole(), first_sizes)
-    query, values, value_window, memory_value = kernel(
+    values, value_window, memory_value = kernel(
         value_kernel,
         (info, normed, second),
-        ((rows, BF16), (rows, BF16), (windows, BF16), ((slots, width), BF16)),
+        ((rows, BF16), (windows, BF16), ((slots, width), BF16)),
         3 * matmul,
         limits[1],
         line,
@@ -983,6 +986,10 @@
     order.done(memory_value)
     values_side = Gather(order, memory_value)
     values_side.go(back[0])
+    (query,) = kernel(
+        query_kernel, (order.turn(normed), second), ((rows, BF16),), matmul, limits[1]
+    )
+    order.done(query)
     for at in range(1, max(len(across), len(along))):
         jobs = []
         if at < len(along):

time: 205 us -> 205 us (level)
    pallas_call x35 -> x36, Pallas kernels: 45.6 us -> 45.8 us  [kernel(): pl.pallas_call(body, in_specs=[pl.BlockSpec(memory_space=spec.get(a.dtype...]
  transfers between devices with their start and end apart: 50 -> 50, of which waited for: 34 -> 35; matrix products, arithmetic and copies ran while one was open for 2% -> 2% of each run, Pallas kernels for 14% -> 14%
where the time goes in v6:
time: 205 us; the launch traced here: 204 us
  waiting for transfers between devices  90.1 us (44%)
  starting transfers between devices  56 us (27%)
  Pallas kernels  47.6 us (23%)
  local copies, waits for them, and re-layouts  7.22 us (4%)
  other arithmetic  2.39 us (1%)
    ppermute x48, waiting for transfers between devices, swap(): lax.ppermute(array, AXES, [(i, i ^ mask) for i in range(device_count())])  86.9 us
    ppermute x48, starting transfers between devices, swap(): lax.ppermute(array, AXES, [(i, i ^ mask) for i in range(device_count())])  53.2 us
    pallas_call x36, Pallas kernels, kernel(): pl.pallas_call(body, in_specs=[pl.BlockSpec(memory_space=spec.get(a.dtype...  45.8 us
  transfers between devices with their start and end apart: 50, of which 35 were waited for; matrix products, arithmetic and copies ran while one was open for 2% of the time, Pallas kernels for 14%

profile of v6, /device:TPU:0, one launch (start us, length us, event | category | flops | bytes accessed | tf_op | source)
XLA Modules:
  0.0 204.4 jit_solution(9169506722658361545)
XLA Ops:
  4.0 4.1 %collective-permute-start = (bf16[80,512]{1,0:T(8,128)(2,1)}, bf16[80,512]{1,0:T(8,128)(2,1)S(1)}, u32[]{:S(2)}, u32[]{:S(2)}) collective-permute-start(bf16[80,512]{1,0:T(8,128)(2,1)} %get-tuple-element.158.refs_0_), channel_id=1, source_target_pairs={{0,4},{1,5},{2,6},{3,7},{4,0},{5,1},{6,2},{7,3},{8,12},{9,13},{10,... | collective-permute-start | bytes 245768 | tf_op jit(solution)/shard_map/ppermute | solution.py:46
  9.7 2.3 %collective-permute-done.refs_1_ = bf16[80,512]{1,0:T(8,128)(2,1)S(1)} collective-permute-done((bf16[80,512]{1,0:T(8,128)(2,1)}, bf16[80,512]{1,0:T(8,128)(2,1)S(1)}, u32[]{:S(2)}, u32[]{:S(2)}) %collective-permute-start) | collective-permute-done | bytes 81952 | tf_op jit(solution)/shard_map/ppermute | solution.py:46
  16.3 3.3 %collective-permute-start.4 = (bf16[2,80,512]{2,1,0:T(8,128)(2,1)S(1)}, bf16[2,80,512]{2,1,0:T(8,128)(2,1)S(1)}, u32[]{:S(2)}, u32[]{:S(2)}) collective-permute-start(bf16[2,80,512]{2,1,0:T(8,128)(2,1)S(1)} %shard_map.290.refs_0_), channel_id=1, source_target_pairs={{0,4},{1,5},{2,6},{3,7},{4,0},{5,1},{6,2},{7,3},{8,12},{9,13},{10,... | collective-permute-start | bytes 491528 | tf_op jit(solution)/shard_map/ppermute | solution.py:46
  24.6 2.5 %collective-permute-done.4.refs_1_ = bf16[2,80,512]{2,1,0:T(8,128)(2,1)S(1)} collective-permute-done((bf16[2,80,512]{2,1,0:T(8,128)(2,1)S(1)}, bf16[2,80,512]{2,1,0:T(8,128)(2,1)S(1)}, u32[]{:S(2)}, u32[]{:S(2)}) %collective-permute-start.4) | collective-permute-done | bytes 163872 | tf_op jit(solution)/shard_map/ppermute | solution.py:46
  29.2 2.9 %collective-permute-start.7 = (bf16[144,512]{1,0:T(8,128)(2,1)}, bf16[144,512]{1,0:T(8,128)(2,1)S(1)}, u32[]{:S(2)}, u32[]{:S(2)}) collective-permute-start(bf16[144,512]{1,0:T(8,128)(2,1)} %get-tuple-element.167.refs_2_), channel_id=1, source_target_pairs={{0,4},{1,5},{2,6},{3,7},{4,0},{5,1},{6,2},{7,3},{8,12},{9,13},{10,... | collective-permute-start | bytes 442376 | tf_op jit(solution)/shard_map/ppermute | solution.py:46
  35.7 2.4 %collective-permute-done.7.refs_3_ = bf16[144,512]{1,0:T(8,128)(2,1)S(1)} collective-permute-done((bf16[144,512]{1,0:T(8,128)(2,1)}, bf16[144,512]{1,0:T(8,128)(2,1)S(1)}, u32[]{:S(2)}, u32[]{:S(2)}) %collective-permute-start.7) | collective-permute-done | bytes 147488 | tf_op jit(solution)/shard_map/ppermute | solution.py:46
  41.0 9.8 %collective-permute-done.8.refs_1_ = bf16[2,2,2,80,512]{4,3,2,1,0:T(8,128)(2,1)S(1)} collective-permute-done((bf16[2,2,2,80,512]{4,3,2,1,0:T(8,128)(2,1)S(1)}, bf16[2,2,2,80,512]{4,3,2,1,0:T(8,128)(2,1)S(1)}, u32[]{:S(2)}, u32[]{:S(2)}) %collective-permute-start.8) | collective-permute-done | bytes 655392 | tf_op jit(solution)/shard_map/ppermute | solution.py:46
  51.5 3.4 %collective-permute-done.9.refs_1_ = bf16[2,2,2,80,512]{4,3,2,1,0:T(8,128)(2,1)S(1)} collective-permute-done((bf16[2,2,2,80,512]{4,3,2,1,0:T(8,128)(2,1)S(1)}, bf16[2,2,2,80,512]{4,3,2,1,0:T(8,128)(2,1)S(1)}, u32[]{:S(2)}, u32[]{:S(2)}) %collective-permute-start.9) | collective-permute-done | bytes 655392 | tf_op jit(solution)/shard_map/ppermute | solution.py:46
  66.6 2.7 %collective-permute-done.13.refs_1_ = bf16[128,512]{1,0:T(8,128)(2,1)S(1)} collective-permute-done((bf16[128,512]{1,0:T(8,128)(2,1)S(1)}, bf16[128,512]{1,0:T(8,128)(2,1)S(1)}, u32[]{:S(2)}, u32[]{:S(2)}) %collective-permute-start.13) | collective-permute-done | bytes 131104 | tf_op jit(solution)/shard_map/ppermute | solution.py:46
  73.2 2.4 %collective-permute-start.17 = (bf16[2,128,512]{2,1,0:T(8,128)(2,1)S(1)}, bf16[2,128,512]{2,1,0:T(8,128)(2,1)S(1)}, u32[]{:S(2)}, u32[]{:S(2)}) collective-permute-start(bf16[2,128,512]{2,1,0:T(8,128)(2,1)S(1)} %get-tuple-element.189.refs_0_), channel_id=1, source_target_pairs={{0,2},{1,3},{2,0},{3,1},{4,6},{5,7},{6,4},{7,5},{8,10},{9,11},{10,... | collective-permute-start | bytes 786440 | tf_op jit(solution)/shard_map/ppermute | solution.py:46
  75.6 10.9 %collective-permute-done.18.refs_3_ = bf16[2,128,512]{2,1,0:T(8,128)(2,1)S(1)} collective-permute-done((bf16[2,128,512]{2,1,0:T(8,128)(2,1)S(1)}, bf16[2,128,512]{2,1,0:T(8,128)(2,1)S(1)}, u32[]{:S(2)}, u32[]{:S(2)}) %collective-permute-start.18) | collective-permute-done | bytes 262176 | tf_op jit(solution)/shard_map/ppermute | solution.py:46
  88.4 4.7 %collective-permute-done.21.refs_1_ = bf16[2,2,128,512]{3,2,1,0:T(8,128)(2,1)S(1)} collective-permute-done((bf16[2,2,128,512]{3,2,1,0:T(8,128)(2,1)S(1)}, bf16[2,2,128,512]{3,2,1,0:T(8,128)(2,1)S(1)}, u32[]{:S(2)}, u32[]{:S(2)}) %collective-permute-start.21) | collective-permute-done | bytes 524320 | tf_op jit(solution)/shard_map/ppermute | solution.py:46
  94.5 3.4 %shard_map.306 = (f32[384,512]{1,0:T(8,128)S(1)}, f32[384,128]{1,0:T(8,128)S(1)}) custom-call(s32[2,7]{1,0:T(2,128)S(1)} %stack.47.info, bf16[384,512]{1,0:T(8,128)(2,1)S(1)} %shard_map.301.query, bf16[384,512]{1,0:T(8,128)(2,1)S(1)} %get-tuple-element.202.keys, bf16[384,512]{1,0:T(8,128)(2,1)S(1)} %get-tuple-element.203.values, ...), custom_call_target="tpu_custom_call" | custom-call | flops 805306368 | bytes 3276856 | tf_op jit(solution)/shard_map/pallas_call | solution.py:342
  98.9 9.7 %shard_map.308 = (bf16[384,512]{1,0:T(8,128)(2,1)}, f32[384,512]{1,0:T(8,128)S(1)}, bf16[384,512]{1,0:T(8,128)(2,1)S(1)}, bf16[16,144,512]{2,1,0:T(8,128)(2,1)S(...) custom-call(s32[2,7]{1,0:T(2,128)S(1)} %stack.47.info, bf16[384,512]{1,0:T(8,128)(2,1)S(1)} %bitcast.69, ...), custom_call_target="tpu_custom_call" | custom-call | flops 5435817984 | bytes 6324280 | tf_op jit(solution)/shard_map/pallas_call | solution.py:342
  108.8 5.6 %shard_map.309 = (bf16[384,512]{1,0:T(8,128)(2,1)S(1)}, bf16[4,128,512]{2,1,0:T(8,128)(2,1)S(1)}, bf16[4,128,512]{2,1,0:T(8,128)(2,1)S(1)}, bf16[4,128,512]{2,1,...) custom-call(s32[2,7]{1,0:T(2,128)S(1)} %stack.47.info, ...), custom_call_target="tpu_custom_call" | custom-call | flops 2013265920 | bytes 4653112 | tf_op jit(solution)/shard_map/pallas_call | solution.py:342
  119.5 3.4 %collective-permute-start.29 = (bf16[2,128,512]{2,1,0:T(8,128)(2,1)S(1)}, bf16[2,128,512]{2,1,0:T(8,128)(2,1)S(1)}, u32[]{:S(2)}, u32[]{:S(2)}) collective-permute-start(bf16[2,128,512]{2,1,0:T(8,128)(2,1)S(1)} %get-tuple-element.229), channel_id=1, source_target_pairs={{0,4},{1,5},{2,6},{3,7},{4,0},{5,1},{6,2},{7,3},{8,12},{9,13},{10,... | collective-permute-start | bytes 786440 | tf_op jit(solution)/shard_map/ppermute | solution.py:46
  122.9 10.0 %collective-permute-done.27.refs_1_ = bf16[2,128,512]{2,1,0:T(8,128)(2,1)S(1)} collective-permute-done((bf16[2,128,512]{2,1,0:T(8,128)(2,1)S(1)}, bf16[2,128,512]{2,1,0:T(8,128)(2,1)S(1)}, u32[]{:S(2)}, u32[]{:S(2)}) %collective-permute-start.27) | collective-permute-done | bytes 262176 | tf_op jit(solution)/shard_map/ppermute | solution.py:46
  145.2 2.7 %shard_map.315 = (f32[384,512]{1,0:T(8,128)S(1)}, f32[384,512]{1,0:T(8,128)S(1)}, f32[16,1024]{1,0:T(8,128)S(1)}, bf16[16,112,512]{2,1,0:T(8,128)(2,1)S(1)}, bf16[16,112,512]{2,1,0:T(8,128)(2,1)S(1)}) custom-call(s32[2,7]{1,0:T(2,128)S(1)} %stack.47.info, bf16[128,512]{1,0:T(8,128)(2,1)S(1)} %add_convert_fusion.1.key_memory, ...), custom_call_target="tpu_custom_call" | custom-call | flops 1006632960 | bytes 7094328 | tf_op jit(solution)/shard_map/pallas_call | solution.py:342
  149.5 2.3 %collective-permute-done.35.rims = f32[16,1024]{1,0:T(8,128)S(1)} collective-permute-done((f32[16,1024]{1,0:T(8,128)S(1)}, f32[16,1024]{1,0:T(8,128)S(1)}, u32[]{:S(2)}, u32[]{:S(2)}) %collective-permute-start.35) | collective-permute-done | bytes 65568 | tf_op jit(solution)/shard_map/ppermute | solution.py:1106
  151.9 2.9 %shard_map.316 = (bf16[384,512]{1,0:T(8,128)(2,1)}, bf16[16,48,512]{2,1,0:T(8,128)(2,1)S(1)}, bf16[16,48,512]{2,1,0:T(8,128)(2,1)S(1)}) custom-call(s32[2,7]{1,0:T(2,128)S(1)} %stack.47.info, bf16[384,512]{1,0:T(8,128)(2,1)S(1)} %bitcast.70, bf16[400,512]{1,0:T(8,128)(2,1)S(1)} %get-tuple-element.181.normed, ...), custom_call_target="tpu_custom_call" | custom-call | flops 1207959552 | bytes 10502200 | tf_op jit(solution)/shard_map/pallas_call | solution.py:342
  162.8 5.1 %collective-permute-done.40.refs_5_ = bf16[2,144,512]{2,1,0:T(8,128)(2,1)S(1)} collective-permute-done((bf16[2,144,512]{2,1,0:T(8,128)(2,1)S(1)}, bf16[2,144,512]{2,1,0:T(8,128)(2,1)S(1)}, u32[]{:S(2)}, u32[]{:S(2)}) %collective-permute-start.40) | collective-permute-done | bytes 294944 | tf_op jit(solution)/shard_map/ppermute | solution.py:46
  169.3 5.1 %collective-permute-done.38.refs_1_ = bf16[2,2,2,80,512]{4,3,2,1,0:T(8,128)(2,1)S(1)} collective-permute-done((bf16[2,2,2,80,512]{4,3,2,1,0:T(8,128)(2,1)S(1)}, bf16[2,2,2,80,512]{4,3,2,1,0:T(8,128)(2,1)S(1)}, u32[]{:S(2)}, u32[]{:S(2)}) %collective-permute-start.38) | collective-permute-done | bytes 655392 | tf_op jit(solution)/shard_map/ppermute | solution.py:46
  180.8 3.3 %collective-permute-done.45 = bf16[144,512]{1,0:T(8,128)(2,1)S(1)} collective-permute-done((bf16[144,512]{1,0:T(8,128)(2,1)S(1)}, bf16[144,512]{1,0:T(8,128)(2,1)S(1)}, u32[]{:S(2)}, u32[]{:S(2)}) %collective-permute-start.45) | collective-permute-done | bytes 147488 | tf_op jit(solution)/shard_map/ppermute | solution.py:46
  190.4 3.9 %collective-permute-done.46.refs_1_ = bf16[2,112,512]{2,1,0:T(8,128)(2,1)S(1)} collective-permute-done((bf16[2,112,512]{2,1,0:T(8,128)(2,1)S(1)}, bf16[2,112,512]{2,1,0:T(8,128)(2,1)S(1)}, u32[]{:S(2)}, u32[]{:S(2)}) %collective-permute-start.46) | collective-permute-done | bytes 229408 | tf_op jit(solution)/shard_map/ppermute | solution.py:46
  (146 shorter events, 94.3 us)
Async XLA Ops:
  13.5 9.0 %collective-permute-start.3 = (bf16[2,80,512]{2,1,0:T(8,128)(2,1)S(1)}, bf16[2,80,512]{2,1,0:T(8,128)(2,1)S(1)}, u32[]{:S(2)}, u32[]{:S(2)}) collective-permute-start(bf16[2,80,512]{2,1,0:T(8,128)(2,1)S(1)} %shard_map.289.refs_0_), channel_id=1, source_target_pairs={{0,2},{1,3},{2,0},{3,1},{4,6},{5,7},{6,4},{7,5},{8,10},{9,11},{10,... | collective-permute-start | bytes 491528 | tf_op jit(solution)/shard_map/ppermute | solution.py:46
  16.3 10.8 %collective-permute-start.4 = (bf16[2,80,512]{2,1,0:T(8,128)(2,1)S(1)}, bf16[2,80,512]{2,1,0:T(8,128)(2,1)S(1)}, u32[]{:S(2)}, u32[]{:S(2)}) collective-permute-start(bf16[2,80,512]{2,1,0:T(8,128)(2,1)S(1)} %shard_map.290.refs_0_), channel_id=1, source_target_pairs={{0,4},{1,5},{2,6},{3,7},{4,0},{5,1},{6,2},{7,3},{8,12},{9,13},{10,... | collective-permute-start | bytes 491528 | tf_op jit(solution)/shard_map/ppermute | solution.py:46
  23.0 10.5 %collective-permute-start.5 = (bf16[2,2,80,512]{3,2,1,0:T(8,128)(2,1)S(1)}, bf16[2,2,80,512]{3,2,1,0:T(8,128)(2,1)S(1)}, u32[]{:S(2)}, u32[]{:S(2)}) collective-permute-start(bf16[2,2,80,512]{3,2,1,0:T(8,128)(2,1)S(1)} %shard_map.291.refs_0_), channel_id=1, source_target_pairs={{0,8},{1,9},{2,10},{3,11},{4,12},{5,13},{6,14},{7,15},{8,0},{9,1},... | collective-permute-start | bytes 983048 | tf_op jit(solution)/shard_map/ppermute | solution.py:46
  27.6 10.4 %collective-permute-start.6 = (bf16[2,2,80,512]{3,2,1,0:T(8,128)(2,1)S(1)}, bf16[2,2,80,512]{3,2,1,0:T(8,128)(2,1)S(1)}, u32[]{:S(2)}, u32[]{:S(2)}) collective-permute-start(bf16[2,2,80,512]{3,2,1,0:T(8,128)(2,1)S(1)} %shard_map.292.refs_0_), channel_id=1, source_target_pairs={{0,16},{1,17},{2,18},{3,19},{4,20},{5,21},{6,22},{7,23},{8,24},{9,... | collective-permute-start | bytes 983048 | tf_op jit(solution)/shard_map/ppermute | solution.py:46
  29.2 8.8 %collective-permute-start.7 = (bf16[144,512]{1,0:T(8,128)(2,1)}, bf16[144,512]{1,0:T(8,128)(2,1)S(1)}, u32[]{:S(2)}, u32[]{:S(2)}) collective-permute-start(bf16[144,512]{1,0:T(8,128)(2,1)} %get-tuple-element.167.refs_2_), channel_id=1, source_target_pairs={{0,4},{1,5},{2,6},{3,7},{4,0},{5,1},{6,2},{7,3},{8,12},{9,13},{10,... | collective-permute-start | bytes 442376 | tf_op jit(solution)/shard_map/ppermute | solution.py:46
  34.1 16.6 %collective-permute-start.8 = (bf16[2,2,2,80,512]{4,3,2,1,0:T(8,128)(2,1)S(1)}, bf16[2,2,2,80,512]{4,3,2,1,0:T(8,128)(2,1)S(1)}, u32[]{:S(2)}, u32[]{:S(2)}) collective-permute-start(bf16[2,2,2,80,512]{4,3,2,1,0:T(8,128)(2,1)S(1)} %shard_map.293.refs_0_), channel_id=1, source_target_pairs={{0,16},{1,17},{2,18},{3,19},{4,20},{5,21},{6,22},{7,23},{8,24},{9,... | collective-permute-start | bytes 1966088 | tf_op jit(solution)/shard_map/ppermute | solution.py:46
  38.7 16.2 %collective-permute-start.9 = (bf16[2,2,2,80,512]{4,3,2,1,0:T(8,128)(2,1)S(1)}, bf16[2,2,2,80,512]{4,3,2,1,0:T(8,128)(2,1)S(1)}, u32[]{:S(2)}, u32[]{:S(2)}) collective-permute-start(bf16[2,2,2,80,512]{4,3,2,1,0:T(8,128)(2,1)S(1)} %get-tuple-element.171.refs_0_), channel_id=1, source_target_pairs={{0,8},{1,9},{2,10},{3,11},{4,12},{5,13},{6,14},{7,15},{8,0},{9,1},... | collective-permute-start | bytes 1966088 | tf_op jit(solution)/shard_map/ppermute | solution.py:46
  40.2 11.2 %collective-permute-start.10 = (bf16[2,144,512]{2,1,0:T(8,128)(2,1)S(1)}, bf16[2,144,512]{2,1,0:T(8,128)(2,1)S(1)}, u32[]{:S(2)}, u32[]{:S(2)}) collective-permute-start(bf16[2,144,512]{2,1,0:T(8,128)(2,1)S(1)} %get-tuple-element.173.refs_2_), channel_id=1, source_target_pairs={{0,2},{1,3},{2,0},{3,1},{4,6},{5,7},{6,4},{7,5},{8,10},{9,11},{10,... | collective-permute-start | bytes 884744 | tf_op jit(solution)/shard_map/ppermute | solution.py:46
  55.7 9.4 %collective-permute-start.15 = (bf16[2,2,144,256]{3,2,1,0:T(8,128)(2,1)S(1)}, bf16[2,2,144,256]{3,2,1,0:T(8,128)(2,1)S(1)}, u32[]{:S(2)}, u32[]{:S(2)}) collective-permute-start(bf16[2,2,144,256]{3,2,1,0:T(8,128)(2,1)S(1)} %get-tuple-element.185.refs_4_), channel_id=1, source_target_pairs={{0,8},{1,9},{2,10},{3,11},{4,12},{5,13},{6,14},{7,15},{8,0},{9,1},... | collective-permute-start | bytes 884744 | tf_op jit(solution)/shard_map/ppermute | solution.py:46
  57.5 9.1 %collective-permute-start.16 = (bf16[2,2,144,256]{3,2,1,0:T(8,128)(2,1)S(1)}, bf16[2,2,144,256]{3,2,1,0:T(8,128)(2,1)S(1)}, u32[]{:S(2)}, u32[]{:S(2)}) collective-permute-start(bf16[2,2,144,256]{3,2,1,0:T(8,128)(2,1)S(1)} %get-tuple-element.187.refs_6_), channel_id=1, source_target_pairs={{0,16},{1,17},{2,18},{3,19},{4,20},{5,21},{6,22},{7,23},{8,24},{9,... | collective-permute-start | bytes 884744 | tf_op jit(solution)/shard_map/ppermute | solution.py:46
  71.4 15.2 %collective-permute-start.19 = (bf16[2,2,2,144,256]{4,3,2,1,0:T(8,128)(2,1)S(1)}, bf16[2,2,2,144,256]{4,3,2,1,0:T(8,128)(2,1)S(1)}, u32[]{:S(2)}, u32[]{:S(2)}) collective-permute-start(bf16[2,2,2,144,256]{4,3,2,1,0:T(8,128)(2,1)S(1)} %get-tuple-element.193.refs_4_), channel_id=1, source_target_pairs={{0,16},{1,17},{2,18},{3,19},{4,20},{5,21},{6,22},{7,23},{8,24},{9,... | collective-permute-start | bytes 1769480 | tf_op jit(solution)/shard_map/ppermute | solution.py:46
  73.0 14.0 %collective-permute-start.20 = (bf16[2,2,2,144,256]{4,3,2,1,0:T(8,128)(2,1)S(1)}, bf16[2,2,2,144,256]{4,3,2,1,0:T(8,128)(2,1)S(1)}, u32[]{:S(2)}, u32[]{:S(2)}) collective-permute-start(bf16[2,2,2,144,256]{4,3,2,1,0:T(8,128)(2,1)S(1)} %get-tuple-element.195.refs_6_), channel_id=1, source_target_pairs={{0,8},{1,9},{2,10},{3,11},{4,12},{5,13},{6,14},{7,15},{8,0},{9,1},... | collective-permute-start | bytes 1769480 | tf_op jit(solution)/shard_map/ppermute | solution.py:46
  73.2 13.2 %collective-permute-start.18 = (bf16[2,128,512]{2,1,0:T(8,128)(2,1)S(1)}, bf16[2,128,512]{2,1,0:T(8,128)(2,1)S(1)}, u32[]{:S(2)}, u32[]{:S(2)}) collective-permute-start(bf16[2,128,512]{2,1,0:T(8,128)(2,1)S(1)} %get-tuple-element.191.refs_2_), channel_id=1, source_target_pairs={{0,4},{1,5},{2,6},{3,7},{4,0},{5,1},{6,2},{7,3},{8,12},{9,13},{10,... | collective-permute-start | bytes 786440 | tf_op jit(solution)/shard_map/ppermute | solution.py:46
  73.2 13.4 %collective-permute-start.17 = (bf16[2,128,512]{2,1,0:T(8,128)(2,1)S(1)}, bf16[2,128,512]{2,1,0:T(8,128)(2,1)S(1)}, u32[]{:S(2)}, u32[]{:S(2)}) collective-permute-start(bf16[2,128,512]{2,1,0:T(8,128)(2,1)S(1)} %get-tuple-element.189.refs_0_), channel_id=1, source_target_pairs={{0,2},{1,3},{2,0},{3,1},{4,6},{5,7},{6,4},{7,5},{8,10},{9,11},{10,... | collective-permute-start | bytes 786440 | tf_op jit(solution)/shard_map/ppermute | solution.py:46
  87.7 10.1 %collective-permute-start.23 = (bf16[2,2,2,2,144,512]{5,4,3,2,1,0:T(8,128)(2,1)S(1)}, bf16[2,2,2,2,144,512]{5,4,3,2,1,0:T(8,128)(2,1)S(1)}, u32[]{:S(2)}, u32[]{:S(2)}) collective-permute-start(bf16[2,2,2,2,144,512]{5,4,3,2,1,0:T(8,128)(2,1)S(1)} %get-tuple-element.205.refs_0_), channel_id=1, source_target_pairs={{0,1},{1,0},{2,3},{3,2},{4,5},{5,4},{6,7},{7,6},{8,9},{9,8},{10,11... | collective-permute-start | bytes 7077896 | tf_op jit(solution)/shard_map/ppermute | solution.py:46
  118.1 16.5 %collective-permute-start.30 = (bf16[2,2,2,144,256]{4,3,2,1,0:T(8,128)(2,1)S(1)}, bf16[2,2,2,144,256]{4,3,2,1,0:T(8,128)(2,1)S(1)}, u32[]{:S(2)}, u32[]{:S(2)}) collective-permute-start(bf16[2,2,2,144,256]{4,3,2,1,0:T(8,128)(2,1)S(1)} %get-tuple-element.232), channel_id=1, source_target_pairs={{0,16},{1,17},{2,18},{3,19},{4,20},{5,21},{6,22},{7,23},{8,24},{9,... | collective-permute-start | bytes 1769480 | tf_op jit(solution)/shard_map/ppermute | solution.py:46
  118.7 15.9 %collective-permute-start.31 = (bf16[2,2,2,144,256]{4,3,2,1,0:T(8,128)(2,1)S(1)}, bf16[2,2,2,144,256]{4,3,2,1,0:T(8,128)(2,1)S(1)}, u32[]{:S(2)}, u32[]{:S(2)}) collective-permute-start(bf16[2,2,2,144,256]{4,3,2,1,0:T(8,128)(2,1)S(1)} %get-tuple-element.235), channel_id=1, source_target_pairs={{0,8},{1,9},{2,10},{3,11},{4,12},{5,13},{6,14},{7,15},{8,0},{9,1},... | collective-permute-start | bytes 1769480 | tf_op jit(solution)/shard_map/ppermute | solution.py:46
  119.5 13.4 %collective-permute-start.27 = (bf16[2,128,512]{2,1,0:T(8,128)(2,1)S(1)}, bf16[2,128,512]{2,1,0:T(8,128)(2,1)S(1)}, u32[]{:S(2)}, u32[]{:S(2)}) collective-permute-start(bf16[2,128,512]{2,1,0:T(8,128)(2,1)S(1)} %get-tuple-element.225), channel_id=1, source_target_pairs={{0,2},{1,3},{2,0},{3,1},{4,6},{5,7},{6,4},{7,5},{8,10},{9,11},{10,... | collective-permute-start | bytes 786440 | tf_op jit(solution)/shard_map/ppermute | solution.py:46
  119.5 15.1 %collective-permute-start.29 = (bf16[2,128,512]{2,1,0:T(8,128)(2,1)S(1)}, bf16[2,128,512]{2,1,0:T(8,128)(2,1)S(1)}, u32[]{:S(2)}, u32[]{:S(2)}) collective-permute-start(bf16[2,128,512]{2,1,0:T(8,128)(2,1)S(1)} %get-tuple-element.229), channel_id=1, source_target_pairs={{0,4},{1,5},{2,6},{3,7},{4,0},{5,1},{6,2},{7,3},{8,12},{9,13},{10,... | collective-permute-start | bytes 786440 | tf_op jit(solution)/shard_map/ppermute | solution.py:46
  147.9 9.1 %collective-permute-start.36 = (bf16[2,2,2,2,112,512]{5,4,3,2,1,0:T(8,128)(2,1)S(1)}, bf16[2,2,2,2,112,512]{5,4,3,2,1,0:T(8,128)(2,1)S(1)}, u32[]{:S(2)}, u32[]{:S(2)}) collective-permute-start(bf16[2,2,2,2,112,512]{5,4,3,2,1,0:T(8,128)(2,1)S(1)} %bitcast.76), channel_id=1, source_target_pairs={{0,1},{1,0},{2,3},{3,2},{4,5},{5,4},{6,7},{7,6},{8,9},{9,8},{10,11... | collective-permute-start | bytes 5505032 | tf_op jit(solution)/shard_map/ppermute | solution.py:46
  157.7 16.7 %collective-permute-start.38 = (bf16[2,2,2,80,512]{4,3,2,1,0:T(8,128)(2,1)S(1)}, bf16[2,2,2,80,512]{4,3,2,1,0:T(8,128)(2,1)S(1)}, u32[]{:S(2)}, u32[]{:S(2)}) collective-permute-start(bf16[2,2,2,80,512]{4,3,2,1,0:T(8,128)(2,1)S(1)} %get-tuple-element.266), channel_id=1, source_target_pairs={{0,16},{1,17},{2,18},{3,19},{4,20},{5,21},{6,22},{7,23},{8,24},{9,... | collective-permute-start | bytes 1966088 | tf_op jit(solution)/shard_map/ppermute | solution.py:46
  160.1 9.2 %collective-permute-start.39 = (bf16[2,2,2,32,512]{4,3,2,1,0:T(8,128)(2,1)S(1)}, bf16[2,2,2,32,512]{4,3,2,1,0:T(8,128)(2,1)S(1)}, u32[]{:S(2)}, u32[]{:S(2)}) collective-permute-start(bf16[2,2,2,32,512]{4,3,2,1,0:T(8,128)(2,1)S(1)} %get-tuple-element.269), channel_id=1, source_target_pairs={{0,8},{1,9},{2,10},{3,11},{4,12},{5,13},{6,14},{7,15},{8,0},{9,1},... | collective-permute-start | bytes 786440 | tf_op jit(solution)/shard_map/ppermute | solution.py:46
  161.7 16.4 %collective-permute-start.41 = (bf16[2,2,2,48,512]{4,3,2,1,0:T(8,128)(2,1)S(1)}, bf16[2,2,2,48,512]{4,3,2,1,0:T(8,128)(2,1)S(1)}, u32[]{:S(2)}, u32[]{:S(2)}) collective-permute-start(bf16[2,2,2,48,512]{4,3,2,1,0:T(8,128)(2,1)S(1)} %get-tuple-element.274), channel_id=1, source_target_pairs={{0,8},{1,9},{2,10},{3,11},{4,12},{5,13},{6,14},{7,15},{8,0},{9,1},... | collective-permute-start | bytes 1179656 | tf_op jit(solution)/shard_map/ppermute | solution.py:46
  175.1 9.0 %collective-permute-start.45 = (bf16[144,512]{1,0:T(8,128)(2,1)S(1)}, bf16[144,512]{1,0:T(8,128)(2,1)S(1)}, u32[]{:S(2)}, u32[]{:S(2)}) collective-permute-start(bf16[144,512]{1,0:T(8,128)(2,1)S(1)} %get-tuple-element.286), channel_id=1, source_target_pairs={{0,4},{1,5},{2,6},{3,7},{4,0},{5,1},{6,2},{7,3},{8,12},{9,13},{10,... | collective-permute-start | bytes 442376 | tf_op jit(solution)/shard_map/ppermute | solution.py:46
  (32 other events, 243.3 us)
